TPU v7x, 32 devices: a whole 2x2x4 slice. The times are simulated.
32 devices in a mesh: fsdp: 8 (over y, x, core), ctx: 4 (over z).
Axes of the slice: x: 2, y: 2, z: 4, core: 2. Of those that a mesh axis runs over, the one named last changes fastest.
Arguments:
- inputs: bfloat16 [8, 2, 1024, 896], P('fsdp', None, 'ctx'), may hold values from -40 to 40
- cotangent: bfloat16 [8, 2, 1024, 896], P('fsdp', None, 'ctx'), may hold values from -6 to 6
- lengths: int32 [8, 2, 4], P('fsdp'), may hold values from 1 to 960, 1024 in all within a row
- order: int32 [8, 2, 8], P('fsdp'), may hold values from 0 to 7, each once within a row
- w_qkv: bfloat16 [896, 1152], P('fsdp'), may hold values from -0.1875 to 0.1875
- b_qkv: bfloat16 [1152], P('fsdp'), may hold values from -3 to 3
- w_out: bfloat16 [896, 896], P('fsdp'), may hold values from -3 to 3
- norm_attn: bfloat16 [896], P('fsdp'), may hold values from 0.25 to 1.75
- norm_mlp: bfloat16 [896], P('fsdp'), may hold values from 0.25 to 1.75
- w_gate_up: bfloat16 [896, 9728], P('fsdp'), may hold values from -0.1875 to 0.1875
- w_down: bfloat16 [4864, 896], P('fsdp'), may hold values from -0.078125 to 0.078125
Outputs:
- outputs: bfloat16 [8, 2, 1024, 896], P('fsdp', None, 'ctx')
- d_inputs: float32 [8, 2, 1024, 896], P('fsdp', None, 'ctx')
- grad_w_qkv: float32 [896, 1152], P('fsdp')
- grad_b_qkv: float32 [1024], P('fsdp')
- grad_b_v: float32 [128], P('fsdp')
- grad_w_out: float32 [896, 896], P('fsdp')
- grad_norm_attn: float32 [896], P('fsdp')
- grad_norm_mlp: float32 [896], P('fsdp')
- grad_w_gate_up: float32 [896, 9728], P('fsdp')
- grad_w_down: float32 [4864, 896], P('fsdp')
Inputs may be any that keep to these rules, and one draw needn't show every extreme that they name: Each row of 4 lengths sums to 1024. `order`: each row holds every block number once.
All inputs are finite; a program needn't handle non-finite values.
Results may differ from a plain program's by a relative error of at most 0.02.
Values may be sent and summed in bfloat16 or wider, within the bound.
A program may use at most 320 MiB of HBM per device.

v0:
```python
import math

import jax
import jax.numpy as jnp
from jax import lax
from jax.sharding import PartitionSpec as P

HQ = 14
KVH = 2
HD = 64
FF = 4864


EPSILON = 1e-06
ROPE_BASE = 1000000.0
NEGATIVE = -1e30


def token_places(order_one, lengths_one, first_row, row_count, block_rows):
    stored = first_row + jnp.arange(row_count, dtype=jnp.int32)
    block_ids = stored // block_rows
    numbers = jnp.arange(order_one.shape[0], dtype=jnp.int32)
    chosen = jnp.sum(
        jnp.where(block_ids[:, None] == numbers[None, :], order_one[None, :], 0), axis=1
    )
    natural = chosen * block_rows + stored % block_rows
    ends = jnp.cumsum(lengths_one)
    passed = (ends[None, :] <= natural[:, None]).astype(jnp.int32)
    segment = jnp.sum(passed, axis=1)
    begin = jnp.sum(passed * lengths_one[None, :], axis=1)
    return (natural, segment, natural - begin)


def rope_tables(position, head_dim):
    half_dim = head_dim // 2
    freqs = jnp.power(
        jnp.float32(ROPE_BASE), -(jnp.arange(half_dim, dtype=jnp.float32) * (2.0 / head_dim))
    )
    angle = position.astype(jnp.float32)[:, None] * freqs[None, :]
    cosine_table = jnp.cos(angle)
    sine_table = jnp.sin(angle)
    cosine_full = jnp.concatenate([cosine_table, cosine_table], axis=1)[:, None, :]
    sine_full = jnp.concatenate([sine_table, sine_table], axis=1)[:, None, :]
    return (cosine_full, sine_full)


def rotate_forward(vectors, cosine_full, sine_full):
    half_dim = vectors.shape[-1] // 2
    swapped = jnp.concatenate([-vectors[..., half_dim:], vectors[..., :half_dim]], axis=-1)
    return vectors * cosine_full + swapped * sine_full


def rotate_backward(gradient, cosine_full, sine_full):
    half_dim = gradient.shape[-1] // 2
    swapped = jnp.concatenate([-gradient[..., half_dim:], gradient[..., :half_dim]], axis=-1)
    return gradient * cosine_full - swapped * sine_full


def contract_rows(left, right):
    return lax.dot_general(
        left, right, (((0,), (0,)), ((), ())), preferred_element_type=jnp.float32
    )


def contract_cols(left, right):
    return lax.dot_general(
        left, right, (((1,), (1,)), ((), ())), preferred_element_type=jnp.float32
    )


def norm_backward(grad_normed, normed, inverse):
    return inverse * (grad_normed - normed * jnp.mean(grad_normed * normed, axis=1, keepdims=True))


def local(
    inputs, cotangent, lengths, order, w_qkv, b_qkv, w_out, norm_attn, norm_mlp, w_gate_up, w_down
):
    micro_count = inputs.shape[1]
    local_rows = inputs.shape[2]
    ctx_count = lax.axis_size("ctx")
    all_rows = local_rows * ctx_count
    first_row = lax.axis_index("ctx") * local_rows
    half_block = local_rows // 2
    group_size = HQ // KVH
    query_width = HQ * HD
    key_width = KVH * HD
    score_scale = 1.0 / math.sqrt(HD)
    outputs = []
    input_grads = []
    totals = None
    for micro_step in range(micro_count):
        weights = (
            lax.all_gather(w_qkv, "fsdp", axis=0, tiled=True),
            lax.all_gather(b_qkv, "fsdp", axis=0, tiled=True),
            lax.all_gather(w_out, "fsdp", axis=0, tiled=True),
            lax.all_gather(norm_attn, "fsdp", axis=0, tiled=True),
            lax.all_gather(norm_mlp, "fsdp", axis=0, tiled=True),
            lax.all_gather(w_gate_up, "fsdp", axis=0, tiled=True),
            lax.all_gather(w_down, "fsdp", axis=0, tiled=True),
        )
        full_qkv, full_bias, full_out, gain_attn, gain_mlp, full_gate_up, full_down = weights
        gain_attn = gain_attn.astype(jnp.float32)
        gain_mlp = gain_mlp.astype(jnp.float32)
        stream = inputs[0, micro_step].astype(jnp.float32)
        order_one = order[0, micro_step]
        lengths_one = lengths[0, micro_step]
        query_nat, query_seg, query_pos = token_places(
            order_one, lengths_one, first_row, local_rows, half_block
        )
        key_nat, key_seg, key_pos = token_places(order_one, lengths_one, 0, all_rows, half_block)
        allowed = (query_seg[:, None] == key_seg[None, :]) & (
            key_nat[None, :] <= query_nat[:, None]
        )
        cosine_full, sine_full = rope_tables(query_pos, HD)
        inv_attn = lax.rsqrt(jnp.mean(stream * stream, axis=1, keepdims=True) + EPSILON)
        normed_attn = stream * inv_attn
        hn_attn = (normed_attn * gain_attn).astype(jnp.bfloat16)
        project = jnp.dot(hn_attn, full_qkv, preferred_element_type=jnp.float32) + full_bias.astype(
            jnp.float32
        )
        queries = rotate_forward(
            project[:, :query_width].reshape(local_rows, HQ, HD), cosine_full, sine_full
        ).astype(jnp.bfloat16)
        keys_local = rotate_forward(
            project[:, query_width : query_width + key_width].reshape(local_rows, KVH, HD),
            cosine_full,
            sine_full,
        )
        keys_local = keys_local.reshape(local_rows, key_width).astype(jnp.bfloat16)
        values_local = project[:, query_width + key_width :].astype(jnp.bfloat16)
        keys_all, values_all = (
            lax.all_gather(keys_local, "ctx", axis=0, tiled=True),
            lax.all_gather(values_local, "ctx", axis=0, tiled=True),
        )
        log_totals = []
        mixed_parts = []
        for key_head in range(KVH):
            query_group = queries[:, key_head * group_size : (key_head + 1) * group_size, :]
            key_group = keys_all[:, key_head * HD : (key_head + 1) * HD]
            value_group = values_all[:, key_head * HD : (key_head + 1) * HD]
            raw_scores = (
                jnp.einsum(
                    "tjd,kd->jtk", query_group, key_group, preferred_element_type=jnp.float32
                )
                * score_scale
            )
            masked = jnp.where(allowed[None], raw_scores, NEGATIVE)
            row_top = jnp.max(masked, axis=2, keepdims=True)
            log_total = row_top + jnp.log(jnp.sum(jnp.exp(masked - row_top), axis=2, keepdims=True))
            probs_low = jnp.exp(masked - log_total).astype(jnp.bfloat16)
            mixed_parts.append(
                jnp.einsum(
                    "jtk,kd->tjd", probs_low, value_group, preferred_element_type=jnp.float32
                )
            )
            log_totals.append(log_total)
        attended = (
            jnp.concatenate(mixed_parts, axis=1)
            .reshape(local_rows, query_width)
            .astype(jnp.bfloat16)
        )
        stream_mid = stream + jnp.dot(attended, full_out, preferred_element_type=jnp.float32)
        inv_mlp = lax.rsqrt(jnp.mean(stream_mid * stream_mid, axis=1, keepdims=True) + EPSILON)
        normed_mlp = stream_mid * inv_mlp
        hn_mlp = (normed_mlp * gain_mlp).astype(jnp.bfloat16)
        gate_up = jnp.dot(hn_mlp, full_gate_up, preferred_element_type=jnp.float32)
        gate_part = gate_up[:, :FF]
        up_part = gate_up[:, FF:]
        hidden = (jax.nn.silu(gate_part) * up_part).astype(jnp.bfloat16)
        result = stream_mid + jnp.dot(hidden, full_down, preferred_element_type=jnp.float32)
        outputs.append(result.astype(jnp.bfloat16))
        grad_out = cotangent[0, micro_step].astype(jnp.float32)
        grad_low = grad_out.astype(jnp.bfloat16)
        term_down = contract_rows(hidden, grad_low)
        grad_hidden = contract_cols(grad_low, full_down)
        gate_sigmoid = jax.nn.sigmoid(gate_part)
        grad_gate = grad_hidden * up_part * gate_sigmoid * (1.0 + gate_part * (1.0 - gate_sigmoid))
        grad_up = grad_hidden * gate_part * gate_sigmoid
        grad_gate_up = jnp.concatenate([grad_gate, grad_up], axis=1).astype(jnp.bfloat16)
        term_gate_up = contract_rows(hn_mlp, grad_gate_up)
        grad_hn_mlp = contract_cols(grad_gate_up, full_gate_up)
        term_gain_mlp = jnp.sum(grad_hn_mlp * normed_mlp, axis=0)
        grad_mid = grad_out + norm_backward(grad_hn_mlp * gain_mlp, normed_mlp, inv_mlp)
        grad_branch = grad_mid.astype(jnp.bfloat16)
        term_out = contract_rows(attended, grad_branch)
        grad_attended = (
            contract_cols(grad_branch, full_out).astype(jnp.bfloat16).reshape(local_rows, HQ, HD)
        )
        query_grads = []
        key_grads = []
        value_grads = []
        for key_head in range(KVH):
            query_group = queries[:, key_head * group_size : (key_head + 1) * group_size, :]
            key_group = keys_all[:, key_head * HD : (key_head + 1) * HD]
            value_group = values_all[:, key_head * HD : (key_head + 1) * HD]
            grad_group = grad_attended[:, key_head * group_size : (key_head + 1) * group_size, :]
            raw_scores = (
                jnp.einsum(
                    "tjd,kd->jtk", query_group, key_group, preferred_element_type=jnp.float32
                )
                * score_scale
            )
            masked = jnp.where(allowed[None], raw_scores, NEGATIVE)
            softmax_full = jnp.exp(masked - log_totals[key_head])
            probs_low = softmax_full.astype(jnp.bfloat16)
            grad_probs = jnp.einsum(
                "tjd,kd->jtk", grad_group, value_group, preferred_element_type=jnp.float32
            )
            delta_rows = jnp.sum(softmax_full * grad_probs, axis=2, keepdims=True)
            grad_scores = (softmax_full * (grad_probs - delta_rows)).astype(jnp.bfloat16)
            query_grads.append(
                jnp.einsum(
                    "jtk,kd->tjd", grad_scores, key_group, preferred_element_type=jnp.float32
                )
                * score_scale
            )
            key_grads.append(
                jnp.einsum(
                    "jtk,tjd->kd", grad_scores, query_group, preferred_element_type=jnp.float32
                )
                * score_scale
            )
            value_grads.append(
                jnp.einsum("jtk,tjd->kd", probs_low, grad_group, preferred_element_type=jnp.float32)
            )
        key_terms = jnp.concatenate(key_grads, axis=1)
        value_terms = jnp.concatenate(value_grads, axis=1)
        grad_keys, grad_values = (
            lax.psum_scatter(
                key_terms.astype(jnp.bfloat16), "ctx", scatter_dimension=0, tiled=True
            ).astype(jnp.float32),
            lax.psum_scatter(
                value_terms.astype(jnp.bfloat16), "ctx", scatter_dimension=0, tiled=True
            ).astype(jnp.float32),
        )
        grad_queries = rotate_backward(
            jnp.concatenate(query_grads, axis=1), cosine_full, sine_full
        ).reshape(local_rows, query_width)
        grad_keys = rotate_backward(
            grad_keys.reshape(local_rows, KVH, HD), cosine_full, sine_full
        ).reshape(local_rows, key_width)
        grad_project = jnp.concatenate([grad_queries, grad_keys, grad_values], axis=1).astype(
            jnp.bfloat16
        )
        term_bias = jnp.sum(grad_project.astype(jnp.float32), axis=0)
        term_bias_qk = term_bias[: query_width + key_width]
        term_bias_v = term_bias[query_width + key_width :]
        term_qkv = contract_rows(hn_attn, grad_project)
        grad_hn_attn = contract_cols(grad_project, full_qkv)
        term_gain_attn = jnp.sum(grad_hn_attn * normed_attn, axis=0)
        grad_input = grad_mid + norm_backward(grad_hn_attn * gain_attn, normed_attn, inv_attn)
        input_grads.append(grad_input)
        grad_terms = (
            term_qkv,
            term_bias_qk,
            term_bias_v,
            term_out,
            term_gain_attn,
            term_gain_mlp,
            term_gate_up,
            term_down,
        )
        if totals is None:
            totals = grad_terms
        else:
            totals = tuple((earlier + later for earlier, later in zip(totals, grad_terms)))
    (
        sum_qkv,
        sum_bias_qk,
        sum_bias_v,
        sum_out,
        sum_gain_attn,
        sum_gain_mlp,
        sum_gate_up,
        sum_down,
    ) = totals
    shares = (
        lax.psum_scatter(
            sum_qkv.astype(jnp.bfloat16), "fsdp", scatter_dimension=0, tiled=True
        ).astype(jnp.float32),
        lax.psum_scatter(
            sum_bias_qk.astype(jnp.bfloat16), "fsdp", scatter_dimension=0, tiled=True
        ).astype(jnp.float32),
        lax.psum_scatter(
            sum_bias_v.astype(jnp.bfloat16), "fsdp", scatter_dimension=0, tiled=True
        ).astype(jnp.float32),
        lax.psum_scatter(
            sum_out.astype(jnp.bfloat16), "fsdp", scatter_dimension=0, tiled=True
        ).astype(jnp.float32),
        lax.psum_scatter(
            sum_gain_attn.astype(jnp.bfloat16), "fsdp", scatter_dimension=0, tiled=True
        ).astype(jnp.float32),
        lax.psum_scatter(
            sum_gain_mlp.astype(jnp.bfloat16), "fsdp", scatter_dimension=0, tiled=True
        ).astype(jnp.float32),
        lax.psum_scatter(
            sum_gate_up.astype(jnp.bfloat16), "fsdp", scatter_dimension=0, tiled=True
        ).astype(jnp.float32),
        lax.psum_scatter(
            sum_down.astype(jnp.bfloat16), "fsdp", scatter_dimension=0, tiled=True
        ).astype(jnp.float32),
    )
    (
        share_qkv,
        share_bias_qk,
        share_bias_v,
        share_out,
        share_gain_attn,
        share_gain_mlp,
        share_gate_up,
        share_down,
    ) = shares
    (
        final_qkv,
        final_bias_qk,
        final_bias_v,
        final_out,
        final_gain_attn,
        final_gain_mlp,
        final_gate_up,
        final_down,
    ) = (
        lax.psum(share_qkv.astype(jnp.bfloat16), "ctx").astype(jnp.float32),
        lax.psum(share_bias_qk.astype(jnp.bfloat16), "ctx").astype(jnp.float32),
        lax.psum(share_bias_v.astype(jnp.bfloat16), "ctx").astype(jnp.float32),
        lax.psum(share_out.astype(jnp.bfloat16), "ctx").astype(jnp.float32),
        lax.psum(share_gain_attn.astype(jnp.bfloat16), "ctx").astype(jnp.float32),
        lax.psum(share_gain_mlp.astype(jnp.bfloat16), "ctx").astype(jnp.float32),
        lax.psum(share_gate_up.astype(jnp.bfloat16), "ctx").astype(jnp.float32),
        lax.psum(share_down.astype(jnp.bfloat16), "ctx").astype(jnp.float32),
    )
    stacked_outputs = jnp.stack(outputs)[None]
    stacked_grads = jnp.stack(input_grads)[None]
    return (
        stacked_outputs,
        stacked_grads,
        final_qkv,
        final_bias_qk,
        final_bias_v,
        final_out,
        final_gain_attn,
        final_gain_mlp,
        final_gate_up,
        final_down,
    )


def solution(mesh):
    return jax.shard_map(
        local,
        mesh=mesh,
        in_specs=(
            P("fsdp", None, "ctx", None),
            P("fsdp", None, "ctx", None),
            P("fsdp", None, None),
            P("fsdp", None, None),
            P("fsdp", None),
            P("fsdp"),
            P("fsdp", None),
            P("fsdp"),
            P("fsdp"),
            P("fsdp", None),
            P("fsdp", None),
        ),
        out_specs=(
            P("fsdp", None, "ctx", None),
            P("fsdp", None, "ctx", None),
            P("fsdp", None),
            P("fsdp"),
            P("fsdp"),
            P("fsdp", None),
            P("fsdp"),
            P("fsdp"),
            P("fsdp", None),
            P("fsdp", None),
        ),
        check_vma=False,
    )
```

profile of v0, /device:TPU:0, one launch (start us, length us, event | category | flops | bytes accessed | tf_op | source)
XLA Modules:
  0.0 859.4 jit_solution(13186137261781437881)
XLA Ops:
  20.0 15.6 %all-reduce.8 = (bf16[1152]{0:T(1024)(128)(2,1)S(1)}, bf16[896]{0:T(1024)(128)(2,1)S(1)}, bf16[896]{0:T(1024)(128)(2,1)S(1)}) all-reduce(bf16[1152]{0:T(1024)(128)(2,1)S(1)} %dynamic-update-slice.1, bf16[896]{0:T(1024)(128)(2,1)S(1)} %dynamic-update-slice, ...), channel_id=1, replica_groups=mesh['fsdp'=8,'ctx'=4] {'fsdp'}, use_global_device_ids=true, to_apply=%add.1 | all-reduce | flops 2944 | bytes 11776
  40.5 2.6 convolution_add_fusion.1
  59.0 14.1 %all_gather.49 = bf16[1024,128]{1,0:T(8,128)(2,1)S(1)} all-gather(bf16[256,128]{1,0:T(8,128)(2,1)} %slice.432), channel_id=1, replica_groups=mesh['fsdp'=8,'ctx'=4] {'ctx'}, dimensions={0}, use_global_device_ids=true | all-gather | bytes 327680 | tf_op jit(solution)/shard_map/all_gather | solution.py:133
  74.2 14.6 %all_gather.50 = bf16[1024,128]{1,0:T(8,128)(2,1)S(1)} all-gather(bf16[256,128]{1,0:T(8,128)(2,1)S(1)} %add_convert_fusion.3), channel_id=1, replica_groups=mesh['fsdp'=8,'ctx'=4] {'ctx'}, dimensions={0}, use_global_device_ids=true | all-gather | bytes 327680 | tf_op jit(solution)/shard_map/all_gather | solution.py:132
  88.8 14.6 %all_gather.43 = bf16[1024,128]{1,0:T(8,128)(2,1)S(1)} all-gather(bf16[256,128]{1,0:T(8,128)(2,1)} %slice.433), channel_id=1, replica_groups=mesh['fsdp'=8,'ctx'=4] {'ctx'}, dimensions={0}, use_global_device_ids=true | all-gather | bytes 327680 | tf_op jit(solution)/shard_map/all_gather | solution.py:133
  104.6 14.0 %all_gather.44 = bf16[1024,128]{1,0:T(8,128)(2,1)S(1)} all-gather(bf16[256,128]{1,0:T(8,128)(2,1)S(1)} %add_convert_fusion.4), channel_id=1, replica_groups=mesh['fsdp'=8,'ctx'=4] {'ctx'}, dimensions={0}, use_global_device_ids=true | all-gather | bytes 327680 | tf_op jit(solution)/shard_map/all_gather | solution.py:132
  121.0 2.8 exponential_reduce_fusion.1
  130.9 3.2 exponential_reduce_fusion.3
  142.1 2.6 multiply_reduce_fusion.5
  144.7 18.1 %all-gather.9.cloned.1.call-done = bf16[896,9728]{1,0:T(8,128)(2,1)} async-done(((bf16[112,9728]{1,0:T(8,128)(2,1)}), bf16[896,9728]{1,0:T(8,128)(2,1)}) %all-gather.9.cloned.1.call-update) | async-done | bytes 17432592 | tf_op jit(solution)/shard_map/all_gather | solution.py:98
  162.8 14.2 %fusion.164 = f32[256,9728]{1,0:T(8,128)} fusion(bf16[896,9728]{1,0:T(8,128)(2,1)} %all-gather.9.cloned.1.call-done, f32[256,896]{1,0:T(8,128)S(1)} %get-tuple-element.99, f32[256]{0:T(256)S(1)} %add_rsqrt_fusion, f32[896]{0:T(1024)S(1)} %convert_element_type.243), kind=kOutput, calls=%fused_computation.334 | convolution fusion | flops 4463427584 | bytes 28316160 | tf_op jit(solution)/shard_map/dot_general | solution.py:166
  177.2 7.8 fusion.163
  185.0 35.3 %all-gather.11.cloned.1.call-done = bf16[4864,896]{1,0:T(8,128)(2,1)} async-done(((bf16[608,896]{1,0:T(8,128)(2,1)}), bf16[4864,896]{1,0:T(8,128)(2,1)}) %all-gather.11.cloned.1.call-update) | async-done | bytes 8716304 | tf_op jit(solution)/shard_map/all_gather | solution.py:99
  220.4 12.0 %multiply_convert_fusion.1 = (bf16[256,4864]{1,0:T(8,128)(2,1)}, bf16[256,4864]{1,0:T(8,128)(2,1)}, bf16[256,4864]{1,0:T(8,128)(2,1)}) fusion(f32[256,9728]{1,0:T(8,128)} %fusion.164, bf16[4864,896]{1,0:T(8,128)(2,1)} %all-gather.11.cloned.1.call-done, bf16[1,2,256,896]{3,2,1,0:T(8,128)(2,1)S(1)} %copy-done.44), kind=kOutput, calls=%fused_computation.41 | convolution fusion | flops 2251292672 | bytes 26607616 | tf_op jit(solution)/shard_map/dot_general | solution.py:66
  232.4 11.0 %multiply_convert_fusion.3 = (bf16[256,4864]{1,0:T(8,128)(2,1)}, bf16[256,4864]{1,0:T(8,128)(2,1)}, bf16[256,4864]{1,0:T(8,128)(2,1)}) fusion(f32[256,9728]{1,0:T(8,128)S(1)} %copy-done.23, bf16[4864,896]{1,0:T(8,128)(2,1)} %all-gather.11.cloned.1.call-done, bf16[1,2,256,896]{3,2,1,0:T(8,128)(2,1)S(1)} %copy-done.44), kind=kOutput, calls=%fused_computation.43 | convolution fusion | flops 2251292672 | bytes 26607616 | tf_op jit(solution)/shard_map/dot_general | solution.py:66
  243.4 11.6 %fusion.21 = f32[256,896]{1,0:T(8,128)} fusion(bf16[896,9728]{1,0:T(8,128)(2,1)} %all-gather.9.cloned.1.call-done, bf16[256,4864]{1,0:T(8,128)(2,1)} %get-tuple-element.56, bf16[256,4864]{1,0:T(8,128)(2,1)} %get-tuple-element.55), kind=kOutput, calls=%fused_computation.54 | convolution fusion | flops 4472700928 | bytes 23330816 | tf_op jit(solution)/shard_map/dot_general | solution.py:66
  255.0 13.0 %multiply_reduce_fusion.1 = (f32[896]{0:T(1024)}, f32[256]{0:T(256)S(1)}, f32[256]{0:T(256)S(1)}, f32[896]{0:T(1024)}, f32[256,896]{1,0:T(8,128)}) fusion(f32[256,896]{1,0:T(8,128)S(1)} %get-tuple-element.104, f32[256]{0:T(256)S(1)} %add_rsqrt_fusion.2, f32[896]{0:T(1024)S(1)} %convert_element_type.243, f32[256,896]{1,0:T(8,128)} %fusion.21, ...), kind=kOutput, calls=%fused_computation.165 | convolution fusion | flops 4475451392 | bytes 26098176 | tf_op jit(solution)/shard_map/dot_general | solution.py:66
  267.9 3.1 multiply_add_fusion.1
  275.3 11.7 %fusion.3 = (f32[7,256]{1,0:T(8,128)S(1)}, f32[7,256]{1,0:T(8,128)S(1)}, f32[1024,256,7]{1,0,2:T(8,128)}) fusion(f32[1024,256,7]{1,0,2:T(8,128)} %copy-done.1, f32[7,256]{1,0:T(8,128)S(1)} %log_add_fusion.1, pred[256,1024]{0,1:T(8,128)(4,1)S(1)} %copy-done.26, f32[1024,256,7]{1,0,2:T(8,128)S(1)} %fusion.105, f32[7,256]{1,0:T(8,128)S(1)} %log_add_fusion, ...), kind=kOutput, calls=%fused_computation.9 | convolution fusion | flops 253227520 | bytes 30144512 | tf_op jit(solution)/shard_map/tjd,kd->jtk/dot_general | solution.py:206
  287.1 11.4 %fusion.5 = (bf16[7,256,1024]{1,2,0:T(8,128)(2,1)}, bf16[7,256,1024]{1,2,0:T(8,128)(2,1)S(1)}) fusion(f32[1024,256,7]{1,0,2:T(8,128)} %get-tuple-element.107, f32[1024,256,7]{1,0,2:T(8,128)S(1)} %bitcast.326, f32[7,256]{1,0:T(8,128)S(1)} %get-tuple-element.24, f32[7,256]{1,0:T(8,128)S(1)} %log_add_fusion.1, pred[256,1024]{0,1:T(8,128)(4,1)S(1)} %copy-done.26, ...), kind=kLoop, calls=%fused_computation.11 | loop fusion | flops 22020096 | bytes 36990976 | tf_op jit(solution)/shard_map/convert_element_type | solution.py:210
  305.5 5.9 fusion.51
  314.0 4.1 fusion.111
  320.2 11.8 %fusion.9 = (f32[7,256]{1,0:T(8,128)S(1)}, f32[7,256]{1,0:T(8,128)S(1)}, f32[1024,256,7]{1,0,2:T(8,128)}) fusion(f32[1024,256,7]{1,0,2:T(8,128)} %copy-done.3, f32[7,256]{1,0:T(8,128)S(1)} %log_add_fusion.3, pred[256,1024]{0,1:T(8,128)(4,1)S(1)} %copy-done.29, f32[1024,256,7]{1,0,2:T(8,128)} %fusion.111, f32[7,256]{1,0:T(8,128)S(1)} %log_add_fusion.2, ...), kind=kOutput, calls=%fused_computation.19 | convolution fusion | flops 253227520 | bytes 30144512 | tf_op jit(solution)/shard_map/tjd,kd->jtk/dot_general | solution.py:206
  332.0 11.6 %fusion.11 = (bf16[7,256,1024]{1,2,0:T(8,128)(2,1)S(1)}, bf16[7,256,1024]{1,2,0:T(8,128)(2,1)S(1)}) fusion(f32[1024,256,7]{1,0,2:T(8,128)} %get-tuple-element.106, f32[1024,256,7]{1,0,2:T(8,128)} %copy-done.3, f32[7,256]{1,0:T(8,128)S(1)} %get-tuple-element.22, f32[7,256]{1,0:T(8,128)S(1)} %log_add_fusion.3, pred[256,1024]{0,1:T(8,128)(4,1)S(1)} %copy-done.29, ...), kind=kLoop, calls=%fused_computation.21 | loop fusion | flops 22020096 | bytes 36990976 | tf_op jit(solution)/shard_map/convert_element_type | solution.py:210
  348.2 5.0 fusion.55
  353.2 5.0 fusion.54
  358.4 3.7 fusion.35
  362.8 3.3 fusion.101
  366.3 3.6 fusion.36
  369.9 3.7 add_convert_fusion.2
  374.0 3.0 fusion.37
  384.6 8.5 reduce-scatter.11.cloned.1.call-done
  393.1 3.8 fusion.132
  396.9 17.0 %reduce-scatter.15.cloned.1.call-done = bf16[256,128]{0,1:T(8,128)(2,1)} async-done(((bf16[1024,128]{0,1:T(8,128)(2,1)}), bf16[256,128]{0,1:T(8,128)(2,1)}) %reduce-scatter.15.cloned.1.call-update) | async-done | bytes 65552 | tf_op jit(solution)/shard_map/reduce_scatter | solution.py:232
  413.9 4.5 fusion.20
  418.5 10.9 %fusion.91 = f32[4864,896]{1,0:T(8,128)} fusion(bf16[256,4864]{1,0:T(8,128)(2,1)} %get-tuple-element.57, bf16[1,2,256,896]{3,2,1,0:T(8,128)(2,1)S(1)} %copy-done.45), kind=kOutput, calls=%fused_computation.189 | convolution fusion | flops 2231369728 | bytes 20381696 | tf_op jit(solution)/shard_map/dot_general | solution.py:60
  429.4 9.5 %add_convert_fusion.1 = bf16[4864,896]{1,0:T(8,128)(2,1)} fusion(f32[4864,896]{1,0:T(8,128)} %fusion.91, bf16[256,4864]{1,0:T(8,128)(2,1)S(1)} %copy-done.24, bf16[1,2,256,896]{3,2,1,0:T(8,128)(2,1)S(1)} %copy-done.45), kind=kOutput, calls=%fused_computation.1 | convolution fusion | flops 2240086016 | bytes 29097984 | tf_op jit(solution)/shard_map/dot_general | solution.py:60
  440.1 19.0 %fusion.22 = f32[896,9728]{1,0:T(8,128)} fusion(bf16[256,4864]{1,0:T(8,128)(2,1)} %get-tuple-element.54, bf16[256,4864]{1,0:T(8,128)(2,1)} %get-tuple-element.53, f32[256,896]{1,0:T(8,128)S(1)} %copy-done.16, f32[896]{0:T(1024)S(1)} %convert_element_type.243, f32[256]{0:T(256)S(1)} %add_rsqrt_fusion.2), kind=kOutput, calls=%fused_computation.55 | convolution fusion | flops 4473389056 | bytes 40768000 | tf_op jit(solution)/shard_map/dot_general | solution.py:60
  459.1 21.7 %add_convert_fusion = bf16[896,9728]{1,0:T(8,128)(2,1)} fusion(f32[896,9728]{1,0:T(8,128)} %fusion.22, bf16[256,4864]{1,0:T(8,128)(2,1)} %get-tuple-element.56, bf16[256,4864]{1,0:T(8,128)(2,1)} %get-tuple-element.55, f32[256,896]{1,0:T(8,128)S(1)} %copy-done.14, f32[256]{0:T(256)S(1)} %add_rsqrt_fusion, f32[896]{0:T(1024)S(1)} %convert_element_type.243), kind=kOutput, calls=%fused_computation | convolution fusion | flops 4490821632 | bytes 58200576 | tf_op jit(solution)/shard_map/dot_general | solution.py:60
  483.2 16.8 %reduce-scatter.17.cloned.1.call-done = bf16[112,1152]{1,0:T(8,128)(2,1)} async-done(((bf16[896,1152]{1,0:T(8,128)(2,1)}), bf16[112,1152]{1,0:T(8,128)(2,1)}) %reduce-scatter.17.cloned.1.call-update) | async-done | bytes 258064 | tf_op jit(solution)/shard_map/reduce_scatter | solution.py:278
  500.0 76.5 %reduce-scatter.23.cloned.1.call-done = bf16[608,896]{1,0:T(8,128)(2,1)} async-done(((bf16[4864,896]{1,0:T(8,128)(2,1)}), bf16[608,896]{1,0:T(8,128)(2,1)}) %reduce-scatter.23.cloned.1.call-update) | async-done | bytes 1089552 | tf_op jit(solution)/shard_map/reduce_scatter | solution.py:299
  576.5 122.7 %reduce-scatter.21.cloned.1.call-done = bf16[112,9728]{1,0:T(8,128)(2,1)} async-done(((bf16[896,9728]{1,0:T(8,128)(2,1)}), bf16[112,9728]{1,0:T(8,128)(2,1)}) %reduce-scatter.21.cloned.1.call-update) | async-done | bytes 2179088 | tf_op jit(solution)/shard_map/reduce_scatter | solution.py:296
  699.3 7.1 fusion.38
  706.5 7.0 fusion.39
  718.1 13.8 %all-reduce.7 = (bf16[1024]{0:T(1024)(128)(2,1)S(1)}, bf16[128]{0:T(256)(128)(2,1)S(1)}, bf16[896]{0:T(1024)(128)(2,1)S(1)}, bf16[896]{0:T(1024)(128)(2,1)S(1)}) all-reduce(bf16[1024]{0:T(1024)(128)(2,1)S(1)} %fusion.148, bf16[128]{0:T(256)(128)(2,1)S(1)} %fusion.150, ...), channel_id=7, replica_groups=mesh['fsdp'=8,'ctx'=4] {'fsdp'}, use_global_device_ids=true, to_apply=%region_40.41.clone | all-reduce | flops 2944 | bytes 11776
  732.3 12.4 %all-reduce.9 = (bf16[128]{0:T(256)(128)(2,1)S(1)}, bf16[16]{0:T(256)(128)(2,1)S(1)}, bf16[112]{0:T(256)(128)(2,1)S(1)}, bf16[112]{0:T(256)(128)(2,1)S(1)}) all-reduce(bf16[128]{0:T(256)(128)(2,1)S(1)} %dynamic-slice.4, bf16[16]{0:T(256)(128)(2,1)S(1)} %dynamic-slice.6, ...), channel_id=1, replica_groups=mesh['fsdp'=8,'ctx'=4] {'ctx'}, use_global_device_ids=true, to_apply=%region_41.42 | all-reduce | flops 368 | bytes 1472 | tf_op jit(solution)/shard_map/psum | solution.py:324
  750.0 93.2 %all-reduce.13.cloned.1.call-done = (bf16[112,1152]{1,0:T(8,128)(2,1)}, bf16[112,896]{1,0:T(8,128)(2,1)}, bf16[112,9728]{1,0:T(8,128)(2,1)}, bf16[608,896]{1,0:T(8,128)(2,1)}) async-done(((bf16[112,1152]{1,0:T(8,128)(2,1)}, bf16[112,896]{1,0:T(8,128)(2,1)}, bf16[112,9728]{1,0:T(8,128)(2,1)}, bf16[608,896]{1,0:T(8,128)(2,1)}), (bf16[112,1152]{1,0:T(8,128)(2,1)}, bf16[112,896]{1,0:T(8,128)(2,1)}, ...) | async-done | bytes 3727376 | tf_op jit(solution)/shard_map/psum | solution.py:323
  846.7 4.1 convert_element_type.288
  (350 shorter events, 97.2 us)
Async XLA Ops:
  7.2 37.7 %copy-start.11 = (bf16[1,2,256,896]{3,2,1,0:T(8,128)(2,1)S(1)}, bf16[1,2,256,896]{3,2,1,0:T(8,128)(2,1)}, u32[]{:S(2)}) copy-start(bf16[1,2,256,896]{3,2,1,0:T(8,128)(2,1)} %param.11) | copy-start | bytes 2752516
  7.2 33.3 %all-gather.5.cloned.1.call-start = ((), (), s32[]{:S(2)}) async-start(), calls=%async_computation.8 | async-start | bytes 2322432 | tf_op jit(solution)/shard_map/all_gather | solution.py:93
  7.9 131.8 %all-gather.7.cloned.1.call-start = ((), (), s32[]{:S(2)}) async-start(), calls=%async_computation.9 | async-start | bytes 1806336 | tf_op jit(solution)/shard_map/all_gather | solution.py:95
  8.7 154.1 %all-gather.9.cloned.1.call-start = ((), (), s32[]{:S(2)}) async-start(), calls=%async_computation.10 | async-start | bytes 19611648 | tf_op jit(solution)/shard_map/all_gather | solution.py:98
  9.4 211.0 %all-gather.11.cloned.1.call-start = ((), (), s32[]{:S(2)}) async-start(), calls=%async_computation.11 | async-start | bytes 9805824 | tf_op jit(solution)/shard_map/all_gather | solution.py:99
  10.0 369.5 %reduce-scatter.13.cloned.1.call-start = ((), (), s32[]{:S(2)}) async-start(), calls=%async_computation.14 | async-start | bytes 327680 | tf_op jit(solution)/shard_map/reduce_scatter | solution.py:229
  11.5 31.7 %copy-start.81 = (f32[256]{0:T(256)}, f32[256]{0:T(256)S(1)}, u32[]{:S(2)}) copy-start(f32[256]{0:T(256)S(1)} %add_rsqrt_fusion.1) | copy-start | bytes 3076
  14.8 104.0 %copy-start.65 = (f32[256,64]{0,1:T(8,128)}, f32[256,64]{0,1:T(8,128)S(1)}, u32[]{:S(2)}) copy-start(f32[256,64]{0,1:T(8,128)S(1)} %pad_maximum_fusion.18) | copy-start | bytes 196612
  14.8 114.7 %copy-start.63 = (f32[256,64]{0,1:T(8,128)}, f32[256,64]{0,1:T(8,128)S(1)}, u32[]{:S(2)}) copy-start(f32[256,64]{0,1:T(8,128)S(1)} %pad_maximum_fusion.17) | copy-start | bytes 196612
  14.8 114.7 %copy-start.61 = (f32[256,64]{0,1:T(8,128)}, f32[256,64]{0,1:T(8,128)S(1)}, u32[]{:S(2)}) copy-start(f32[256,64]{0,1:T(8,128)S(1)} %pad_maximum_fusion.16) | copy-start | bytes 196612
  35.6 14.4 %copy-start.75 = (f32[896]{0:T(1024)}, f32[896]{0:T(1024)S(1)}, u32[]{:S(2)}) copy-start(f32[896]{0:T(1024)S(1)} %convert_element_type.232) | copy-start | bytes 10756
  37.3 12.7 %copy-start.79 = (f32[256]{0:T(256)}, f32[256]{0:T(256)S(1)}, u32[]{:S(2)}) copy-start(f32[256]{0:T(256)S(1)} %add_rsqrt_fusion.3) | copy-start | bytes 3076
  37.7 89.7 %copy-start.25 = (pred[256,1024]{0,1:T(8,128)(4,1)}, pred[256,1024]{0,1:T(8,128)(4,1)S(1)}, u32[]{:S(2)}) copy-start(pred[256,1024]{0,1:T(8,128)(4,1)S(1)} %compare_and_fusion) | copy-start | bytes 786436
  38.0 99.7 %copy-start.27 = (pred[256,1024]{0,1:T(8,128)(4,1)}, pred[256,1024]{0,1:T(8,128)(4,1)S(1)}, u32[]{:S(2)}) copy-start(pred[256,1024]{0,1:T(8,128)(4,1)S(1)} %compare_and_fusion.1) | copy-start | bytes 786436
  73.1 54.3 %copy-start.55 = (bf16[1024,128]{1,0:T(8,128)(2,1)}, bf16[1024,128]{1,0:T(8,128)(2,1)S(1)}, u32[]{:S(2)}) copy-start(bf16[1024,128]{1,0:T(8,128)(2,1)S(1)} %all_gather.49) | copy-start | bytes 786436
  88.8 35.0 %copy-start.32 = (bf16[1024,128]{1,0:T(8,128)(2,1)}, bf16[1024,128]{1,0:T(8,128)(2,1)S(1)}, u32[]{:S(2)}) copy-start(bf16[1024,128]{1,0:T(8,128)(2,1)S(1)} %all_gather.50) | copy-start | bytes 786436
  103.5 34.2 %copy-start.52 = (bf16[1024,128]{1,0:T(8,128)(2,1)}, bf16[1024,128]{1,0:T(8,128)(2,1)S(1)}, u32[]{:S(2)}) copy-start(bf16[1024,128]{1,0:T(8,128)(2,1)S(1)} %all_gather.43) | copy-start | bytes 786436
  118.6 12.3 %copy-start.30 = (bf16[1024,128]{1,0:T(8,128)(2,1)}, bf16[1024,128]{1,0:T(8,128)(2,1)S(1)}, u32[]{:S(2)}) copy-start(bf16[1024,128]{1,0:T(8,128)(2,1)S(1)} %all_gather.44) | copy-start | bytes 786436
  139.7 37.4 %copy-start.37 = (bf16[256,14,64]{0,2,1:T(8,128)(2,1)}, bf16[256,14,64]{0,2,1:T(8,128)(2,1)S(1)}, u32[]{:S(2)}) copy-start(bf16[256,14,64]{0,2,1:T(8,128)(2,1)S(1)} %pad_maximum_fusion.10) | copy-start | bytes 1376260
  142.1 125.8 %copy-start.13 = (f32[256,896]{1,0:T(8,128)}, f32[256,896]{1,0:T(8,128)S(1)}, u32[]{:S(2)}) copy-start(f32[256,896]{1,0:T(8,128)S(1)} %get-tuple-element.99) | copy-start | bytes 2752516
  144.7 123.2 %copy-start.15 = (f32[256,896]{1,0:T(8,128)}, f32[256,896]{1,0:T(8,128)S(1)}, u32[]{:S(2)}) copy-start(f32[256,896]{1,0:T(8,128)S(1)} %get-tuple-element.104) | copy-start | bytes 2752516
  162.8 14.4 %copy-start = (bf16[896,9728]{1,0:T(8,128)(2,1)S(1)}, bf16[896,9728]{1,0:T(8,128)(2,1)}, u32[]{:S(2)}) copy-start(bf16[896,9728]{1,0:T(8,128)(2,1)} %all-gather.9.cloned.1.call-done) | copy-start | bytes 52297732
  177.2 43.2 %copy-start.44 = (bf16[1,2,256,896]{3,2,1,0:T(8,128)(2,1)S(1)}, bf16[1,2,256,896]{3,2,1,0:T(8,128)(2,1)}, u32[]{:S(2)}) copy-start(bf16[1,2,256,896]{3,2,1,0:T(8,128)(2,1)} %param.12) | copy-start | bytes 2752516
  220.4 12.0 %copy-start.23 = (f32[256,9728]{1,0:T(8,128)S(1)}, f32[256,9728]{1,0:T(8,128)}, u32[]{:S(2)}) copy-start(f32[256,9728]{1,0:T(8,128)} %fusion.163) | copy-start | bytes 29884420
  255.0 17.0 %copy-start.9 = (bf16[896,896]{1,0:T(8,128)(2,1)S(1)}, bf16[896,896]{1,0:T(8,128)(2,1)}, u32[]{:S(2)}) copy-start(bf16[896,896]{1,0:T(8,128)(2,1)} %all-gather.7.cloned.1.call-done) | copy-start | bytes 4816900
  272.9 14.1 %copy-start.57 = (bf16[256,896]{0,1:T(8,128)(2,1)}, bf16[256,896]{0,1:T(8,128)(2,1)S(1)}, u32[]{:S(2)}) copy-start(bf16[256,896]{0,1:T(8,128)(2,1)S(1)} %copy.188) | copy-start | bytes 1376260
  273.0 14.1 %slice-start = ((s8[7340032]{0:T(1024)(128)(4,1)}), s8[4194304]{0:T(1024)(128)(4,1)S(1)}, s32[]{:S(2)}) async-start(s8[7340032]{0:T(1024)(128)(4,1)} %bitcast.325), calls=%async_computation.21 | async-start | bytes 8388608
  275.3 11.8 %copy-start.5 = (f32[1024,256,7]{1,0,2:T(8,128)}, f32[1024,256,7]{1,0,2:T(8,128)S(1)}, u32[]{:S(2)}) copy-start(f32[1024,256,7]{1,0,2:T(8,128)S(1)} %fusion.105) | copy-start | bytes 22020100
  275.3 11.8 %slice-start.1 = ((s8[7340032]{0:T(1024)(128)(4,1)}), s8[3145728]{0:T(1024)(128)(4,1)S(1)}, s32[]{:S(2)}) async-start(s8[7340032]{0:T(1024)(128)(4,1)} %bitcast.325), calls=%async_computation.22 | async-start | bytes 6291456
  287.1 13.4 %copy-start.33 = (bf16[1024,128]{1,0:T(8,128)(2,1)S(1)}, bf16[1024,128]{1,0:T(8,128)(2,1)}, u32[]{:S(2)}) copy-start(bf16[1024,128]{1,0:T(8,128)(2,1)} %copy-done.32) | copy-start | bytes 786436
  320.1 61.0 %reduce-scatter.9.cloned.1.call-start = ((), (), s32[]{:S(2)}) async-start(), calls=%async_computation.12 | async-start | bytes 327680 | tf_op jit(solution)/shard_map/reduce_scatter | solution.py:229
  353.2 39.9 %reduce-scatter.11.cloned.1.call-start = ((), (), s32[]{:S(2)}) async-start(), calls=%async_computation.13 | async-start | bytes 327680 | tf_op jit(solution)/shard_map/reduce_scatter | solution.py:232
  358.3 55.6 %reduce-scatter.15.cloned.1.call-start = ((), (), s32[]{:S(2)}) async-start(), calls=%async_computation.15 | async-start | bytes 327680 | tf_op jit(solution)/shard_map/reduce_scatter | solution.py:232
  366.2 116.9 %reduce-scatter.19.cloned.1.call-start = ((), (), s32[]{:S(2)}) async-start(), calls=%async_computation.17 | async-start | bytes 1806336 | tf_op jit(solution)/shard_map/reduce_scatter | solution.py:287
  373.7 19.3 %copy-start.12 = (bf16[1,2,256,896]{3,2,1,0:T(8,128)(2,1)S(1)}, bf16[1,2,256,896]{3,2,1,0:T(8,128)(2,1)}, u32[]{:S(2)}) copy-start(bf16[1,2,256,896]{3,2,1,0:T(8,128)(2,1)} %param.11) | copy-start | bytes 2752516
  373.7 19.3 %copy-start.76 = (f32[896]{0:T(1024)S(1)}, f32[896]{0:T(1024)}, u32[]{:S(2)}) copy-start(f32[896]{0:T(1024)} %copy-done.75) | copy-start | bytes 10756
  373.7 19.3 %copy-start.80 = (f32[256]{0:T(256)S(1)}, f32[256]{0:T(256)}, u32[]{:S(2)}) copy-start(f32[256]{0:T(256)} %copy-done.79) | copy-start | bytes 3076
  373.8 126.2 %reduce-scatter.17.cloned.1.call-start = ((), (), s32[]{:S(2)}) async-start(), calls=%async_computation.16 | async-start | bytes 2322432 | tf_op jit(solution)/shard_map/reduce_scatter | solution.py:278
  378.3 35.7 %copy-start.82 = (f32[256]{0:T(256)S(1)}, f32[256]{0:T(256)}, u32[]{:S(2)}) copy-start(f32[256]{0:T(256)} %copy-done.81) | copy-start | bytes 3076
  379.2 34.7 %copy-start.41 = (bf16[256,14,64]{0,2,1:T(8,128)(2,1)S(1)}, bf16[256,14,64]{0,2,1:T(8,128)(2,1)}, u32[]{:S(2)}) copy-start(bf16[256,14,64]{0,2,1:T(8,128)(2,1)} %fusion.58) | copy-start | bytes 1376260
  379.4 39.0 %copy-start.42 = (bf16[256,14,64]{0,2,1:T(8,128)(2,1)}, bf16[256,14,64]{0,2,1:T(8,128)(2,1)S(1)}, u32[]{:S(2)}) copy-start(bf16[256,14,64]{0,2,1:T(8,128)(2,1)S(1)} %fusion.61) | copy-start | bytes 1376260
  393.1 25.4 %copy-start.45 = (bf16[1,2,256,896]{3,2,1,0:T(8,128)(2,1)S(1)}, bf16[1,2,256,896]{3,2,1,0:T(8,128)(2,1)}, u32[]{:S(2)}) copy-start(bf16[1,2,256,896]{3,2,1,0:T(8,128)(2,1)} %param.12) | copy-start | bytes 2752516
  418.4 158.1 %reduce-scatter.23.cloned.1.call-start = ((), (), s32[]{:S(2)}) async-start(), calls=%async_computation.19 | async-start | bytes 9805824 | tf_op jit(solution)/shard_map/reduce_scatter | solution.py:299
  438.9 20.2 %copy-start.14 = (f32[256,896]{1,0:T(8,128)S(1)}, f32[256,896]{1,0:T(8,128)}, u32[]{:S(2)}) copy-start(f32[256,896]{1,0:T(8,128)} %copy-done.13) | copy-start | bytes 2752516
  438.9 260.3 %reduce-scatter.21.cloned.1.call-start = ((), (), s32[]{:S(2)}) async-start(), calls=%async_computation.18 | async-start | bytes 19611648 | tf_op jit(solution)/shard_map/reduce_scatter | solution.py:296
  480.9 362.3 %all-reduce.13.cloned.1.call-start = ((), (), s32[]{:S(2)}) async-start(), calls=%async_computation.20 | async-start | bytes 7454720 | tf_op jit(solution)/shard_map/psum | solution.py:323
  713.5 33.2 %copy-start.19 = (f32[256,896]{1,0:T(8,128)S(1)}, f32[256,896]{1,0:T(8,128)}, u32[]{:S(2)}) copy-start(f32[256,896]{1,0:T(8,128)} %get-tuple-element.61) | copy-start | bytes 2752516
  713.5 33.2 %copy-start.22 = (f32[256,896]{1,0:T(8,128)S(1)}, f32[256,896]{1,0:T(8,128)}, u32[]{:S(2)}) copy-start(f32[256,896]{1,0:T(8,128)} %copy-done.20) | copy-start | bytes 2752516
  (55 other events, 331.7 us)
Sparse Core Ops, SparseCore 0:
  9.9 30.5 all-gather.4
  42.4 25.8 all-gather.6
  70.1 92.6 all-gather.8
  164.6 55.7 all-gather.10
  320.2 19.6 reduce-scatter.12
  353.3 19.6 reduce-scatter.8
  375.3 17.7 reduce-scatter.10
  396.0 17.9 reduce-scatter.14
  417.9 37.0 reduce-scatter.18
  459.2 40.7 reduce-scatter.16
  503.6 72.9 reduce-scatter.22
  580.1 119.1 reduce-scatter.20
  701.9 141.2 all-reduce.12
where the time goes:
time: 865 us; the launch traced here: 859 us
  waiting for transfers between devices  393 us (45%)
  matrix products  258 us (30%)
  blocking collectives  99.1 us (11%)
  other arithmetic  64.1 us (7%)
  local copies, waits for them, and re-layouts  24.7 us (3%)
  between operations  19.1 us (2%)
    reduce_scatter x1, waiting for transfers between devices, local(): lax.psum_scatter(sum_gate_up.astype(jnp.bfloat16), 'fsdp', scatter_dimens...  123 us
    psum x1, waiting for transfers between devices, local(): lax.psum(share_qkv.astype(jnp.bfloat16), 'ctx').astype(jnp.float32)  93.2 us
    dot_general x8, matrix products, contract_rows(): lax.dot_general(left, right, (((0,), (0,)), ((), ())), preferred_element_...  76.5 us
    reduce_scatter x1, waiting for transfers between devices, local(): lax.psum_scatter(sum_down.astype(jnp.bfloat16), 'fsdp', scatter_dimension...  76.5 us
    dot_general x8, matrix products, contract_cols(): lax.dot_general(left, right, (((1,), (1,)), ((), ())), preferred_element_...  52.8 us
    all_gather x1, waiting for transfers between devices, local(): lax.all_gather(w_down, 'fsdp', axis=0, tiled=True)  35.3 us
    dot_general x4, matrix products, local(): jnp.einsum('tjd,kd->jtk', grad_group, value_group, preferred_element_type...  30 us
    unnamed x2, blocking collectives  29.4 us
  transfers between devices with their start and end apart: 13, of which 9 were waited for; matrix products, arithmetic and copies ran while one was open for 27% of the time, Pallas kernels for 0%

commit v1 on v0

v1 whole, which is shorter than its diff:
```python
import functools
import math

import jax
import jax.numpy as jnp
import numpy as np
from jax import lax
from jax.experimental import pallas as pl
from jax.experimental.pallas import tpu as pltpu
from jax.sharding import PartitionSpec as P

HQ = 14
KVH = 2
HD = 64
EPSILON = 1e-06
ROPE_BASE = 1000000.0
NEGATIVE = -1e30
TP = 4
LANES = 128
CHUNK = 256
BF = jnp.bfloat16
F32 = jnp.float32
MESH = pl.DeviceIdType.MESH
VMEM_LIMIT = 60 * 1024 * 1024


def flip1(v):
    return v + 1 - 2 * (v % 2)


def flip2(v):
    return v + 2 - 4 * ((v // 2) % 2)


def dot(a, b):
    return jnp.dot(a, b, preferred_element_type=F32)


def dot_nt(a, b):
    return lax.dot_general(a, b, (((1,), (1,)), ((), ())), preferred_element_type=F32)


class Links:
    def __init__(self, send_sems, recv_sems):
        self.send_sems, self.recv_sems = send_sems, recv_sems
        self.started = []

    def put(self, src, dst, device):
        at = len(self.started)
        copy = pltpu.make_async_remote_copy(
            src_ref=src,
            dst_ref=dst,
            send_sem=self.send_sems.at[at],
            recv_sem=self.recv_sems.at[at],
            device_id=device,
            device_id_type=MESH,
        )
        copy.start()
        self.started.append((copy, device))
        return at

    def arrive(self, at, slot):
        pltpu.make_async_remote_copy(
            src_ref=slot,
            dst_ref=slot,
            send_sem=self.send_sems.at[at],
            recv_sem=self.recv_sems.at[at],
            device_id=self.started[at][1],
            device_id_type=MESH,
        ).wait_recv()

    def drain(self):
        for copy, _ in self.started:
            copy.wait_send()


def enter(devices):
    barrier = pltpu.get_barrier_semaphore()
    for device in devices:
        pl.semaphore_signal(barrier, inc=1, device_id=device, device_id_type=MESH)
    pl.semaphore_wait(barrier, len(devices))


def gather_kernel(
    n, wq, wo, sm, wgu, wd, gd, wq_all, wo_all, sm_all, wgu_t, wd_t, gd_all, send, recv, here
):
    replicas = n // TP
    f, c = lax.axis_index("fsdp"), lax.axis_index("ctx")
    t, r = f % TP, f // TP
    sib, par, cross = (flip1(f), c), (flip2(f), c), (flip2(flip1(f)), c)
    peers = [((f + TP * j) % n, c) for j in range(1, replicas)]
    back = [(f - TP * j + n) % n for j in range(1, replicas)]
    rback = [(r - j + replicas) % replicas for j in range(1, replicas)]
    enter([sib, par, cross] + peers)
    links = Links(send, recv)
    local = []

    def keep(src, dst):
        copy = pltpu.make_async_copy(src, dst, here.at[len(local)])
        copy.start()
        local.append(copy)

    pending = []
    both = []
    for own, every in ((wq, wq_all), (wo, wo_all), (sm, sm_all)):
        ys = [links.put(own, every.at[f], peer) for peer in peers]
        x = links.put(own, every.at[f], par)
        s = links.put(own, every.at[f], sib)
        keep(own, every.at[f])
        both.append((every, ys, x, s))
    gd_x = links.put(gd, gd_all.at[t], par)
    gd_s = links.put(gd, gd_all.at[t], sib)
    keep(gd, gd_all.at[t])
    gu_s = links.put(wgu.at[flip1(t)], wgu_t.at[r, t], sib)
    gu_x = links.put(wgu.at[flip2(t)], wgu_t.at[r, t], par)
    gu_c = links.put(wgu.at[flip2(flip1(t))], wgu_t.at[r, t], cross)
    keep(wgu.at[t], wgu_t.at[r, t])
    for j, peer in enumerate(peers):
        at = links.put(wgu.at[t], wgu_t.at[r, t], peer)
        pending.append((at, wgu_t.at[rback[j], t]))
        at = links.put(wd, wd_t.at[r], peer)
        pending.append((at, wd_t.at[rback[j]]))
    keep(wd, wd_t.at[r])
    later = []
    for every, ys, x, s in both:
        pending.append((s, every.at[flip1(f)]))
        for j, at in enumerate(ys):
            links.arrive(at, every.at[back[j]])
            at_x = links.put(every.at[back[j]], every.at[back[j]], par)
            later.append((every, at_x, flip2(back[j])))
            at_s = links.put(every.at[back[j]], every.at[back[j]], sib)
            pending.append((at_s, every.at[flip1(back[j])]))
        links.arrive(x, every.at[flip2(f)])
        at_s = links.put(every.at[flip2(f)], every.at[flip2(f)], sib)
        pending.append((at_s, every.at[flip2(flip1(f))]))
    for at, other in ((gu_s, flip1(t)), (gu_x, flip2(t)), (gu_c, flip2(flip1(t)))):
        links.arrive(at, wgu_t.at[r, other])
        for j, peer in enumerate(peers):
            at_y = links.put(wgu_t.at[r, other], wgu_t.at[r, other], peer)
            pending.append((at_y, wgu_t.at[rback[j], other]))
    for every, at, slot in later:
        links.arrive(at, every.at[slot])
        at_s = links.put(every.at[slot], every.at[slot], sib)
        pending.append((at_s, every.at[flip1(slot)]))
    links.arrive(gd_x, gd_all.at[flip2(t)])
    at_s = links.put(gd_all.at[flip2(t)], gd_all.at[flip2(t)], sib)
    pending.append((at_s, gd_all.at[flip2(flip1(t))]))
    pending.append((gd_s, gd_all.at[flip1(t)]))
    for at, slot in pending:
        links.arrive(at, slot)
    links.drain()
    for copy in local:
        copy.wait()


def gather_weights(n, wq, wo, sm, wgu, wd, gd):
    replicas = n // TP
    copies = 3 * ((replicas - 1) * 4 + 3) + 3 + (replicas - 1) * 5 + 3
    anywhere = pl.BlockSpec(memory_space=pl.ANY)
    shapes = (
        jax.ShapeDtypeStruct((n,) + wq.shape, BF),
        jax.ShapeDtypeStruct((n,) + wo.shape, BF),
        jax.ShapeDtypeStruct((n,) + sm.shape, BF),
        jax.ShapeDtypeStruct((replicas,) + wgu.shape, BF),
        jax.ShapeDtypeStruct((replicas,) + wd.shape, BF),
        jax.ShapeDtypeStruct((TP,) + gd.shape, BF),
    )
    return pl.pallas_call(
        functools.partial(gather_kernel, n),
        out_shape=shapes,
        in_specs=[anywhere] * 6,
        out_specs=[anywhere] * 6,
        scratch_shapes=[
            pltpu.SemaphoreType.DMA((copies,)),
            pltpu.SemaphoreType.DMA((copies,)),
            pltpu.SemaphoreType.DMA((6,)),
        ],
        compiler_params=pltpu.CompilerParams(collective_id=0, has_side_effects=True),
        name="gather_weights",
    )(wq, wo, sm, wgu, wd, gd)


def begin_of(natural, lens, m, count):
    begin = jnp.zeros_like(natural)
    end = jnp.int32(0)
    for j in range(count):
        piece = lens[m, j]
        end = end + piece
        begin = begin + jnp.where(end <= natural, piece, 0)
    return begin


def fill_tables(m, rows, c, freq, order, lens, cos_ref, sin_ref):
    block = rows // 2
    lane = lax.broadcasted_iota(jnp.int32, (block, LANES), 1)
    low = (lane % HD) < (HD // 2)
    for b in range(2):
        natural = order[m, c * 2 + b] * block + lax.broadcasted_iota(
            jnp.int32, (block, LANES), 0
        )
        position = natural - begin_of(natural, lens, m, lens.shape[1])
        angle = position.astype(F32) * freq[0:1, :]
        at = m * rows + b * block
        cos_ref[at : at + block, :] = jnp.cos(angle)
        sine = jnp.sin(angle)
        sin_ref[at : at + block, :] = jnp.where(low, -sine, sine)


def swap_halves(u):
    lane = lax.broadcasted_iota(jnp.int32, u.shape, 1)
    low = (lane % HD) < (HD // 2)
    return jnp.where(low, pltpu.roll(u, LANES - HD // 2, 1), pltpu.roll(u, HD // 2, 1))


def fill_bias(m, rows, c, order, lens, bias_ref):
    block = rows // 2
    lane = lax.broadcasted_iota(jnp.int32, (1, rows), 1)
    query = jnp.where(
        lane < block,
        order[m, c * 2] * block + lane,
        order[m, c * 2 + 1] * block + lane - block,
    )
    begin = begin_of(query, lens, m, lens.shape[1])

    def body(k, carry):
        key = order[m, k] * block + lax.broadcasted_iota(jnp.int32, (block, rows), 0)
        allowed = (key <= query) & (key >= begin)
        at = pl.multiple_of(k * block, block)
        bias_ref[pl.ds(at, block), :] = jnp.where(allowed, 0.0, NEGATIVE)
        return carry

    lax.fori_loop(0, order.shape[1], body, 0)


def fill_heads(whole, var_ref):
    rolled = pltpu.roll(whole, HD, 1)
    low = lax.broadcasted_iota(jnp.int32, whole.shape, 1) < HD
    var_ref[0, 0] = jnp.where(low, whole, 0.0).astype(BF)
    var_ref[0, 1] = jnp.where(low, 0.0, rolled).astype(BF)
    var_ref[1, 0] = jnp.where(low, rolled, 0.0).astype(BF)
    var_ref[1, 1] = jnp.where(low, 0.0, whole).astype(BF)


def fill_heads_turned(whole, var_ref):
    turned = whole.T
    rolled = jnp.concatenate([turned[HD:], turned[:HD]], axis=0)
    low = lax.broadcasted_iota(jnp.int32, turned.shape, 0) < HD
    var_ref[0, 0] = jnp.where(low, turned, 0.0).astype(BF)
    var_ref[0, 1] = jnp.where(low, 0.0, rolled).astype(BF)
    var_ref[1, 0] = jnp.where(low, rolled, 0.0).astype(BF)
    var_ref[1, 1] = jnp.where(low, 0.0, turned).astype(BF)


def inverse_norm(v):
    return lax.rsqrt(jnp.mean(v * v, axis=1, keepdims=True) + EPSILON)


def forward_kernel(
    size, order, lens, x, wq, wo, bias_qkv, gain_attn, gain_mlp, freq,
    h2, x2, qs, kv, lse, obt,
    cos_ref, sin_ref, bias_ref, kvar, vvar, ob, land, send, recv, out_sem,
):
    micro, rows, ctx = size
    group = HQ // KVH
    pairs = HQ // 2
    width = HQ * HD
    f, c = lax.axis_index("fsdp"), lax.axis_index("ctx")
    others = [(f, (c + j) % ctx) for j in range(1, ctx)]
    back = [(c - j + ctx) % ctx for j in range(1, ctx)]
    enter(others)
    links = Links(send, recv)
    arrivals = []
    for m in range(micro):
        fill_tables(m, rows, c, freq, order, lens, cos_ref, sin_ref)
    for m in range(micro):
        stream = x[m].astype(F32)
        h1 = (stream * inverse_norm(stream) * gain_attn[...]).astype(BF)
        project = dot(h1, wq[...]) + bias_qkv[...]
        cosine = cos_ref[m * rows : (m + 1) * rows, :]
        sine = sin_ref[m * rows : (m + 1) * rows, :]
        keys = project[:, width : width + LANES]
        keys = keys * cosine + swap_halves(keys) * sine
        land[m, c, :, :LANES] = keys.astype(BF)
        land[m, c, :, LANES:] = project[:, width + LANES :].astype(BF)
        arrivals.append([links.put(land.at[m, c], land.at[m, c], other) for other in others])
        for p in range(pairs):
            query = project[:, p * LANES : (p + 1) * LANES]
            query = query * cosine + swap_halves(query) * sine
            qs[m, p] = (query.astype(BF).astype(F32) * (1.0 / math.sqrt(HD))).astype(BF)
    out_copies = []
    for m in range(micro):
        fill_bias(m, rows, c, order, lens, bias_ref)
        for at, source in zip(arrivals[m], back):
            links.arrive(at, land.at[m, source])
        copy = pltpu.make_async_copy(land.at[m], kv.at[m], out_sem.at[m])
        copy.start()
        out_copies.append(copy)
        both = land[m].reshape(ctx * rows, 2 * LANES).astype(F32)
        fill_heads(both[:, :LANES], kvar)
        fill_heads_turned(both[:, LANES:], vvar)

        def pair(p, carry):
            query = qs[m, p]
            mixed = jnp.zeros((LANES, rows), F32)
            for parity in range(2):
                head = 2 * p + parity
                g = head // group
                scores = dot_nt(kvar[g, parity], query) + bias_ref[...]
                top = jnp.max(scores, axis=0, keepdims=True)
                probs = jnp.exp(scores - top)
                total = jnp.sum(probs, axis=0, keepdims=True)
                mixed = mixed + dot(vvar[g, parity], probs.astype(BF)) / total
                lse[m, pl.ds(head, 1), :] = top + jnp.log(total)
            at = pl.multiple_of(p * LANES, LANES)
            obt[m, pl.ds(at, LANES), :] = mixed.astype(BF)
            ob[:, pl.ds(at, LANES)] = mixed.T.astype(BF)
            return carry

        lax.fori_loop(0, pairs, pair, 0)
        middle = x[m].astype(F32) + dot(ob[...], wo[...])
        x2[m] = middle
        h2[m] = (middle * inverse_norm(middle) * gain_mlp[...]).astype(BF)
    links.drain()
    for copy in out_copies:
        copy.wait()


def attention_forward(ctx, order, lens, x, wq, wo, bias_qkv, gain_attn, gain_mlp, freq):
    micro, rows, width = x.shape
    keys = rows * ctx
    vmem = pl.BlockSpec(memory_space=pltpu.VMEM)
    smem = pl.BlockSpec(memory_space=pltpu.SMEM)
    copies = micro * (ctx - 1)
    return pl.pallas_call(
        functools.partial(forward_kernel, (micro, rows, ctx)),
        out_shape=(
            jax.ShapeDtypeStruct((micro, rows, width), BF),
            jax.ShapeDtypeStruct((micro, rows, width), F32),
            jax.ShapeDtypeStruct((micro, HQ // 2, rows, LANES), BF),
            jax.ShapeDtypeStruct((micro, ctx, rows, 2 * LANES), BF),
            jax.ShapeDtypeStruct((micro, HQ, rows), F32),
            jax.ShapeDtypeStruct((micro, HQ * HD, rows), BF),
        ),
        in_specs=[smem, smem] + [vmem] * 7,
        out_specs=[vmem, vmem, vmem, pl.BlockSpec(memory_space=pl.ANY), vmem, vmem],
        scratch_shapes=[
            pltpu.VMEM((micro * rows, LANES), F32),
            pltpu.VMEM((micro * rows, LANES), F32),
            pltpu.VMEM((keys, rows), F32),
            pltpu.VMEM((KVH, 2, keys, LANES), BF),
            pltpu.VMEM((KVH, 2, LANES, keys), BF),
            pltpu.VMEM((rows, HQ * HD), BF),
            pltpu.VMEM((micro, ctx, rows, 2 * LANES), BF),
            pltpu.SemaphoreType.DMA((copies,)),
            pltpu.SemaphoreType.DMA((copies,)),
            pltpu.SemaphoreType.DMA((micro,)),
        ],
        compiler_params=pltpu.CompilerParams(
            collective_id=1, has_side_effects=True, vmem_limit_bytes=VMEM_LIMIT
        ),
        name="attention_forward",
    )(order, lens, x, wq, wo, bias_qkv, gain_attn, gain_mlp, freq)


def mlp_kernel(
    size, h2, gd, wgu, wd,
    out, gh2, grads,
    hbuf, turned_h, turned_g, acc_out, acc_gh, dgate, dup, ddown,
    sib_out, sib_in, par_out, par_in, keep_sum, stage, send, recv, out_sem,
):
    micro, rows, width, replicas, padded = size
    quarter = replicas * padded
    both = 2 * rows
    f, c = lax.axis_index("fsdp"), lax.axis_index("ctx")
    t = f % TP
    core = t % 2
    mine, theirs = t - core, flip2(t) - core
    sib, par = (flip1(f), c), (flip2(f), c)
    enter([sib, par])
    links = Links(send, recv)
    from_sib, from_par = [], []
    for m in range(micro):
        hbuf[m, t] = h2[m]
        from_sib.append(links.put(hbuf.at[m, t], hbuf.at[m, t], sib))
        from_par.append(links.put(hbuf.at[m, t], hbuf.at[m, t], par))
    from_cross = [None] * micro

    def forward_on(m):
        links.arrive(from_par[m], hbuf.at[m, flip2(t)])
        from_cross[m] = links.put(hbuf.at[m, flip2(t)], hbuf.at[m, flip2(t)], sib)

    def chunk(m, side, first, j):
        at = pl.multiple_of(j * CHUNK, CHUNK)
        up_at = pl.multiple_of(quarter + j * CHUNK, CHUNK)
        hidden_in = hbuf[m, pl.ds(side, 2)].reshape(both, width)
        grad_in = gd[m, pl.ds(side, 2)].reshape(both, width)
        w_gate = wgu[:, pl.ds(at, CHUNK)]
        w_up = wgu[:, pl.ds(up_at, CHUNK)]
        w_down = wd[pl.ds(at, CHUNK), :]
        gate = dot(hidden_in, w_gate)
        up = dot(hidden_in, w_up)
        gm = dot_nt(grad_in, w_down)
        sg = 0.5 * jnp.tanh(0.5 * gate) + 0.5
        silu = gate * sg
        mb = (silu * up).astype(BF)
        ggate = (gm * up * (sg + silu * (1.0 - sg))).astype(BF)
        gup = (gm * silu).astype(BF)
        acc_out[...] += dot(mb, w_down)
        acc_gh[...] += dot_nt(ggate, w_gate) + dot_nt(gup, w_up)
        if first:
            dgate[:, pl.ds(at, CHUNK)] = dot(turned_h[...], ggate)
            dup[:, pl.ds(at, CHUNK)] = dot(turned_h[...], gup)
            ddown[:, pl.ds(at, CHUNK)] = dot(turned_g[...], mb)
        else:
            dgate[:, pl.ds(at, CHUNK)] += dot(turned_h[...], ggate)
            dup[:, pl.ds(at, CHUNK)] += dot(turned_h[...], gup)
            ddown[:, pl.ds(at, CHUNK)] += dot(turned_g[...], mb)

    def compute(m, side, first, middle):
        turned_h[...] = hbuf[m, pl.ds(side, 2)].reshape(both, width).T
        turned_g[...] = gd[m, pl.ds(side, 2)].reshape(both, width).T
        acc_out[...] = jnp.zeros_like(acc_out)
        acc_gh[...] = jnp.zeros_like(acc_gh)
        chunks = quarter // CHUNK

        def body(j, carry):
            chunk(m, side, first, j)
            return carry

        lax.fori_loop(0, 1, body, 0)
        middle()
        lax.fori_loop(1, chunks, body, 0)

    def share(step):
        here = pl.multiple_of(core * rows, rows)
        there = pl.multiple_of(rows - core * rows, rows)
        ats = []
        for k, acc in enumerate((acc_gh, acc_out)):
            sib_out[step, k] = acc[pl.ds(there, rows), :].astype(BF)
            ats.append(links.put(sib_out.at[step, k], sib_in.at[step, k], sib))
            keep_sum[k] = acc[pl.ds(here, rows), :]
        return ats

    def pass_on(step, m, ats):
        got = []
        for k, at in enumerate(ats):
            links.arrive(at, sib_in.at[step, k])
            par_out[m, k] = (keep_sum[k] + sib_in[step, k].astype(F32)).astype(BF)
            got.append(links.put(par_out.at[m, k], par_in.at[m, k], par))
        return got

    def stay(step, m, ats):
        for k, at in enumerate(ats):
            links.arrive(at, sib_in.at[step, k])
            (gh2, out)[k][m] = keep_sum[k] + sib_in[step, k].astype(F32)

    def finish(m, ats):
        for k, (at, ref) in enumerate(zip(ats, (gh2, out))):
            links.arrive(at, par_in.at[m, k])
            ref[m] = ref[m] + par_in[m, k].astype(F32)

    plan = [(0, True)] + [(m, False) for m in range(micro)] + [(m, True) for m in range(1, micro)]
    waiting = None
    sums = [None] * micro
    ready_own = [False] * micro
    for step, (m, own) in enumerate(plan):
        if own:
            links.arrive(from_sib[m], hbuf.at[m, flip1(t)])
        else:
            links.arrive(from_cross[m], hbuf.at[m, flip2(flip1(t))])

        def middle(step=step):
            if step < micro:
                forward_on(step)
            if step > 0:
                last_m, last_own = plan[step - 1]
                if last_own:
                    stay(step - 1, last_m, waiting)
                else:
                    sums[last_m] = pass_on(step - 1, last_m, waiting)

        compute(m, mine if own else theirs, step == 0, middle)
        waiting = share(step)
    high = width // (replicas * TP)
    copies = []
    for replica in range(replicas):
        for k in range(TP + 2):
            slot = len(copies) % 2
            if len(copies) >= 2:
                copies[-2].wait()
            if k < TP:
                piece = slice((replica * TP + k) * high, (replica * TP + k + 1) * high)
                stage[slot, :, :quarter] = dgate[piece, :].astype(BF)
                stage[slot, :, quarter:] = dup[piece, :].astype(BF)
            else:
                for q in range(2 * replicas):
                    at = (k - TP) * 2 * replicas + q
                    stage[slot, :, q * padded : (q + 1) * padded] = ddown[
                        at * high : (at + 1) * high, replica * padded : (replica + 1) * padded
                    ].astype(BF)
            copy = pltpu.make_async_copy(stage.at[slot], grads.at[replica, k], out_sem.at[slot])
            copy.start()
            copies.append(copy)
    last_m, last_own = plan[-1]
    if last_own:
        stay(len(plan) - 1, last_m, waiting)
    else:
        sums[last_m] = pass_on(len(plan) - 1, last_m, waiting)
    for m in range(micro):
        finish(m, sums[m])
    for copy in copies[-2:]:
        copy.wait()
    links.drain()


def mlp(n, h2, gd, wgu, wd):
    micro, rows, width = h2.shape
    replicas = n // TP
    padded = wd.shape[0] // replicas
    quarter = replicas * padded
    vmem = pl.BlockSpec(memory_space=pltpu.VMEM)
    steps = 2 * micro
    copies = micro * 3 + steps * 2 + micro * 2
    return pl.pallas_call(
        functools.partial(mlp_kernel, (micro, rows, width, replicas, padded)),
        out_shape=(
            jax.ShapeDtypeStruct((micro, rows, width), F32),
            jax.ShapeDtypeStruct((micro, rows, width), F32),
            jax.ShapeDtypeStruct((replicas, TP + 2, width // n, 2 * quarter), BF),
        ),
        in_specs=[vmem] * 4,
        out_specs=[vmem, vmem, pl.BlockSpec(memory_space=pl.ANY)],
        scratch_shapes=[
            pltpu.VMEM((micro, TP, rows, width), BF),
            pltpu.VMEM((width, 2 * rows), BF),
            pltpu.VMEM((width, 2 * rows), BF),
            pltpu.VMEM((2 * rows, width), F32),
            pltpu.VMEM((2 * rows, width), F32),
            pltpu.VMEM((width, quarter), F32),
            pltpu.VMEM((width, quarter), F32),
            pltpu.VMEM((width, quarter), F32),
            pltpu.VMEM((steps, 2, rows, width), BF),
            pltpu.VMEM((steps, 2, rows, width), BF),
            pltpu.VMEM((micro, 2, rows, width), BF),
            pltpu.VMEM((micro, 2, rows, width), BF),
            pltpu.VMEM((2, rows, width), F32),
            pltpu.VMEM((2, width // n, 2 * quarter), BF),
            pltpu.SemaphoreType.DMA((copies,)),
            pltpu.SemaphoreType.DMA((copies,)),
            pltpu.SemaphoreType.DMA((2,)),
        ],
        compiler_params=pltpu.CompilerParams(
            collective_id=2, has_side_effects=True, vmem_limit_bytes=VMEM_LIMIT
        ),
        name="mlp",
    )(h2, gd, wgu, wd)


def backward_kernel(
    size, order, lens, gh2, x2, gy, x, wq, wo, gain_attn, gain_mlp, freq, qs, kv, lse, obt,
    dx, dwq, dwo, dbias, dgain_attn, dgain_mlp,
    cos_ref, sin_ref, bias_ref, kvar, kvar_turned, vvar, gx2, go_ref, gp, gk, gv, part, land,
    send, recv,
):
    micro, rows, ctx = size
    group = HQ // KVH
    pairs = HQ // 2
    width = HQ * HD
    scale = 1.0 / math.sqrt(HD)
    f, c = lax.axis_index("fsdp"), lax.axis_index("ctx")
    others = [(f, (c + j) % ctx) for j in range(1, ctx)]
    back = [(c - j + ctx) % ctx for j in range(1, ctx)]
    enter(others)
    links = Links(send, recv)
    arrivals = []
    for m in range(micro):
        fill_tables(m, rows, c, freq, order, lens, cos_ref, sin_ref)
        stream = x2[m]
        inverse = inverse_norm(stream)
        normed = stream * inverse
        grad = gh2[m]
        term = jnp.sum(grad * normed, axis=0, keepdims=True)
        dgain_mlp[...] = term if m == 0 else dgain_mlp[...] + term
        grad = grad * gain_mlp[...]
        grad = gy[m].astype(F32) + inverse * (
            grad - normed * jnp.mean(grad * normed, axis=1, keepdims=True)
        )
        gx2[m] = grad
        low = grad.astype(BF)
        term = dot(obt[m], low)
        dwo[...] = term if m == 0 else dwo[...] + term
        spread = dot_nt(low, wo[...]).astype(BF)
        for p in range(pairs):
            go_ref[m, p] = spread[:, p * LANES : (p + 1) * LANES]
    for m in range(micro):
        fill_bias(m, rows, c, order, lens, bias_ref)
        both = kv[m].reshape(ctx * rows, 2 * LANES).astype(F32)
        fill_heads(both[:, :LANES], kvar)
        fill_heads_turned(both[:, :LANES], kvar_turned)
        fill_heads(both[:, LANES:], vvar)
        gk[...] = jnp.zeros_like(gk)
        gv[...] = jnp.zeros_like(gv)
        cosine = cos_ref[m * rows : (m + 1) * rows, :]
        sine = sin_ref[m * rows : (m + 1) * rows, :]

        def pair(p, carry):
            query = qs[m, p]
            go = go_ref[m, p]
            grad_query = jnp.zeros((LANES, rows), F32)
            for parity in range(2):
                head = 2 * p + parity
                g = head // group
                scores = dot_nt(kvar[g, parity], query) + bias_ref[...]
                probs = jnp.exp(scores - lse[m, pl.ds(head, 1), :])
                grad_probs = dot_nt(vvar[g, parity], go)
                delta = jnp.sum(probs * grad_probs, axis=0, keepdims=True)
                grad_scores = (probs * (grad_probs - delta)).astype(BF)
                grad_query = grad_query + dot(kvar_turned[g, parity], grad_scores)
                gk[g, parity] += dot(grad_scores, query)
                gv[g, parity] += dot(probs.astype(BF), go)
            turned = grad_query.T * scale
            turned = turned * cosine - swap_halves(turned) * sine
            at = pl.multiple_of(p * LANES, LANES)
            gp[m * rows : (m + 1) * rows, pl.ds(at, LANES)] = turned.astype(BF)
            return carry

        lax.fori_loop(0, pairs, pair, 0)
        low = lax.broadcasted_iota(jnp.int32, (ctx * rows, LANES), 1) < HD
        for k, acc in enumerate((gk, gv)):
            first = acc[0, 0] + pltpu.roll(acc[0, 1], HD, 1)
            second = pltpu.roll(acc[1, 0], HD, 1) + acc[1, 1]
            merged = jnp.where(low, first, second).astype(BF)
            part[m, :, :, k * LANES : (k + 1) * LANES] = merged.reshape(ctx, rows, LANES)
        arrivals.append(
            [
                links.put(part.at[m, other[1]], land.at[m, c], other)
                for other in others
            ]
        )
    for m in range(micro):
        total = part[m, c].astype(F32)
        for at, source in zip(arrivals[m], back):
            links.arrive(at, land.at[m, source])
            total = total + land[m, source].astype(F32)
        cosine = cos_ref[m * rows : (m + 1) * rows, :]
        sine = sin_ref[m * rows : (m + 1) * rows, :]
        grad_keys = total[:, :LANES]
        grad_keys = grad_keys * cosine - swap_halves(grad_keys) * sine
        gp[m * rows : (m + 1) * rows, width : width + LANES] = grad_keys.astype(BF)
        gp[m * rows : (m + 1) * rows, width + LANES :] = total[:, LANES:].astype(BF)
    for m in range(micro):
        grad_project = gp[m * rows : (m + 1) * rows, :]
        stream = x[m].astype(F32)
        inverse = inverse_norm(stream)
        normed = stream * inverse
        h1 = (normed * gain_attn[...]).astype(BF)
        term = dot(h1.T, grad_project)
        dwq[...] = term if m == 0 else dwq[...] + term
        term = jnp.sum(grad_project.astype(F32), axis=0, keepdims=True)
        dbias[...] = term if m == 0 else dbias[...] + term
        grad = dot_nt(grad_project, wq[...])
        term = jnp.sum(grad * normed, axis=0, keepdims=True)
        dgain_attn[...] = term if m == 0 else dgain_attn[...] + term
        grad = grad * gain_attn[...]
        dx[m] = gx2[m] + inverse * (
            grad - normed * jnp.mean(grad * normed, axis=1, keepdims=True)
        )
    links.drain()


def attention_backward(
    ctx, order, lens, gh2, x2, gy, x, wq, wo, gain_attn, gain_mlp, freq, qs, kv, lse, obt
):
    micro, rows, width = x.shape
    keys = rows * ctx
    vmem = pl.BlockSpec(memory_space=pltpu.VMEM)
    smem = pl.BlockSpec(memory_space=pltpu.SMEM)
    copies = micro * (ctx - 1)
    return pl.pallas_call(
        functools.partial(backward_kernel, (micro, rows, ctx)),
        out_shape=(
            jax.ShapeDtypeStruct((micro, rows, width), F32),
            jax.ShapeDtypeStruct(wq.shape, F32),
            jax.ShapeDtypeStruct(wo.shape, F32),
            jax.ShapeDtypeStruct((1, wq.shape[1]), F32),
            jax.ShapeDtypeStruct((1, width), F32),
            jax.ShapeDtypeStruct((1, width), F32),
        ),
        in_specs=[smem, smem] + [vmem] * 13,
        out_specs=[vmem] * 6,
        scratch_shapes=[
            pltpu.VMEM((micro * rows, LANES), F32),
            pltpu.VMEM((micro * rows, LANES), F32),
            pltpu.VMEM((keys, rows), F32),
            pltpu.VMEM((KVH, 2, keys, LANES), BF),
            pltpu.VMEM((KVH, 2, LANES, keys), BF),
            pltpu.VMEM((KVH, 2, keys, LANES), BF),
            pltpu.VMEM((micro, rows, width), F32),
            pltpu.VMEM((micro, HQ // 2, rows, LANES), BF),
            pltpu.VMEM((micro * rows, wq.shape[1]), BF),
            pltpu.VMEM((KVH, 2, keys, LANES), F32),
            pltpu.VMEM((KVH, 2, keys, LANES), F32),
            pltpu.VMEM((micro, ctx, rows, 2 * LANES), BF),
            pltpu.VMEM((micro, ctx, rows, 2 * LANES), BF),
            pltpu.SemaphoreType.DMA((copies,)),
            pltpu.SemaphoreType.DMA((copies,)),
        ],
        compiler_params=pltpu.CompilerParams(
            collective_id=3, has_side_effects=True, vmem_limit_bytes=VMEM_LIMIT
        ),
        name="attention_backward",
    )(order, lens, gh2, x2, gy, x, wq, wo, gain_attn, gain_mlp, freq, qs, kv, lse, obt)


def add_pieces(dst, a, b, width):
    def body(k, carry):
        at = pl.multiple_of(k * 512, 512)
        dst[:, pl.ds(at, 512)] = (
            a[:, pl.ds(at, 512)].astype(F32) + b[:, pl.ds(at, 512)].astype(F32)
        ).astype(BF)
        return carry

    lax.fori_loop(0, width // 512, body, 0)


def reduce_kernel(
    n, ctx, grads, att,
    out_gu, out_rest,
    peer_in, core_in, core_sum, par_in, par_sum, ring_in,
    total, pre_in, suf_in, pre_out, suf_out, final, land,
    send, recv, pre_s, pre_r, suf_s, suf_r, fin_s, fin_r, here,
):
    replicas = n // TP
    wide = grads.shape[-1]
    slim = att.shape[-1]
    pieces = TP + 3
    f, c = lax.axis_index("fsdp"), lax.axis_index("ctx")
    t, r = f % TP, f // TP
    core, side = t % 2, t // 2
    sib, par, cross = (flip1(f), c), (flip2(f), c), (flip2(flip1(f)), c)
    peers = [((f + TP * j) % n, c) for j in range(1, replicas)]
    barrier = pltpu.get_barrier_semaphore()
    around = [sib, par, cross] + peers
    for device in around:
        pl.semaphore_signal(barrier, inc=1, device_id=device, device_id_type=MESH)
    left, right = (f, (c + ctx - 1) % ctx), (f, (c + 1) % ctx)
    for device in (left, right):
        pl.semaphore_signal(barrier, inc=1, device_id=device, device_id_type=MESH)
    pl.semaphore_wait(barrier, len(around) + 2)
    links = Links(send, recv)
    to_sib = links.put(att.at[:, :, 1 - core], core_in, sib)
    to_peers = [
        links.put(grads.at[(r + j + 1) % replicas], peer_in.at[j], peer)
        for j, peer in enumerate(peers)
    ]
    links.arrive(to_sib, core_in)
    for replica in range(replicas):
        for s in range(2):
            add_pieces(
                core_sum.at[replica, s], att.at[replica, s, core], core_in.at[replica, s], slim
            )
    to_par = links.put(core_sum.at[:, 1 - side], par_in, par)
    links.arrive(to_par, par_in)
    for replica in range(replicas):
        add_pieces(par_sum.at[replica], core_sum.at[replica, side], par_in.at[replica], slim)
    ring = [
        links.put(par_sum.at[(r + j + 1) % replicas], ring_in.at[j], peer)
        for j, peer in enumerate(peers)
    ]
    for j, at in enumerate(to_peers):
        links.arrive(at, peer_in.at[j])
        for k in range(TP + 2):
            add_pieces(
                total.at[k], grads.at[r, k] if j == 0 else total.at[k], peer_in.at[j, k], wide
            )
    for j, at in enumerate(ring):
        links.arrive(at, ring_in.at[j])
        source = par_sum.at[r] if j == 0 else total.at[TP + 2, :, pl.ds(0, slim)]
        add_pieces(total.at[TP + 2, :, pl.ds(0, slim)], source, ring_in.at[j], slim)

    def scan_copy(k, src, dst, s, q, device):
        return pltpu.make_async_remote_copy(
            src_ref=src.at[k],
            dst_ref=dst.at[k],
            send_sem=s.at[k],
            recv_sem=q.at[k],
            device_id=device,
            device_id_type=MESH,
        )

    def scan(k, order_at, src, got, s, q, ahead):
        @pl.when(order_at > 0)
        def _():
            scan_copy(k, src, got, s, q, ahead).wait_recv()

        @pl.when(order_at < ctx - 1)
        def _():
            @pl.when(order_at > 0)
            def _():
                add_pieces(src.at[k], total.at[k], got.at[k], wide)

            @pl.when(order_at == 0)
            def _():
                local = pltpu.make_async_copy(total.at[k], src.at[k], here.at[0])
                local.start()
                local.wait()

            scan_copy(k, src, got, s, q, ahead).start()

    def finish(k):
        @pl.when(c > 0)
        def _():
            add_pieces(final.at[k], total.at[k], pre_in.at[k], wide)

        @pl.when(c == 0)
        def _():
            add_pieces(final.at[k], total.at[k], suf_in.at[k], wide)

        @pl.when((c > 0) & (c < ctx - 1))
        def _():
            add_pieces(final.at[k], final.at[k], suf_in.at[k], wide)

        @pl.when((k < TP) & (k != t))
        def _():
            pltpu.make_async_remote_copy(
                src_ref=final.at[k],
                dst_ref=land.at[t],
                send_sem=fin_s.at[k],
                recv_sem=fin_r.at[t],
                device_id=(f - t + k, c),
                device_id_type=MESH,
            ).start()

    late = jnp.maximum(c, ctx - 1 - c)

    def tick(time, carry):
        k = time - c

        @pl.when((k >= 0) & (k < pieces))
        def _():
            scan(k, c, pre_out, pre_in, pre_s, pre_r, right)

        k2 = time - (ctx - 1 - c)

        @pl.when((k2 >= 0) & (k2 < pieces))
        def _():
            scan(k2, ctx - 1 - c, suf_out, suf_in, suf_s, suf_r, left)

        k3 = time - late

        @pl.when((k3 >= 0) & (k3 < pieces))
        def _():
            finish(k3)

        return carry

    lax.fori_loop(0, pieces + ctx - 1, tick, 0)
    out_rest[...] = final[TP:].astype(F32)
    for k in range(TP):
        @pl.when(k == t)
        def _():
            out_gu[k] = final[k].astype(F32)

        @pl.when(k != t)
        def _():
            copy = pltpu.make_async_remote_copy(
                src_ref=final.at[k],
                dst_ref=land.at[k],
                send_sem=fin_s.at[k],
                recv_sem=fin_r.at[k],
                device_id=(f - t + k, c),
                device_id_type=MESH,
            )
            copy.wait_recv()
            copy.wait_send()
            out_gu[k] = land[k].astype(F32)

    def settle(k, carry):
        @pl.when(c < ctx - 1)
        def _():
            scan_copy(k, pre_out, pre_in, pre_s, pre_r, right).wait_send()

        @pl.when(c > 0)
        def _():
            scan_copy(k, suf_out, suf_in, suf_s, suf_r, left).wait_send()

        return carry

    lax.fori_loop(0, pieces, settle, 0)
    links.drain()


def reduce_grads(n, ctx, grads, att):
    replicas = n // TP
    _, _, high, wide = grads.shape
    slim = att.shape[-1]
    pieces = TP + 3
    copies = 2 + 2 * (replicas - 1)
    vmem = pl.BlockSpec(memory_space=pltpu.VMEM)
    sems = pltpu.SemaphoreType.DMA
    piece = pltpu.VMEM((pieces, high, wide), BF)
    return pl.pallas_call(
        functools.partial(reduce_kernel, n, ctx),
        out_shape=(
            jax.ShapeDtypeStruct((TP, high, wide), F32),
            jax.ShapeDtypeStruct((3, high, wide), F32),
        ),
        in_specs=[vmem, vmem],
        out_specs=[vmem, vmem],
        scratch_shapes=[
            pltpu.VMEM((replicas - 1, TP + 2, high, wide), BF),
            pltpu.VMEM((replicas, 2, high, slim), BF),
            pltpu.VMEM((replicas, 2, high, slim), BF),
            pltpu.VMEM((replicas, high, slim), BF),
            pltpu.VMEM((replicas, high, slim), BF),
            pltpu.VMEM((replicas - 1, high, slim), BF),
            piece, piece, piece, piece, piece, piece,
            pltpu.VMEM((TP, high, wide), BF),
            sems((copies,)), sems((copies,)),
            sems((pieces,)), sems((pieces,)), sems((pieces,)), sems((pieces,)),
            sems((TP,)), sems((TP,)), sems((1,)),
        ],
        compiler_params=pltpu.CompilerParams(
            collective_id=4, has_side_effects=True, vmem_limit_bytes=VMEM_LIMIT
        ),
        name="reduce_grads",
    )(grads, att)


def pad_to(v, axis, size):
    pads = [(0, 0)] * v.ndim
    pads[axis] = (0, size - v.shape[axis])
    return jnp.pad(v, pads)


def local(
    inputs, cotangent, lengths, order, w_qkv, b_qkv, w_out, norm_attn, norm_mlp, w_gate_up, w_down
):
    n = lax.axis_size("fsdp")
    ctx = lax.axis_size("ctx")
    replicas = n // TP
    x, gy = inputs[0], cotangent[0]
    micro, rows, width = x.shape
    high = w_gate_up.shape[0]
    units = w_down.shape[0]
    padded = -(-units // LANES) * LANES
    quarter = replicas * padded
    proj = w_qkv.shape[1]
    qk = (HQ + KVH) * HD
    vw = KVH * HD

    wgu = w_gate_up.reshape(high, 2, replicas, TP, units)
    wgu = pad_to(wgu.transpose(3, 0, 1, 2, 4), 4, padded).reshape(TP, high, 2 * quarter)
    wd = pad_to(w_down, 0, padded)
    small = jnp.concatenate(
        [
            pad_to(b_qkv, 0, 2 * LANES).reshape(2, LANES),
            pad_to(norm_attn, 0, LANES)[None],
            pad_to(norm_mlp, 0, LANES)[None],
            jnp.zeros((12, LANES), BF),
        ]
    )
    wq_all, wo_all, sm_all, wgu_t, wd_t, gd_all = gather_weights(
        n, w_qkv, w_out, small, wgu, wd, gy
    )
    wq_all = wq_all.reshape(width, proj)
    wo_all = wo_all.reshape(width, width)
    bias = sm_all[:, :2].reshape(n, 2 * LANES)[:, : b_qkv.shape[0]].reshape(1, proj).astype(F32)
    gain_attn = sm_all[:, 2, :high].reshape(1, width).astype(F32)
    gain_mlp = sm_all[:, 3, :high].reshape(1, width).astype(F32)
    wgu_t = wgu_t.reshape(width, 2 * quarter)
    wd_t = wd_t.reshape(quarter, width)

    half = HD // 2
    freqs = np.power(np.float32(ROPE_BASE), -(np.arange(half, dtype=np.float32) * (2.0 / HD)))
    freq = jnp.asarray(np.tile(freqs.astype(np.float32), (8, LANES // half)))
    h2, x2, qs, kv, lse, obt = attention_forward(
        ctx, order[0], lengths[0], x, wq_all, wo_all, bias, gain_attn, gain_mlp, freq
    )
    gd_all = gd_all.transpose(1, 0, 2, 3)
    out, gh2, grads = mlp(n, h2, gd_all, wgu_t, wd_t)
    outputs = (x2 + out).astype(BF)
    dx, dwq, dwo, dbias, dgain_attn, dgain_mlp = attention_backward(
        ctx, order[0], lengths[0], gh2, x2, gy, x, wq_all, wo_all, gain_attn, gain_mlp, freq,
        qs, kv, lse, obt,
    )
    vectors = jnp.stack(
        [
            pad_to(dbias[0, :qk].reshape(n, qk // n), 1, LANES),
            pad_to(dbias[0, qk:].reshape(n, vw // n), 1, LANES),
            pad_to(dgain_attn.reshape(n, high), 1, LANES),
            pad_to(dgain_mlp.reshape(n, high), 1, LANES),
        ],
        axis=1,
    )
    slim = -(-(proj + width + LANES) // 512) * 512
    att = jnp.concatenate(
        [dwq.reshape(n, high, proj), dwo.reshape(n, high, width), pad_to(vectors, 1, high)], axis=2
    ).astype(BF)
    att = pad_to(att, 2, slim).reshape(replicas, 2, 2, high, slim)
    out_gu, out_rest = reduce_grads(n, ctx, grads, att)
    g_gu = out_gu.reshape(TP, high, 2, replicas, padded)[..., :units]
    g_gu = g_gu.transpose(1, 2, 3, 0, 4).reshape(high, 2 * replicas * TP * units)
    g_down = out_rest[:2].reshape(2, high, 2 * replicas, padded).transpose(0, 2, 1, 3)
    g_down = g_down.reshape(width, padded)[:, :units].T
    last = out_rest[2]
    g_qkv = last[:, :proj]
    g_out = last[:, proj : proj + width]
    vec = last[:4, proj + width : proj + width + LANES]
    return (
        outputs[None],
        dx[None],
        g_qkv,
        vec[0, : qk // n],
        vec[1, : vw // n],
        g_out,
        vec[2, :high],
        vec[3, :high],
        g_gu,
        g_down,
    )


def solution(mesh):
    return jax.shard_map(
        local,
        mesh=mesh,
        in_specs=(
            P("fsdp", None, "ctx", None),
            P("fsdp", None, "ctx", None),
            P("fsdp", None, None),
            P("fsdp", None, None),
            P("fsdp", None),
            P("fsdp"),
            P("fsdp", None),
            P("fsdp"),
            P("fsdp"),
            P("fsdp", None),
            P("fsdp", None),
        ),
        out_specs=(
            P("fsdp", None, "ctx", None),
            P("fsdp", None, "ctx", None),
            P("fsdp", None),
            P("fsdp"),
            P("fsdp"),
            P("fsdp", None),
            P("fsdp"),
            P("fsdp"),
            P("fsdp", None),
            P("fsdp", None),
        ),
        check_vma=False,
    )
```

time: 865 us -> 591 us (0.68)
  the two profiles are of different devices: /device:TPU:0 before, /device:TPU:4 now
where the time goes in v1:
time: 591 us; the launch traced here: 582 us
  Pallas kernels  514 us (87%)
  local copies, waits for them, and re-layouts  58 us (10%)
  other arithmetic  8.96 us (2%)
    pallas_call x1, Pallas kernels, reduce_grads(): pl.pallas_call(functools.partial(reduce_kernel, n, ctx), out_shape=(jax.S...  215 us
    pallas_call x1, Pallas kernels, gather_weights(): pl.pallas_call(functools.partial(gather_kernel, n), out_shape=shapes, in_...  97.1 us
    pallas_call x1, Pallas kernels, mlp(): pl.pallas_call(functools.partial(mlp_kernel, (micro, rows, width, replica...  87 us
    pallas_call x1, Pallas kernels, attention_backward(): pl.pallas_call(functools.partial(backward_kernel, (micro, rows, ctx)), ou...  68.9 us
    pallas_call x1, Pallas kernels, attention_forward(): pl.pallas_call(functools.partial(forward_kernel, (micro, rows, ctx)), out...  45.5 us

profile of v1, /device:TPU:4, one launch (start us, length us, event | category | flops | bytes accessed | tf_op | source)
XLA Modules:
  0.0 582.2 jit_solution(17722034453549883591)
XLA Ops:
  0.6 0.7 pad_bitcast_fusion.5
  1.3 0.1 pad.62.clone
  1.4 0.7 pad_bitcast_fusion.3
  2.1 0.7 maximum_maximum_fusion.sm
  2.7 2.3 pad.46.wd
  5.1 5.5 reshape.120
  10.5 1.8 copy.42
  12.3 1.9 pad.45
  14.2 2.7 reshape.121.wgu
  16.9 97.1 %gather_weights.1 = (bf16[8,112,1152]{2,1,0:T(8,128)(2,1)}, bf16[8,112,896]{2,1,0:T(8,128)(2,1)}, bf16[8,16,128]{2,1,0:T(8,128)(2,1)}, bf16[2,4,112,2560]{3,2,1,...) custom-call(bf16[112,1152]{1,0:T(8,128)(2,1)} %wq.1, bf16[112,896]{1,0:T(8,128)(2,1)} %wo.1, ...), custom_call_target="tpu_custom_call" | custom-call | tf_op jit(solution)/shard_map/gather_weights/pallas_call | solution.py:168
  114.1 0.7 slice_bitcast_fusion.3
  114.8 0.8 convert_reduce_fusion
  115.7 0.7 reshape.138.gain_mlp
  116.3 0.7 reshape.137.gain_attn
  117.0 0.7 reshape.136.bias_qkv
  117.7 4.2 copy.40
  121.8 45.5 %attention_forward.1 = (bf16[2,256,896]{2,1,0:T(8,128)(2,1)}, f32[2,256,896]{2,1,0:T(8,128)}, bf16[2,7,256,128]{3,2,1,0:T(8,128)(2,1)}, bf16[2,4,256,256]{3,2,1,...) custom-call(s32[2,8]{1,0:T(2,128)} %bitcast.79, s32[2,4]{1,0:T(2,128)} %bitcast.81, ...), custom_call_target="tpu_custom_call" | custom-call | tf_op jit(solution)/shard_map/attention_forward/pallas_call | solution.py:334
  167.3 0.0 copy-start
  167.3 87.0 %mlp.1 = (f32[2,256,896]{2,1,0:T(8,128)}, f32[2,256,896]{2,1,0:T(8,128)}, bf16[2,6,112,2560]{3,2,1,0:T(8,128)(2,1)}) custom-call(bf16[2,256,896]{2,1,0:T(8,128)(2,1)} %get-tuple-element.37.h2, bf16[2,4,256,896]{3,2,1,0:T(8,128)(2,1)} %bitcast.60, bf16[896,2560]{1,0:T(8,128)(2,1)} %bitcast.70, bf16[1280,896]{1,0:T(8,128)(2,1)} %bitcast.75), custom_call_target="tpu_custom_call" | custom-call | tf_op jit(solution)/shard_map/mlp/pallas_call | solution.py:524
  254.4 2.6 fusion.2
  257.0 68.9 %attention_backward.1 = (f32[2,256,896]{2,1,0:T(8,128)}, f32[896,1152]{1,0:T(8,128)}, f32[896,896]{1,0:T(8,128)}, f32[1,1152]{1,0:T(1,128)}, f32[1,896]{1,0:T(1,128)}, /*index=5*/f32[1,896]{1,0:T(1,128)}) custom-call(s32[2,8]{1,0:T(2,128)} %bitcast.80, s32[2,4]{1,0:T(2,128)} %bitcast.82, f32[2,256,896]{2,1,0:T(8,128)} %get-tuple-element.42.gh2, ...), custom_call_target="tpu_custom_call" | custom-call | tf_op jit(solution)/shard_map/attention_backward/pallas_call | solution.py:679
  325.9 0.7 convert_reduce_fusion.3
  326.6 0.1 reshape.129
  326.7 0.7 convert_reduce_fusion.2
  327.4 0.1 reshape.130
  327.5 0.7 convert.41
  328.3 0.1 reshape_squeeze.3
  328.4 2.2 convert.40
  330.6 0.9 copy-done.1
  331.5 0.2 convert.39
  331.7 0.3 fusion.1
  332.1 2.6 pad.51
  334.6 215.4 %reduce_grads.1 = (f32[4,112,2560]{2,1,0:T(8,128)}, f32[3,112,2560]{2,1,0:T(8,128)}) custom-call(bf16[2,6,112,2560]{3,2,1,0:T(8,128)(2,1)} %get-tuple-element.48.grads, bf16[2,2,2,112,2560]{4,3,2,1,0:T(8,128)(2,1)} %bitcast.59), custom_call_target="tpu_custom_call" | custom-call | tf_op jit(solution)/shard_map/reduce_grads/pallas_call | solution.py:902
  550.0 6.5 %reshape.132 = f32[4,112,2,2,640]{4,3,2,1,0:T(2,128)} reshape(f32[4,112,2560]{2,1,0:T(8,128)} %get-tuple-element.55) | data formatting | bytes 9175040 | tf_op jit(solution)/shard_map/reshape | solution.py:1002
  556.5 3.9 slice_bitcast_fusion
  560.4 5.0 copy.30
  565.4 6.5 %reshape.133 = f32[112,9728]{1,0:T(8,128)} reshape(f32[112,2,2,4,608]{4,3,2,1,0:T(4,128)} %copy.30) | data formatting | bytes 8716288 | tf_op jit(solution)/shard_map/reshape | solution.py:1003
  571.9 1.3 slice_bitcast_fusion.2
  573.2 1.8 slice.69
  575.0 0.1 copy.41
  575.2 0.1 slice_bitcast_fusion.1
  575.3 2.0 copy.32
  577.4 0.5 slice_bitcast_fusion.6
  577.9 0.5 slice_bitcast_fusion.7
  578.4 0.5 slice_bitcast_fusion.4
  578.9 0.8 slice.77
  579.7 0.8 slice.74
  580.5 1.2 copy.45
  (14 shorter events, 0.1 us)
Async XLA Ops:
  167.3 87.1 %copy-start = (f32[2,256,896]{2,1,0:T(8,128)S(1)}, f32[2,256,896]{2,1,0:T(8,128)}, u32[]{:S(2)}) copy-start(f32[2,256,896]{2,1,0:T(8,128)} %get-tuple-element.36.x2) | copy-start | bytes 5505028
  328.4 3.1 copy-start.1
  577.4 3.1 copy-start.2

commit v2 on v1

--- a/solution.py
+++ b/solution.py
@@ -18,6 +18,10 @@
 TP = 4
 LANES = 128
 CHUNK = 256
+PIECES = 3 * TP
+ALL_PIECES = PIECES + 2
+RING = 4
+VEC = 32
 BF = jnp.bfloat16
 F32 = jnp.float32
 MESH = pl.DeviceIdType.MESH
@@ -484,17 +488,16 @@
     high = width // (replicas * TP)
     copies = []
     for replica in range(replicas):
-        for k in range(TP + 2):
+        for k in range(PIECES):
             slot = len(copies) % 2
             if len(copies) >= 2:
                 copies[-2].wait()
-            if k < TP:
-                piece = slice((replica * TP + k) * high, (replica * TP + k + 1) * high)
-                stage[slot, :, :quarter] = dgate[piece, :].astype(BF)
-                stage[slot, :, quarter:] = dup[piece, :].astype(BF)
+            if k < 2 * TP:
+                at = (replica * TP + k // 2) * high
+                stage[slot] = (dgate, dup)[k % 2][at : at + high, :].astype(BF)
             else:
-                for q in range(2 * replicas):
-                    at = (k - TP) * 2 * replicas + q
+                for q in range(replicas):
+                    at = (k - 2 * TP) * replicas + q
                     stage[slot, :, q * padded : (q + 1) * padded] = ddown[
                         at * high : (at + 1) * high, replica * padded : (replica + 1) * padded
                     ].astype(BF)
@@ -526,7 +529,7 @@
         out_shape=(
             jax.ShapeDtypeStruct((micro, rows, width), F32),
             jax.ShapeDtypeStruct((micro, rows, width), F32),
-            jax.ShapeDtypeStruct((replicas, TP + 2, width // n, 2 * quarter), BF),
+            jax.ShapeDtypeStruct((replicas, PIECES, width // n, quarter), BF),
         ),
         in_specs=[vmem] * 4,
         out_specs=[vmem, vmem, pl.BlockSpec(memory_space=pl.ANY)],
@@ -544,7 +547,7 @@
             pltpu.VMEM((micro, 2, rows, width), BF),
             pltpu.VMEM((micro, 2, rows, width), BF),
             pltpu.VMEM((2, rows, width), F32),
-            pltpu.VMEM((2, width // n, 2 * quarter), BF),
+            pltpu.VMEM((2, width // n, quarter), BF),
             pltpu.SemaphoreType.DMA((copies,)),
             pltpu.SemaphoreType.DMA((copies,)),
             pltpu.SemaphoreType.DMA((2,)),
@@ -556,21 +559,323 @@
     )(h2, gd, wgu, wd)
 
 
+def add_into(dst, a, b):
+    width = dst.shape[-1]
+    step = 256 if width % 256 == 0 else LANES
+
+    def body(k, carry):
+        at = pl.ds(pl.multiple_of(k * step, step), step)
+        dst[:, at] = (a[:, at].astype(F32) + b[:, at].astype(F32)).astype(BF)
+        return carry
+
+    lax.fori_loop(0, width // step, body, 0)
+
+
+class Sums:
+    def __init__(self, n, ctx, grads, fin, scratch):
+        self.n, self.ctx, self.grads, self.fin = n, ctx, grads, fin
+        (
+            self.total, self.peer_in, self.pre, self.suf, self.suf_out, self.land,
+            self.core_o, self.par_o, self.ring_o, self.core_q, self.par_q, self.ring_q,
+            self.vec, self.vec_in,
+            self.ys, self.yr, self.ps, self.pr, self.ss, self.sr, self.fs, self.fr,
+            self.asend, self.arecv, self.own_sem, self.out_sem,
+        ) = scratch
+        self.replicas = n // TP
+        self.f, self.c = lax.axis_index("fsdp"), lax.axis_index("ctx")
+        f, c = self.f, self.c
+        self.t, self.r = f % TP, f // TP
+        self.core, self.side = self.t % 2, self.t // 2
+        self.sib, self.par, self.cross = (flip1(f), c), (flip2(f), c), (flip2(flip1(f)), c)
+        self.peers = [((f + TP * j) % n, c) for j in range(1, self.replicas)]
+        self.left, self.right = (f, (c + ctx - 1) % ctx), (f, (c + 1) % ctx)
+        self.links = Links(self.asend, self.arecv)
+
+    @staticmethod
+    def scratch(n, high, wide, width, proj):
+        replicas = n // TP
+        sems = pltpu.SemaphoreType.DMA
+        peers = replicas - 1
+        return [
+            pltpu.VMEM((ALL_PIECES, high, wide), BF),
+            pltpu.VMEM((peers, PIECES, high, wide), BF),
+            pltpu.VMEM((ALL_PIECES, high, wide), BF),
+            pltpu.VMEM((ALL_PIECES, high, wide), BF),
+            pltpu.VMEM((RING, high, wide), BF),
+            pltpu.VMEM((2 * TP, high, wide), BF),
+            pltpu.VMEM((replicas, 2, high, width), BF),
+            pltpu.VMEM((replicas, high, width), BF),
+            pltpu.VMEM((peers, high, width), BF),
+            pltpu.VMEM((replicas, 2, high, proj), BF),
+            pltpu.VMEM((replicas, high, proj), BF),
+            pltpu.VMEM((peers, high, proj), BF),
+            pltpu.VMEM((3, VEC, LANES), F32),
+            pltpu.VMEM((2 + peers, VEC, LANES), F32),
+            sems((peers * PIECES,)), sems((peers * PIECES,)),
+            sems((ALL_PIECES,)), sems((ALL_PIECES,)), sems((ALL_PIECES,)), sems((ALL_PIECES,)),
+            sems((2 * TP,)), sems((2 * TP,)),
+            sems((6 + 3 * peers,)), sems((6 + 3 * peers,)), sems((1,)), sems((ALL_PIECES,)),
+        ]
+
+    def around(self):
+        return [self.sib, self.par, self.cross] + self.peers + [self.left, self.right]
+
+    def peer_copy(self, j, k):
+        at = j * PIECES + k
+        return pltpu.make_async_remote_copy(
+            src_ref=self.grads.at[(self.r + j + 1) % self.replicas, k],
+            dst_ref=self.peer_in.at[j, k],
+            send_sem=self.ys.at[at],
+            recv_sem=self.yr.at[at],
+            device_id=self.peers[j],
+            device_id_type=MESH,
+        )
+
+    def own_copy(self):
+        return pltpu.make_async_copy(
+            self.grads.at[self.r], self.total.at[pl.ds(0, PIECES)], self.own_sem.at[0]
+        )
+
+    def start(self, ahead):
+        self.own_copy().start()
+        for k in range(ahead):
+            for j in range(self.replicas - 1):
+                self.peer_copy(j, k).start()
+        self.ahead = ahead
+
+    def pre_copy(self, k, src):
+        return pltpu.make_async_remote_copy(
+            src_ref=src.at[k], dst_ref=self.pre.at[k], send_sem=self.ps.at[k],
+            recv_sem=self.pr.at[k], device_id=self.right, device_id_type=MESH,
+        )
+
+    def suf_copy(self, k, src):
+        return pltpu.make_async_remote_copy(
+            src_ref=src, dst_ref=self.suf.at[k], send_sem=self.ss.at[k],
+            recv_sem=self.sr.at[k], device_id=self.left, device_id_type=MESH,
+        )
+
+    def fin_copy(self, k, slot):
+        return pltpu.make_async_remote_copy(
+            src_ref=self.suf.at[k], dst_ref=self.land.at[slot], send_sem=self.fs.at[k],
+            recv_sem=self.fr.at[slot], device_id=(self.f - self.t + k // 2, self.c),
+            device_id_type=MESH,
+        )
+
+    def out_copy(self, k, src):
+        return pltpu.make_async_copy(src.at[k], self.fin.at[k], self.out_sem.at[k])
+
+    def tick(self, time):
+        c, ctx, total = self.c, self.ctx, self.total
+
+        @pl.when(time + self.ahead < PIECES)
+        def _():
+            for j in range(self.replicas - 1):
+                self.peer_copy(j, time + self.ahead).start()
+
+        @pl.when(time < PIECES)
+        def _():
+            for j in range(self.replicas - 1):
+                self.peer_copy(j, time).wait_recv()
+                add_into(total.at[time], total.at[time], self.peer_in.at[j, time])
+
+        k = time - c
+
+        @pl.when((k >= 0) & (k < ALL_PIECES))
+        def _():
+            @pl.when(c > 0)
+            def _():
+                self.pre_copy(k, total).wait_recv()
+                add_into(self.pre.at[k], self.pre.at[k], total.at[k])
+
+                @pl.when(c < ctx - 1)
+                def _():
+                    self.pre_copy(k, self.pre).start()
+
+            @pl.when(c == 0)
+            def _():
+                self.pre_copy(k, total).start()
+
+        k2 = time - (ctx - 1 - c)
+
+        @pl.when((k2 >= 0) & (k2 < ALL_PIECES))
+        def _():
+            @pl.when(c < ctx - 1)
+            def _():
+                self.suf_copy(k2, total.at[k2]).wait_recv()
+
+            @pl.when((c > 0) & (c < ctx - 1))
+            def _():
+                @pl.when(k2 >= RING)
+                def _():
+                    self.suf_copy(k2 - RING, self.suf_out.at[(k2 - RING) % RING]).wait_send()
+
+                add_into(self.suf_out.at[k2 % RING], self.suf.at[k2], total.at[k2])
+                self.suf_copy(k2, self.suf_out.at[k2 % RING]).start()
+
+            @pl.when(c == ctx - 1)
+            def _():
+                self.suf_copy(k2, total.at[k2]).start()
+
+        k3 = time - jnp.maximum(c, ctx - 1 - c)
+
+        @pl.when((k3 >= 0) & (k3 < ALL_PIECES))
+        def _():
+            @pl.when(c == 0)
+            def _():
+                add_into(self.suf.at[k3], self.suf.at[k3], total.at[k3])
+
+            @pl.when((c > 0) & (c < ctx - 1))
+            def _():
+                add_into(self.suf.at[k3], self.suf.at[k3], self.pre.at[k3])
+
+            @pl.when((k3 < 2 * TP) & (k3 // 2 != self.t))
+            def _():
+                @pl.when(c == ctx - 1)
+                def _():
+                    self.fin_copy_from(k3, self.pre).start()
+
+                @pl.when(c < ctx - 1)
+                def _():
+                    self.fin_copy_from(k3, self.suf).start()
+
+            @pl.when((k3 >= 2 * TP) | (k3 // 2 == self.t))
+            def _():
+                @pl.when(c == ctx - 1)
+                def _():
+                    self.out_copy(k3, self.pre).start()
+
+                @pl.when(c < ctx - 1)
+                def _():
+                    self.out_copy(k3, self.suf).start()
+
+    def fin_copy_from(self, k, src):
+        return pltpu.make_async_remote_copy(
+            src_ref=src.at[k], dst_ref=self.land.at[2 * self.t + k % 2], send_sem=self.fs.at[k],
+            recv_sem=self.fr.at[2 * self.t + k % 2],
+            device_id=(self.f - self.t + k // 2, self.c), device_id_type=MESH,
+        )
+
+    @property
+    def ticks(self):
+        return ALL_PIECES + self.ctx - 1
+
+    def close(self):
+        c, ctx = self.c, self.ctx
+
+        def arrive(k, carry):
+            @pl.when(k // 2 != self.t)
+            def _():
+                pltpu.make_async_remote_copy(
+                    src_ref=self.land.at[k], dst_ref=self.land.at[k], send_sem=self.fs.at[k],
+                    recv_sem=self.fr.at[k], device_id=(self.f - self.t + k // 2, c),
+                    device_id_type=MESH,
+                ).wait_recv()
+                self.out_copy(k, self.land).start()
+                self.fin_copy_from(k, self.suf).wait_send()
+
+            return carry
+
+        lax.fori_loop(0, 2 * TP, arrive, 0)
+
+        def settle(k, carry):
+            @pl.when(c < ctx - 1)
+            def _():
+                self.pre_copy(k, self.total).wait_send()
+
+            @pl.when((c == ctx - 1) | ((c > 0) & (k >= ALL_PIECES - RING)))
+            def _():
+                self.suf_copy(k, self.total.at[k]).wait_send()
+
+            self.out_copy(k, self.suf).wait()
+            return carry
+
+        lax.fori_loop(0, ALL_PIECES, settle, 0)
+
+        def peers(k, carry):
+            for j in range(self.replicas - 1):
+                self.peer_copy(j, k).wait_send()
+            return carry
+
+        lax.fori_loop(0, PIECES, peers, 0)
+        self.links.drain()
+
+
+    def fold(self, own, got_core, got_par, got_ring, place, extra=None):
+        replicas = self.replicas
+        at = self.links.put(own.at[:, :, 1 - self.core], got_core, self.sib)
+        at_vec = None
+        if extra is not None:
+            at_vec = self.links.put(self.vec.at[0], self.vec_in.at[0], self.sib)
+        yield
+        self.links.arrive(at, got_core)
+        for replica in range(replicas):
+            for s in range(2):
+                add_into(
+                    got_core.at[replica, s], got_core.at[replica, s],
+                    own.at[replica, s, self.core],
+                )
+        at = self.links.put(got_core.at[:, 1 - self.side], got_par, self.par)
+        if extra is not None:
+            self.links.arrive(at_vec, self.vec_in.at[0])
+            self.vec[1] = self.vec[0] + self.vec_in[0]
+            at_vec = self.links.put(self.vec.at[1], self.vec_in.at[1], self.par)
+        yield
+        self.links.arrive(at, got_par)
+        for replica in range(replicas):
+            add_into(got_par.at[replica], got_par.at[replica], got_core.at[replica, self.side])
+        ats, vec_ats = [], []
+        if extra is not None:
+            self.links.arrive(at_vec, self.vec_in.at[1])
+            self.vec[2] = self.vec[1] + self.vec_in[1]
+        for j, peer in enumerate(self.peers):
+            ats.append(
+                self.links.put(got_par.at[(self.r + j + 1) % replicas], got_ring.at[j], peer)
+            )
+            if extra is not None:
+                vec_ats.append(self.links.put(self.vec.at[2], self.vec_in.at[2 + j], peer))
+        yield
+        width = got_ring.shape[-1]
+        for j, at in enumerate(ats):
+            self.links.arrive(at, got_ring.at[j])
+            source = got_par.at[self.r] if j == 0 else place
+            add_into(place, source, got_ring.at[j])
+        if extra is not None:
+            vec = self.vec[2]
+            for j, at in enumerate(vec_ats):
+                self.links.arrive(at, self.vec_in.at[2 + j])
+                vec = vec + self.vec_in[2 + j]
+            extra[...] = vec.astype(BF)
+        yield
+
+
 def backward_kernel(
-    size, order, lens, gh2, x2, gy, x, wq, wo, gain_attn, gain_mlp, freq, qs, kv, lse, obt,
-    dx, dwq, dwo, dbias, dgain_attn, dgain_mlp,
-    cos_ref, sin_ref, bias_ref, kvar, kvar_turned, vvar, gx2, go_ref, gp, gk, gv, part, land,
-    send, recv,
+    size, merged, order, lens, gh2, x2, gy, x, wq, wo, gain_attn, gain_mlp, freq, qs, kv, lse, obt,
+    grads, dx, *rest
 ):
-    micro, rows, ctx = size
+    n, micro, rows, ctx = size
+    outs = 1 if merged else 3
+    fin, rest = rest[:outs], rest[outs:]
+    (
+        cos_ref, sin_ref, bias_ref, kvar, kvar_turned, vvar, go_ref, gp, h1t, gk, gv, part, land,
+        att_o, att_q, vec_wide, send, recv,
+    ), rest = rest[:18], rest[18:]
     group = HQ // KVH
     pairs = HQ // 2
     width = HQ * HD
+    replicas = n // TP
+    high = width // n
+    proj = wq.shape[1]
     scale = 1.0 / math.sqrt(HD)
     f, c = lax.axis_index("fsdp"), lax.axis_index("ctx")
     others = [(f, (c + j) % ctx) for j in range(1, ctx)]
     back = [(c - j + ctx) % ctx for j in range(1, ctx)]
-    enter(others)
+    if merged:
+        sums = Sums(n, ctx, grads, fin[0], rest)
+        enter(others + sums.around())
+        sums.start(2)
+    else:
+        enter(others)
     links = Links(send, recv)
     arrivals = []
     for m in range(micro):
@@ -580,19 +885,33 @@
         normed = stream * inverse
         grad = gh2[m]
         term = jnp.sum(grad * normed, axis=0, keepdims=True)
-        dgain_mlp[...] = term if m == 0 else dgain_mlp[...] + term
+        at = proj + width
+        vec_wide[:, at : at + width] = term if m == 0 else vec_wide[:, at : at + width] + term
         grad = grad * gain_mlp[...]
         grad = gy[m].astype(F32) + inverse * (
             grad - normed * jnp.mean(grad * normed, axis=1, keepdims=True)
         )
-        gx2[m] = grad
-        low = grad.astype(BF)
-        term = dot(obt[m], low)
-        dwo[...] = term if m == 0 else dwo[...] + term
-        spread = dot_nt(low, wo[...]).astype(BF)
+        dx[m] = grad
+        spread = dot_nt(grad.astype(BF), wo[...]).astype(BF)
         for p in range(pairs):
             go_ref[m, p] = spread[:, p * LANES : (p + 1) * LANES]
+    for k in range(n):
+        term = dot(obt[0, k * high : (k + 1) * high, :], dx[0].astype(BF))
+        for m in range(1, micro):
+            term = term + dot(obt[m, k * high : (k + 1) * high, :], dx[m].astype(BF))
+        att_o[k // TP, (k // 2) % 2, k % 2] = term.astype(BF)
+    if merged:
+        sums.total[PIECES] = jnp.zeros(sums.total.shape[1:], BF)
+        sums.total[PIECES + 1] = jnp.zeros(sums.total.shape[1:], BF)
+        sums.own_copy().wait()
+        fold_o = sums.fold(
+            att_o, sums.core_o, sums.par_o, sums.ring_o,
+            sums.total.at[PIECES, :, pl.ds(0, width)],
+        )
+        next(fold_o)
     for m in range(micro):
+        if merged and m > 0:
+            next(fold_o)
         fill_bias(m, rows, c, order, lens, bias_ref)
         both = kv[m].reshape(ctx * rows, 2 * LANES).astype(F32)
         fill_heads(both[:, :LANES], kvar)
@@ -622,6 +941,13 @@
             turned = turned * cosine - swap_halves(turned) * sine
             at = pl.multiple_of(p * LANES, LANES)
             gp[m * rows : (m + 1) * rows, pl.ds(at, LANES)] = turned.astype(BF)
+            if merged:
+                step = m * pairs + p
+
+                @pl.when(step % 3 != 2)
+                def _():
+                    sums.tick(step - step // 3)
+
             return carry
 
         lax.fori_loop(0, pairs, pair, 0)
@@ -629,13 +955,17 @@
         for k, acc in enumerate((gk, gv)):
             first = acc[0, 0] + pltpu.roll(acc[0, 1], HD, 1)
             second = pltpu.roll(acc[1, 0], HD, 1) + acc[1, 1]
-            merged = jnp.where(low, first, second).astype(BF)
-            part[m, :, :, k * LANES : (k + 1) * LANES] = merged.reshape(ctx, rows, LANES)
+            whole = jnp.where(low, first, second).astype(BF)
+            part[m, :, :, k * LANES : (k + 1) * LANES] = whole.reshape(ctx, rows, LANES)
         arrivals.append(
-            [
-                links.put(part.at[m, other[1]], land.at[m, c], other)
-                for other in others
-            ]
+            [links.put(part.at[m, other[1]], land.at[m, c], other) for other in others]
+        )
+    if merged:
+        next(fold_o)
+    for m in range(micro):
+        stream = x[m].astype(F32)
+        h1t[:, m * rows : (m + 1) * rows] = (
+            (stream * inverse_norm(stream) * gain_attn[...]).T.astype(BF)
         )
     for m in range(micro):
         total = part[m, c].astype(F32)
@@ -648,46 +978,90 @@
         grad_keys = grad_keys * cosine - swap_halves(grad_keys) * sine
         gp[m * rows : (m + 1) * rows, width : width + LANES] = grad_keys.astype(BF)
         gp[m * rows : (m + 1) * rows, width + LANES :] = total[:, LANES:].astype(BF)
+    for k in range(n):
+        term = dot(h1t[k * high : (k + 1) * high, :], gp[...])
+        att_q[k // TP, (k // 2) % 2, k % 2] = term.astype(BF)
     for m in range(micro):
         grad_project = gp[m * rows : (m + 1) * rows, :]
         stream = x[m].astype(F32)
         inverse = inverse_norm(stream)
         normed = stream * inverse
-        h1 = (normed * gain_attn[...]).astype(BF)
-        term = dot(h1.T, grad_project)
-        dwq[...] = term if m == 0 else dwq[...] + term
         term = jnp.sum(grad_project.astype(F32), axis=0, keepdims=True)
-        dbias[...] = term if m == 0 else dbias[...] + term
+        vec_wide[:, :proj] = term if m == 0 else vec_wide[:, :proj] + term
         grad = dot_nt(grad_project, wq[...])
         term = jnp.sum(grad * normed, axis=0, keepdims=True)
-        dgain_attn[...] = term if m == 0 else dgain_attn[...] + term
+        at = slice(proj, proj + width)
+        vec_wide[:, at] = term if m == 0 else vec_wide[:, at] + term
         grad = grad * gain_attn[...]
-        dx[m] = gx2[m] + inverse * (
+        dx[m] = dx[m] + inverse * (
             grad - normed * jnp.mean(grad * normed, axis=1, keepdims=True)
         )
+    vec = sums.vec.at[0] if merged else fin[2]
+    vec[...] = jnp.zeros((VEC, LANES), F32)
+    for k in range(vec_wide.shape[1] // LANES):
+        vec[k : k + 1, :] = vec_wide[:, k * LANES : (k + 1) * LANES]
+    if merged:
+        next(fold_o)
+        done = micro * pairs - (micro * pairs) // 3
+        fold_sums(sums, att_q, done, width, proj)
+    else:
+        fin[0][...] = att_o[...]
+        fin[1][...] = att_q[...]
     links.drain()
 
 
+def fold_sums(sums, att_q, done, width, proj):
+    fold_q = sums.fold(
+        att_q, sums.core_q, sums.par_q, sums.ring_q,
+        sums.total.at[PIECES + 1, :, pl.ds(0, proj)],
+        sums.total.at[PIECES + 1, pl.ds(0, VEC), pl.ds(proj, LANES)],
+    )
+    between = max(0, min(2, PIECES - done))
+
+    def body(k, carry):
+        sums.tick(k)
+        return carry
+
+    next(fold_q)
+    for _ in range(between):
+        sums.tick(jnp.int32(done))
+        done += 1
+        next(fold_q)
+    for _ in range(3 - between):
+        next(fold_q)
+    lax.fori_loop(done, sums.ticks, body, 0)
+    sums.close()
+
+
 def attention_backward(
-    ctx, order, lens, gh2, x2, gy, x, wq, wo, gain_attn, gain_mlp, freq, qs, kv, lse, obt
+    n, ctx, order, lens, gh2, x2, gy, x, wq, wo, gain_attn, gain_mlp, freq, qs, kv, lse, obt, grads
 ):
     micro, rows, width = x.shape
     keys = rows * ctx
+    proj = wq.shape[1]
+    replicas = n // TP
+    high, wide = grads.shape[2:]
+    merged = ctx <= 4
     vmem = pl.BlockSpec(memory_space=pltpu.VMEM)
     smem = pl.BlockSpec(memory_space=pltpu.SMEM)
+    anywhere = pl.BlockSpec(memory_space=pl.ANY)
     copies = micro * (ctx - 1)
-    return pl.pallas_call(
-        functools.partial(backward_kernel, (micro, rows, ctx)),
-        out_shape=(
-            jax.ShapeDtypeStruct((micro, rows, width), F32),
-            jax.ShapeDtypeStruct(wq.shape, F32),
-            jax.ShapeDtypeStruct(wo.shape, F32),
-            jax.ShapeDtypeStruct((1, wq.shape[1]), F32),
-            jax.ShapeDtypeStruct((1, width), F32),
-            jax.ShapeDtypeStruct((1, width), F32),
-        ),
-        in_specs=[smem, smem] + [vmem] * 13,
-        out_specs=[vmem] * 6,
+    out_shape = [jax.ShapeDtypeStruct((micro, rows, width), F32)]
+    shape_o = (replicas, 2, 2, high, width)
+    shape_q = (replicas, 2, 2, high, proj)
+    if merged:
+        out_shape += [jax.ShapeDtypeStruct((ALL_PIECES, high, wide), BF)]
+    else:
+        out_shape += [
+            jax.ShapeDtypeStruct(shape_o, BF),
+            jax.ShapeDtypeStruct(shape_q, BF),
+            jax.ShapeDtypeStruct((VEC, LANES), F32),
+        ]
+    result = pl.pallas_call(
+        functools.partial(backward_kernel, (n, micro, rows, ctx), merged),
+        out_shape=out_shape,
+        in_specs=[smem, smem] + [vmem] * 13 + [anywhere],
+        out_specs=[vmem] + ([anywhere] if merged else [vmem] * 3),
         scratch_shapes=[
             pltpu.VMEM((micro * rows, LANES), F32),
             pltpu.VMEM((micro * rows, LANES), F32),
@@ -695,236 +1069,103 @@
             pltpu.VMEM((KVH, 2, keys, LANES), BF),
             pltpu.VMEM((KVH, 2, LANES, keys), BF),
             pltpu.VMEM((KVH, 2, keys, LANES), BF),
-            pltpu.VMEM((micro, rows, width), F32),
             pltpu.VMEM((micro, HQ // 2, rows, LANES), BF),
-            pltpu.VMEM((micro * rows, wq.shape[1]), BF),
+            pltpu.VMEM((micro * rows, proj), BF),
+            pltpu.VMEM((width, micro * rows), BF),
             pltpu.VMEM((KVH, 2, keys, LANES), F32),
             pltpu.VMEM((KVH, 2, keys, LANES), F32),
             pltpu.VMEM((micro, ctx, rows, 2 * LANES), BF),
             pltpu.VMEM((micro, ctx, rows, 2 * LANES), BF),
+            pltpu.VMEM(shape_o, BF),
+            pltpu.VMEM(shape_q, BF),
+            pltpu.VMEM((1, proj + 2 * width), F32),
             pltpu.SemaphoreType.DMA((copies,)),
             pltpu.SemaphoreType.DMA((copies,)),
-        ],
+        ]
+        + (Sums.scratch(n, high, wide, width, proj) if merged else []),
         compiler_params=pltpu.CompilerParams(
             collective_id=3, has_side_effects=True, vmem_limit_bytes=VMEM_LIMIT
         ),
         name="attention_backward",
-    )(order, lens, gh2, x2, gy, x, wq, wo, gain_attn, gain_mlp, freq, qs, kv, lse, obt)
-
-
-def add_pieces(dst, a, b, width):
-    def body(k, carry):
-        at = pl.multiple_of(k * 512, 512)
-        dst[:, pl.ds(at, 512)] = (
-            a[:, pl.ds(at, 512)].astype(F32) + b[:, pl.ds(at, 512)].astype(F32)
-        ).astype(BF)
-        return carry
-
-    lax.fori_loop(0, width // 512, body, 0)
-
-
-def reduce_kernel(
-    n, ctx, grads, att,
-    out_gu, out_rest,
-    peer_in, core_in, core_sum, par_in, par_sum, ring_in,
-    total, pre_in, suf_in, pre_out, suf_out, final, land,
-    send, recv, pre_s, pre_r, suf_s, suf_r, fin_s, fin_r, here,
-):
-    replicas = n // TP
-    wide = grads.shape[-1]
-    slim = att.shape[-1]
-    pieces = TP + 3
-    f, c = lax.axis_index("fsdp"), lax.axis_index("ctx")
-    t, r = f % TP, f // TP
-    core, side = t % 2, t // 2
-    sib, par, cross = (flip1(f), c), (flip2(f), c), (flip2(flip1(f)), c)
-    peers = [((f + TP * j) % n, c) for j in range(1, replicas)]
-    barrier = pltpu.get_barrier_semaphore()
-    around = [sib, par, cross] + peers
-    for device in around:
-        pl.semaphore_signal(barrier, inc=1, device_id=device, device_id_type=MESH)
-    left, right = (f, (c + ctx - 1) % ctx), (f, (c + 1) % ctx)
-    for device in (left, right):
-        pl.semaphore_signal(barrier, inc=1, device_id=device, device_id_type=MESH)
-    pl.semaphore_wait(barrier, len(around) + 2)
-    links = Links(send, recv)
-    to_sib = links.put(att.at[:, :, 1 - core], core_in, sib)
-    to_peers = [
-        links.put(grads.at[(r + j + 1) % replicas], peer_in.at[j], peer)
-        for j, peer in enumerate(peers)
-    ]
-    links.arrive(to_sib, core_in)
-    for replica in range(replicas):
-        for s in range(2):
-            add_pieces(
-                core_sum.at[replica, s], att.at[replica, s, core], core_in.at[replica, s], slim
-            )
-    to_par = links.put(core_sum.at[:, 1 - side], par_in, par)
-    links.arrive(to_par, par_in)
-    for replica in range(replicas):
-        add_pieces(par_sum.at[replica], core_sum.at[replica, side], par_in.at[replica], slim)
-    ring = [
-        links.put(par_sum.at[(r + j + 1) % replicas], ring_in.at[j], peer)
-        for j, peer in enumerate(peers)
-    ]
-    for j, at in enumerate(to_peers):
-        links.arrive(at, peer_in.at[j])
-        for k in range(TP + 2):
-            add_pieces(
-                total.at[k], grads.at[r, k] if j == 0 else total.at[k], peer_in.at[j, k], wide
-            )
-    for j, at in enumerate(ring):
-        links.arrive(at, ring_in.at[j])
-        source = par_sum.at[r] if j == 0 else total.at[TP + 2, :, pl.ds(0, slim)]
-        add_pieces(total.at[TP + 2, :, pl.ds(0, slim)], source, ring_in.at[j], slim)
-
-    def scan_copy(k, src, dst, s, q, device):
-        return pltpu.make_async_remote_copy(
-            src_ref=src.at[k],
-            dst_ref=dst.at[k],
-            send_sem=s.at[k],
-            recv_sem=q.at[k],
-            device_id=device,
-            device_id_type=MESH,
-        )
-
-    def scan(k, order_at, src, got, s, q, ahead):
-        @pl.when(order_at > 0)
-        def _():
-            scan_copy(k, src, got, s, q, ahead).wait_recv()
-
-        @pl.when(order_at < ctx - 1)
-        def _():
-            @pl.when(order_at > 0)
-            def _():
-                add_pieces(src.at[k], total.at[k], got.at[k], wide)
-
-            @pl.when(order_at == 0)
-            def _():
-                local = pltpu.make_async_copy(total.at[k], src.at[k], here.at[0])
-                local.start()
-                local.wait()
-
-            scan_copy(k, src, got, s, q, ahead).start()
-
-    def finish(k):
-        @pl.when(c > 0)
-        def _():
-            add_pieces(final.at[k], total.at[k], pre_in.at[k], wide)
-
-        @pl.when(c == 0)
-        def _():
-            add_pieces(final.at[k], total.at[k], suf_in.at[k], wide)
-
-        @pl.when((c > 0) & (c < ctx - 1))
-        def _():
-            add_pieces(final.at[k], final.at[k], suf_in.at[k], wide)
-
-        @pl.when((k < TP) & (k != t))
-        def _():
-            pltpu.make_async_remote_copy(
-                src_ref=final.at[k],
-                dst_ref=land.at[t],
-                send_sem=fin_s.at[k],
-                recv_sem=fin_r.at[t],
-                device_id=(f - t + k, c),
-                device_id_type=MESH,
-            ).start()
-
-    late = jnp.maximum(c, ctx - 1 - c)
-
-    def tick(time, carry):
-        k = time - c
-
-        @pl.when((k >= 0) & (k < pieces))
-        def _():
-            scan(k, c, pre_out, pre_in, pre_s, pre_r, right)
-
-        k2 = time - (ctx - 1 - c)
-
-        @pl.when((k2 >= 0) & (k2 < pieces))
-        def _():
-            scan(k2, ctx - 1 - c, suf_out, suf_in, suf_s, suf_r, left)
-
-        k3 = time - late
-
-        @pl.when((k3 >= 0) & (k3 < pieces))
-        def _():
-            finish(k3)
-
-        return carry
-
-    lax.fori_loop(0, pieces + ctx - 1, tick, 0)
-    out_rest[...] = final[TP:].astype(F32)
-    for k in range(TP):
-        @pl.when(k == t)
-        def _():
-            out_gu[k] = final[k].astype(F32)
-
-        @pl.when(k != t)
-        def _():
-            copy = pltpu.make_async_remote_copy(
-                src_ref=final.at[k],
-                dst_ref=land.at[k],
-                send_sem=fin_s.at[k],
-                recv_sem=fin_r.at[k],
-                device_id=(f - t + k, c),
-                device_id_type=MESH,
-            )
-            copy.wait_recv()
-            copy.wait_send()
-            out_gu[k] = land[k].astype(F32)
-
-    def settle(k, carry):
-        @pl.when(c < ctx - 1)
-        def _():
-            scan_copy(k, pre_out, pre_in, pre_s, pre_r, right).wait_send()
-
-        @pl.when(c > 0)
-        def _():
-            scan_copy(k, suf_out, suf_in, suf_s, suf_r, left).wait_send()
-
-        return carry
-
-    lax.fori_loop(0, pieces, settle, 0)
-    links.drain()
-
-
-def reduce_grads(n, ctx, grads, att):
-    replicas = n // TP
-    _, _, high, wide = grads.shape
-    slim = att.shape[-1]
-    pieces = TP + 3
-    copies = 2 + 2 * (replicas - 1)
+    )(order, lens, gh2, x2, gy, x, wq, wo, gain_attn, gain_mlp, freq, qs, kv, lse, obt, grads)
+    if merged:
+        return result
+    dx, att_o, att_q, vec = result
+    return dx, reduce_grads(n, ctx, grads, att_o, att_q, vec)
+
+
+def reduce_kernel(n, ctx, grads, att_o, att_q, vec, fin, *scratch):
+    sums = Sums(n, ctx, grads, fin, scratch)
+    width, proj = att_o.shape[-1], att_q.shape[-1]
+    enter(sums.around())
+    sums.start(2)
+    sums.vec[0] = vec[...]
+    sums.total[PIECES] = jnp.zeros(sums.total.shape[1:], BF)
+    sums.total[PIECES + 1] = jnp.zeros(sums.total.shape[1:], BF)
+    sums.own_copy().wait()
+    for _ in sums.fold(
+        att_o, sums.core_o, sums.par_o, sums.ring_o, sums.total.at[PIECES, :, pl.ds(0, width)]
+    ):
+        pass
+    fold_sums(sums, att_q, 0, width, proj)
+
+
+def reduce_grads(n, ctx, grads, att_o, att_q, vec):
+    high, wide = grads.shape[2:]
     vmem = pl.BlockSpec(memory_space=pltpu.VMEM)
-    sems = pltpu.SemaphoreType.DMA
-    piece = pltpu.VMEM((pieces, high, wide), BF)
+    anywhere = pl.BlockSpec(memory_space=pl.ANY)
     return pl.pallas_call(
         functools.partial(reduce_kernel, n, ctx),
-        out_shape=(
-            jax.ShapeDtypeStruct((TP, high, wide), F32),
-            jax.ShapeDtypeStruct((3, high, wide), F32),
-        ),
-        in_specs=[vmem, vmem],
-        out_specs=[vmem, vmem],
-        scratch_shapes=[
-            pltpu.VMEM((replicas - 1, TP + 2, high, wide), BF),
-            pltpu.VMEM((replicas, 2, high, slim), BF),
-            pltpu.VMEM((replicas, 2, high, slim), BF),
-            pltpu.VMEM((replicas, high, slim), BF),
-            pltpu.VMEM((replicas, high, slim), BF),
-            pltpu.VMEM((replicas - 1, high, slim), BF),
-            piece, piece, piece, piece, piece, piece,
-            pltpu.VMEM((TP, high, wide), BF),
-            sems((copies,)), sems((copies,)),
-            sems((pieces,)), sems((pieces,)), sems((pieces,)), sems((pieces,)),
-            sems((TP,)), sems((TP,)), sems((1,)),
-        ],
+        out_shape=jax.ShapeDtypeStruct((ALL_PIECES, high, wide), BF),
+        in_specs=[anywhere, vmem, vmem, vmem],
+        out_specs=anywhere,
+        scratch_shapes=Sums.scratch(n, high, wide, att_o.shape[-1], att_q.shape[-1]),
         compiler_params=pltpu.CompilerParams(
             collective_id=4, has_side_effects=True, vmem_limit_bytes=VMEM_LIMIT
         ),
         name="reduce_grads",
-    )(grads, att)
+    )(grads, att_o, att_q, vec)
+
+
+def finish_kernel(size, fin, g_gu, g_down, g_qkv, g_out, vec, turn):
+    n, units, padded, proj, width = size
+    replicas = n // TP
+    high = width // n
+    for half in range(2):
+        for k in range(TP):
+            whole = fin[2 * k + half].astype(F32)
+            for q in range(replicas):
+                at = ((half * replicas + q) * TP + k) * units
+                g_gu[:, at : at + units] = whole[:, q * padded : q * padded + units]
+    for k in range(n):
+        at = (k % replicas) * padded
+        turn[k * high : (k + 1) * high, :] = fin[2 * TP + k // replicas, :, at : at + padded].astype(
+            F32
+        )
+    g_down[...] = turn[...].T[:units, :]
+    g_out[...] = fin[PIECES, :, :width].astype(F32)
+    g_qkv[...] = fin[PIECES + 1, :, :proj].astype(F32)
+    vec[...] = fin[PIECES + 1, :VEC, proj : proj + LANES].astype(F32)
+
+
+def finish_grads(n, fin, units, padded, proj, width):
+    high = width // n
+    vmem = pl.BlockSpec(memory_space=pltpu.VMEM)
+    return pl.pallas_call(
+        functools.partial(finish_kernel, (n, units, padded, proj, width)),
+        out_shape=(
+            jax.ShapeDtypeStruct((high, 2 * n * units), F32),
+            jax.ShapeDtypeStruct((units, width), F32),
+            jax.ShapeDtypeStruct((high, proj), F32),
+            jax.ShapeDtypeStruct((high, width), F32),
+            jax.ShapeDtypeStruct((VEC, LANES), F32),
+        ),
+        in_specs=[vmem],
+        out_specs=[vmem] * 5,
+        scratch_shapes=[pltpu.VMEM((width, padded), F32)],
+        compiler_params=pltpu.CompilerParams(vmem_limit_bytes=VMEM_LIMIT),
+        name="finish_grads",
+    )(fin)
 
 
 def pad_to(v, axis, size):
@@ -980,42 +1221,26 @@
     gd_all = gd_all.transpose(1, 0, 2, 3)
     out, gh2, grads = mlp(n, h2, gd_all, wgu_t, wd_t)
     outputs = (x2 + out).astype(BF)
-    dx, dwq, dwo, dbias, dgain_attn, dgain_mlp = attention_backward(
-        ctx, order[0], lengths[0], gh2, x2, gy, x, wq_all, wo_all, gain_attn, gain_mlp, freq,
-        qs, kv, lse, obt,
+    dx, fin = attention_backward(
+        n, ctx, order[0], lengths[0], gh2, x2, gy, x, wq_all, wo_all, gain_attn, gain_mlp, freq,
+        qs, kv, lse, obt, grads,
     )
-    vectors = jnp.stack(
-        [
-            pad_to(dbias[0, :qk].reshape(n, qk // n), 1, LANES),
-            pad_to(dbias[0, qk:].reshape(n, vw // n), 1, LANES),
-            pad_to(dgain_attn.reshape(n, high), 1, LANES),
-            pad_to(dgain_mlp.reshape(n, high), 1, LANES),
-        ],
-        axis=1,
-    )
-    slim = -(-(proj + width + LANES) // 512) * 512
-    att = jnp.concatenate(
-        [dwq.reshape(n, high, proj), dwo.reshape(n, high, width), pad_to(vectors, 1, high)], axis=2
-    ).astype(BF)
-    att = pad_to(att, 2, slim).reshape(replicas, 2, 2, high, slim)
-    out_gu, out_rest = reduce_grads(n, ctx, grads, att)
-    g_gu = out_gu.reshape(TP, high, 2, replicas, padded)[..., :units]
-    g_gu = g_gu.transpose(1, 2, 3, 0, 4).reshape(high, 2 * replicas * TP * units)
-    g_down = out_rest[:2].reshape(2, high, 2 * replicas, padded).transpose(0, 2, 1, 3)
-    g_down = g_down.reshape(width, padded)[:, :units].T
-    last = out_rest[2]
-    g_qkv = last[:, :proj]
-    g_out = last[:, proj : proj + width]
-    vec = last[:4, proj + width : proj + width + LANES]
+    g_gu, g_down, g_qkv, g_out, vec = finish_grads(n, fin, units, padded, proj, width)
+    vec = vec.reshape(VEC * LANES)
+    f = lax.axis_index("fsdp")
+
+    def own(first, size):
+        return lax.dynamic_slice(vec, (first + f * size,), (size,))
+
     return (
         outputs[None],
         dx[None],
         g_qkv,
-        vec[0, : qk // n],
-        vec[1, : vw // n],
+        own(0, qk // n),
+        own(qk, vw // n),
         g_out,
-        vec[2, :high],
-        vec[3, :high],
+        own(proj, high),
+        own(proj + width, high),
         g_gu,
         g_down,
     )

time: 591 us -> 449 us (0.76)
  the two profiles are of different devices: /device:TPU:4 before, /device:TPU:0 now
where the time goes in v2:
time: 449 us; the launch traced here: 441 us
  Pallas kernels  411 us (92%)
  local copies, waits for them, and re-layouts  24.4 us (5%)
    pallas_call x1, Pallas kernels, attention_backward(): pl.pallas_call(functools.partial(backward_kernel, (n, micro, rows, ctx),...  170 us
    pallas_call x1, Pallas kernels, gather_weights(): pl.pallas_call(functools.partial(gather_kernel, n), out_shape=shapes, in_...  98.6 us
    pallas_call x1, Pallas kernels, mlp(): pl.pallas_call(functools.partial(mlp_kernel, (micro, rows, width, replica...  90.4 us
    pallas_call x1, Pallas kernels, attention_forward(): pl.pallas_call(functools.partial(forward_kernel, (micro, rows, ctx)), out...  45.8 us

profile of v2, /device:TPU:0, one launch (start us, length us, event | category | flops | bytes accessed | tf_op | source)
XLA Modules:
  0.0 441.0 jit_solution(18290671440937778086)
XLA Ops:
  0.6 0.7 pad_bitcast_fusion
  1.3 0.1 pad.27.clone
  1.4 0.7 pad_bitcast_fusion.2
  2.1 0.7 maximum_maximum_fusion.sm
  2.7 5.5 %reshape.91 = bf16[112,2,2,4,608]{4,3,2,1,0:T(4,128)(2,1)S(1)} reshape(bf16[112,9728]{1,0:T(8,128)(2,1)} %param.21) | data formatting | bytes 4358144 | tf_op jit(solution)/shard_map/reshape | solution.py:1193
  8.2 1.8 copy.29
  10.0 1.9 pad.22
  11.9 0.0 copy-start.3
  11.9 2.7 reshape.92.wgu
  14.6 0.0 copy-done.3
  14.6 1.1 pad.23.wd
  15.7 98.6 %gather_weights.1 = (bf16[8,112,1152]{2,1,0:T(8,128)(2,1)}, bf16[8,112,896]{2,1,0:T(8,128)(2,1)}, bf16[8,16,128]{2,1,0:T(8,128)(2,1)}, bf16[2,4,112,2560]{3,2,1,...) custom-call(bf16[112,1152]{1,0:T(8,128)(2,1)} %wq.1, bf16[112,896]{1,0:T(8,128)(2,1)} %wo.1, ...), custom_call_target="tpu_custom_call" | custom-call | tf_op jit(solution)/shard_map/gather_weights/pallas_call | solution.py:172
  114.4 0.8 convert_reduce_fusion
  115.2 0.7 reshape.100.gain_attn
  115.8 0.7 reshape.101.gain_mlp
  116.5 0.7 slice_bitcast_fusion
  117.2 0.7 reshape.99.bias_qkv
  117.9 0.0 copy-start.1
  117.9 45.8 %attention_forward.1 = (bf16[2,256,896]{2,1,0:T(8,128)(2,1)}, f32[2,256,896]{2,1,0:T(8,128)}, bf16[2,7,256,128]{3,2,1,0:T(8,128)(2,1)}, bf16[2,4,256,256]{3,2,1,...) custom-call(s32[2,8]{1,0:T(2,128)} %bitcast.43, s32[2,4]{1,0:T(2,128)} %bitcast.45, ...), custom_call_target="tpu_custom_call" | custom-call | tf_op jit(solution)/shard_map/attention_forward/pallas_call | solution.py:338
  163.8 0.0 copy-done.1
  163.8 2.2 copy.28
  165.9 90.4 %mlp.1 = (f32[2,256,896]{2,1,0:T(8,128)}, f32[2,256,896]{2,1,0:T(8,128)}, bf16[2,12,112,1280]{3,2,1,0:T(8,128)(2,1)}) custom-call(bf16[2,256,896]{2,1,0:T(8,128)(2,1)} %get-tuple-element.36.h2, bf16[2,4,256,896]{3,2,1,0:T(8,128)(2,1)} %bitcast.29, bf16[896,2560]{1,0:T(8,128)(2,1)} %bitcast.35, bf16[1280,896]{1,0:T(8,128)(2,1)} %bitcast.40), custom_call_target="tpu_custom_call" | custom-call | tf_op jit(solution)/shard_map/mlp/pallas_call | solution.py:527
  256.3 170.2 %attention_backward.1 = (f32[2,256,896]{2,1,0:T(8,128)}, bf16[14,112,1280]{2,1,0:T(8,128)(2,1)}) custom-call(s32[2,8]{1,0:T(2,128)} %bitcast.44, s32[2,4]{1,0:T(2,128)} %bitcast.46, f32[2,256,896]{2,1,0:T(8,128)} %get-tuple-element.41.gh2, f32[2,256,896]{2,1,0:T(8,128)} %get-tuple-element.35.x2, bf16[2,256,896]{2,1,0:T(8,128)(2,1)} %bitcast.39, ...), custom_call_target="tpu_custom_call" | custom-call | tf_op jit(solution)/shard_map/attention_backward/pallas_call | solution.py:1060
  426.6 0.0 copy-start
  426.6 6.1 %finish_grads.1 = (f32[112,9728]{1,0:T(8,128)}, f32[608,896]{1,0:T(8,128)}, f32[112,1152]{1,0:T(8,128)}, f32[112,896]{1,0:T(8,128)}, f32[32,128]{1,0:T(8,128)}) custom-call(bf16[14,112,1280]{2,1,0:T(8,128)(2,1)} %get-tuple-element.48.fin), custom_call_target="tpu_custom_call" | custom-call | tf_op jit(solution)/shard_map/finish_grads/pallas_call | solution.py:1154
  432.7 1.4 fusion.1
  434.0 1.3 dynamic_slice.13
  435.3 1.3 dynamic_slice.12
  436.6 0.0 copy-done
  436.6 0.0 copy-start.2
  436.6 2.7 fusion
  439.3 0.0 copy-done.2
  439.3 1.2 copy.32
  (3 shorter events, 0.0 us)
Async XLA Ops:
  11.9 2.8 copy-start.3
  117.9 45.8 %copy-start.1 = (bf16[4,2,256,896]{3,2,1,0:T(8,128)(2,1)S(1)}, bf16[4,2,256,896]{3,2,1,0:T(8,128)(2,1)}, u32[]{:S(2)}) copy-start(bf16[4,2,256,896]{3,2,1,0:T(8,128)(2,1)} %get-tuple-element.37) | copy-start | bytes 11010052
  426.6 10.0 %copy-start = (f32[2,256,896]{2,1,0:T(8,128)S(1)}, f32[2,256,896]{2,1,0:T(8,128)}, u32[]{:S(2)}) copy-start(f32[2,256,896]{2,1,0:T(8,128)} %get-tuple-element.35.x2) | copy-start | bytes 5505028
  436.6 2.7 copy-start.2

commit v3 on v2

--- a/solution.py
+++ b/solution.py
@@ -18,9 +18,13 @@
 TP = 4
 LANES = 128
 CHUNK = 256
-PIECES = 3 * TP
-ALL_PIECES = PIECES + 2
-RING = 4
+PIECES = 6 * TP
+ALL_PIECES = PIECES + 4
+RING = 6
+HOP = 2
+RATE = 3
+EARLY = 2
+SLOTS = 8
 VEC = 32
 BF = jnp.bfloat16
 F32 = jnp.float32
@@ -60,7 +64,7 @@
             device_id_type=MESH,
         )
         copy.start()
-        self.started.append((copy, device))
+        self.started.append((src, device))
         return at
 
     def arrive(self, at, slot):
@@ -74,8 +78,30 @@
         ).wait_recv()
 
     def drain(self):
-        for copy, _ in self.started:
-            copy.wait_send()
+        for at, (src, device) in enumerate(self.started):
+            pltpu.make_async_remote_copy(
+                src_ref=src,
+                dst_ref=src,
+                send_sem=self.send_sems.at[at],
+                recv_sem=self.recv_sems.at[at],
+                device_id=device,
+                device_id_type=MESH,
+            ).wait_send()
+
+
+class Staged:
+    def __init__(self, pairs, sems):
+        self.copies = [
+            pltpu.make_async_copy(src, dst, sems.at[at]) for at, (src, dst) in enumerate(pairs)
+        ]
+        self.waited = 0
+        for copy in self.copies:
+            copy.start()
+
+    def need(self, count):
+        for copy in self.copies[self.waited : count]:
+            copy.wait()
+        self.waited = max(self.waited, count)
 
 
 def enter(devices):
@@ -112,16 +138,19 @@
         s = links.put(own, every.at[f], sib)
         keep(own, every.at[f])
         both.append((every, ys, x, s))
-    gd_x = links.put(gd, gd_all.at[t], par)
-    gd_s = links.put(gd, gd_all.at[t], sib)
-    keep(gd, gd_all.at[t])
-    gu_s = links.put(wgu.at[flip1(t)], wgu_t.at[r, t], sib)
-    gu_x = links.put(wgu.at[flip2(t)], wgu_t.at[r, t], par)
-    gu_c = links.put(wgu.at[flip2(flip1(t))], wgu_t.at[r, t], cross)
-    keep(wgu.at[t], wgu_t.at[r, t])
+    gd_x = links.put(gd, gd_all.at[:, t], par)
+    gd_s = links.put(gd, gd_all.at[:, t], sib)
+    keep(gd, gd_all.at[:, t])
+    arrivals = []
+    for half in range(2):
+        for other, device in ((flip1(t), sib), (flip2(t), par), (flip2(flip1(t)), cross)):
+            at = links.put(wgu.at[other, half], wgu_t.at[half, r, t], device)
+            arrivals.append((at, half, other))
+        keep(wgu.at[t, half], wgu_t.at[half, r, t])
+        for j, peer in enumerate(peers):
+            at = links.put(wgu.at[t, half], wgu_t.at[half, r, t], peer)
+            pending.append((at, wgu_t.at[half, rback[j], t]))
     for j, peer in enumerate(peers):
-        at = links.put(wgu.at[t], wgu_t.at[r, t], peer)
-        pending.append((at, wgu_t.at[rback[j], t]))
         at = links.put(wd, wd_t.at[r], peer)
         pending.append((at, wd_t.at[rback[j]]))
     keep(wd, wd_t.at[r])
@@ -137,19 +166,19 @@
         links.arrive(x, every.at[flip2(f)])
         at_s = links.put(every.at[flip2(f)], every.at[flip2(f)], sib)
         pending.append((at_s, every.at[flip2(flip1(f))]))
-    for at, other in ((gu_s, flip1(t)), (gu_x, flip2(t)), (gu_c, flip2(flip1(t)))):
-        links.arrive(at, wgu_t.at[r, other])
+    for at, half, other in arrivals:
+        links.arrive(at, wgu_t.at[half, r, other])
         for j, peer in enumerate(peers):
-            at_y = links.put(wgu_t.at[r, other], wgu_t.at[r, other], peer)
-            pending.append((at_y, wgu_t.at[rback[j], other]))
+            at_y = links.put(wgu_t.at[half, r, other], wgu_t.at[half, r, other], peer)
+            pending.append((at_y, wgu_t.at[half, rback[j], other]))
     for every, at, slot in later:
         links.arrive(at, every.at[slot])
         at_s = links.put(every.at[slot], every.at[slot], sib)
         pending.append((at_s, every.at[flip1(slot)]))
-    links.arrive(gd_x, gd_all.at[flip2(t)])
-    at_s = links.put(gd_all.at[flip2(t)], gd_all.at[flip2(t)], sib)
-    pending.append((at_s, gd_all.at[flip2(flip1(t))]))
-    pending.append((gd_s, gd_all.at[flip1(t)]))
+    links.arrive(gd_x, gd_all.at[:, flip2(t)])
+    at_s = links.put(gd_all.at[:, flip2(t)], gd_all.at[:, flip2(t)], sib)
+    pending.append((at_s, gd_all.at[:, flip2(flip1(t))]))
+    pending.append((gd_s, gd_all.at[:, flip1(t)]))
     for at, slot in pending:
         links.arrive(at, slot)
     links.drain()
@@ -159,15 +188,17 @@
 
 def gather_weights(n, wq, wo, sm, wgu, wd, gd):
     replicas = n // TP
-    copies = 3 * ((replicas - 1) * 4 + 3) + 3 + (replicas - 1) * 5 + 3
+    peers = replicas - 1
+    copies = 3 * (4 * peers + 3) + 3 + 2 * (3 + 4 * peers) + peers
     anywhere = pl.BlockSpec(memory_space=pl.ANY)
+    high, quarter = wgu.shape[2:]
     shapes = (
         jax.ShapeDtypeStruct((n,) + wq.shape, BF),
         jax.ShapeDtypeStruct((n,) + wo.shape, BF),
         jax.ShapeDtypeStruct((n,) + sm.shape, BF),
-        jax.ShapeDtypeStruct((replicas,) + wgu.shape, BF),
+        jax.ShapeDtypeStruct((2, replicas, TP, high, quarter), BF),
         jax.ShapeDtypeStruct((replicas,) + wd.shape, BF),
-        jax.ShapeDtypeStruct((TP,) + gd.shape, BF),
+        jax.ShapeDtypeStruct((gd.shape[0], TP) + gd.shape[1:], BF),
     )
     return pl.pallas_call(
         functools.partial(gather_kernel, n),
@@ -177,7 +208,7 @@
         scratch_shapes=[
             pltpu.SemaphoreType.DMA((copies,)),
             pltpu.SemaphoreType.DMA((copies,)),
-            pltpu.SemaphoreType.DMA((6,)),
+            pltpu.SemaphoreType.DMA((7,)),
         ],
         compiler_params=pltpu.CompilerParams(collective_id=0, has_side_effects=True),
         name="gather_weights",
@@ -259,106 +290,149 @@
     return lax.rsqrt(jnp.mean(v * v, axis=1, keepdims=True) + EPSILON)
 
 
-def forward_kernel(
-    size, order, lens, x, wq, wo, bias_qkv, gain_attn, gain_mlp, freq,
-    h2, x2, qs, kv, lse, obt,
-    cos_ref, sin_ref, bias_ref, kvar, vvar, ob, land, send, recv, out_sem,
-):
-    micro, rows, ctx = size
-    group = HQ // KVH
-    pairs = HQ // 2
-    width = HQ * HD
-    f, c = lax.axis_index("fsdp"), lax.axis_index("ctx")
-    others = [(f, (c + j) % ctx) for j in range(1, ctx)]
-    back = [(c - j + ctx) % ctx for j in range(1, ctx)]
-    enter(others)
-    links = Links(send, recv)
-    arrivals = []
-    for m in range(micro):
-        fill_tables(m, rows, c, freq, order, lens, cos_ref, sin_ref)
-    for m in range(micro):
-        stream = x[m].astype(F32)
-        h1 = (stream * inverse_norm(stream) * gain_attn[...]).astype(BF)
-        project = dot(h1, wq[...]) + bias_qkv[...]
-        cosine = cos_ref[m * rows : (m + 1) * rows, :]
-        sine = sin_ref[m * rows : (m + 1) * rows, :]
-        keys = project[:, width : width + LANES]
-        keys = keys * cosine + swap_halves(keys) * sine
-        land[m, c, :, :LANES] = keys.astype(BF)
-        land[m, c, :, LANES:] = project[:, width + LANES :].astype(BF)
-        arrivals.append([links.put(land.at[m, c], land.at[m, c], other) for other in others])
-        for p in range(pairs):
-            query = project[:, p * LANES : (p + 1) * LANES]
-            query = query * cosine + swap_halves(query) * sine
-            qs[m, p] = (query.astype(BF).astype(F32) * (1.0 / math.sqrt(HD))).astype(BF)
-    out_copies = []
-    for m in range(micro):
-        fill_bias(m, rows, c, order, lens, bias_ref)
-        for at, source in zip(arrivals[m], back):
-            links.arrive(at, land.at[m, source])
-        copy = pltpu.make_async_copy(land.at[m], kv.at[m], out_sem.at[m])
-        copy.start()
-        out_copies.append(copy)
-        both = land[m].reshape(ctx * rows, 2 * LANES).astype(F32)
-        fill_heads(both[:, :LANES], kvar)
-        fill_heads_turned(both[:, LANES:], vvar)
-
-        def pair(p, carry):
-            query = qs[m, p]
-            mixed = jnp.zeros((LANES, rows), F32)
-            for parity in range(2):
-                head = 2 * p + parity
-                g = head // group
-                scores = dot_nt(kvar[g, parity], query) + bias_ref[...]
-                top = jnp.max(scores, axis=0, keepdims=True)
-                probs = jnp.exp(scores - top)
-                total = jnp.sum(probs, axis=0, keepdims=True)
-                mixed = mixed + dot(vvar[g, parity], probs.astype(BF)) / total
-                lse[m, pl.ds(head, 1), :] = top + jnp.log(total)
-            at = pl.multiple_of(p * LANES, LANES)
-            obt[m, pl.ds(at, LANES), :] = mixed.astype(BF)
-            ob[:, pl.ds(at, LANES)] = mixed.T.astype(BF)
-            return carry
-
-        lax.fori_loop(0, pairs, pair, 0)
-        middle = x[m].astype(F32) + dot(ob[...], wo[...])
-        x2[m] = middle
-        h2[m] = (middle * inverse_norm(middle) * gain_mlp[...]).astype(BF)
-    links.drain()
-    for copy in out_copies:
-        copy.wait()
-
-
-def attention_forward(ctx, order, lens, x, wq, wo, bias_qkv, gain_attn, gain_mlp, freq):
-    micro, rows, width = x.shape
-    keys = rows * ctx
-    vmem = pl.BlockSpec(memory_space=pltpu.VMEM)
-    smem = pl.BlockSpec(memory_space=pltpu.SMEM)
-    copies = micro * (ctx - 1)
-    return pl.pallas_call(
-        functools.partial(forward_kernel, (micro, rows, ctx)),
-        out_shape=(
+class Forward:
+    def __init__(self, size, order, lens, x, freq, outs, scratch):
+        self.micro, self.rows, self.ctx = size
+        self.order, self.lens, self.x, self.freq = order, lens, x, freq
+        self.h2, self.x2, self.qs, self.kv, self.lse, self.obt = outs
+        (
+            self.cos_ref, self.sin_ref, self.bias_ref, self.kvar, self.vvar, self.ob, self.h1,
+            self.land, send, recv, self.out_sem,
+        ) = scratch
+        f, c = lax.axis_index("fsdp"), lax.axis_index("ctx")
+        self.c = c
+        self.others = [(f, (c + j) % self.ctx) for j in range(1, self.ctx)]
+        self.back = [(c - j + self.ctx) % self.ctx for j in range(1, self.ctx)]
+        self.links = Links(send, recv)
+        self.arrivals, self.out_copies = [], []
+
+    @staticmethod
+    def scratch(micro, rows, ctx, width):
+        keys = rows * ctx
+        copies = micro * (ctx - 1)
+        return [
+            pltpu.VMEM((micro * rows, LANES), F32),
+            pltpu.VMEM((micro * rows, LANES), F32),
+            pltpu.VMEM((keys, rows), F32),
+            pltpu.VMEM((KVH, 2, keys, LANES), BF),
+            pltpu.VMEM((KVH, 2, LANES, keys), BF),
+            pltpu.VMEM((micro, rows, HQ * HD), BF),
+            pltpu.VMEM((micro, rows, width), BF),
+            pltpu.VMEM((micro, ctx, rows, 2 * LANES), BF),
+            pltpu.SemaphoreType.DMA((copies,)),
+            pltpu.SemaphoreType.DMA((copies,)),
+            pltpu.SemaphoreType.DMA((micro,)),
+        ]
+
+    @staticmethod
+    def shapes(micro, rows, ctx, width):
+        return (
             jax.ShapeDtypeStruct((micro, rows, width), BF),
             jax.ShapeDtypeStruct((micro, rows, width), F32),
             jax.ShapeDtypeStruct((micro, HQ // 2, rows, LANES), BF),
             jax.ShapeDtypeStruct((micro, ctx, rows, 2 * LANES), BF),
             jax.ShapeDtypeStruct((micro, HQ, rows), F32),
             jax.ShapeDtypeStruct((micro, HQ * HD, rows), BF),
-        ),
+        )
+
+    @staticmethod
+    def specs():
+        vmem = pl.BlockSpec(memory_space=pltpu.VMEM)
+        return [vmem, vmem, vmem, pl.BlockSpec(memory_space=pl.ANY), vmem, vmem]
+
+    def tables(self):
+        for m in range(self.micro):
+            fill_tables(
+                m, self.rows, self.c, self.freq, self.order, self.lens, self.cos_ref, self.sin_ref
+            )
+
+    def norms(self, gain_attn):
+        for m in range(self.micro):
+            stream = self.x[m].astype(F32)
+            self.h1[m] = (stream * inverse_norm(stream) * gain_attn).astype(BF)
+
+    def project(self, m, wq, bias_qkv):
+        rows, width = self.rows, HQ * HD
+        project = dot(self.h1[m], wq) + bias_qkv
+        cosine = self.cos_ref[m * rows : (m + 1) * rows, :]
+        sine = self.sin_ref[m * rows : (m + 1) * rows, :]
+        keys = project[:, width : width + LANES]
+        keys = keys * cosine + swap_halves(keys) * sine
+        self.land[m, self.c, :, :LANES] = keys.astype(BF)
+        self.land[m, self.c, :, LANES:] = project[:, width + LANES :].astype(BF)
+        own = self.land.at[m, self.c]
+        self.arrivals.append([self.links.put(own, own, other) for other in self.others])
+        for p in range(HQ // 2):
+            query = project[:, p * LANES : (p + 1) * LANES]
+            query = query * cosine + swap_halves(query) * sine
+            self.qs[m, p] = (query.astype(BF).astype(F32) * (1.0 / math.sqrt(HD))).astype(BF)
+
+    def attend(self, m, tick):
+        rows, ctx, group, pairs = self.rows, self.ctx, HQ // KVH, HQ // 2
+        fill_bias(m, rows, self.c, self.order, self.lens, self.bias_ref)
+        for at, source in zip(self.arrivals[m], self.back):
+            self.links.arrive(at, self.land.at[m, source])
+        copy = pltpu.make_async_copy(self.land.at[m], self.kv.at[m], self.out_sem.at[m])
+        copy.start()
+        self.out_copies.append(copy)
+        both = self.land[m].reshape(ctx * rows, 2 * LANES).astype(F32)
+        fill_heads(both[:, :LANES], self.kvar)
+        fill_heads_turned(both[:, LANES:], self.vvar)
+
+        def pair(p, carry):
+            query = self.qs[m, p]
+            mixed = jnp.zeros((LANES, rows), F32)
+            for parity in range(2):
+                head = 2 * p + parity
+                g = head // group
+                scores = dot_nt(self.kvar[g, parity], query) + self.bias_ref[...]
+                top = jnp.max(scores, axis=0, keepdims=True)
+                probs = jnp.exp(scores - top)
+                total = jnp.sum(probs, axis=0, keepdims=True)
+                mixed = mixed + dot(self.vvar[g, parity], probs.astype(BF)) / total
+                self.lse[m, pl.ds(head, 1), :] = top + jnp.log(total)
+            at = pl.multiple_of(p * LANES, LANES)
+            self.obt[m, pl.ds(at, LANES), :] = mixed.astype(BF)
+            self.ob[m, :, pl.ds(at, LANES)] = mixed.T.astype(BF)
+            tick(p)
+            return carry
+
+        lax.fori_loop(0, pairs, pair, 0)
+
+    def close(self, m, wo, gain_mlp):
+        middle = self.x[m].astype(F32) + dot(self.ob[m], wo)
+        self.x2[m] = middle
+        self.h2[m] = (middle * inverse_norm(middle) * gain_mlp).astype(BF)
+
+    def drain(self):
+        self.links.drain()
+        for copy in self.out_copies:
+            copy.wait()
+
+
+def forward_kernel(size, order, lens, x, wq, wo, bias_qkv, gain_attn, gain_mlp, freq, *rest):
+    work = Forward(size, order, lens, x, freq, rest[:6], rest[6:])
+    enter(work.others)
+    work.tables()
+    work.norms(gain_attn[...])
+    for m in range(work.micro):
+        work.project(m, wq[...], bias_qkv[...])
+    for m in range(work.micro):
+        work.attend(m, lambda p: None)
+        work.close(m, wo[...], gain_mlp[...])
+    work.drain()
+
+
+def attention_forward(ctx, order, lens, x, wq, wo, bias_qkv, gain_attn, gain_mlp, freq):
+    micro, rows, width = x.shape
+    vmem = pl.BlockSpec(memory_space=pltpu.VMEM)
+    smem = pl.BlockSpec(memory_space=pltpu.SMEM)
+    return pl.pallas_call(
+        functools.partial(forward_kernel, (micro, rows, ctx)),
+        out_shape=Forward.shapes(micro, rows, ctx, width),
         in_specs=[smem, smem] + [vmem] * 7,
-        out_specs=[vmem, vmem, vmem, pl.BlockSpec(memory_space=pl.ANY), vmem, vmem],
-        scratch_shapes=[
-            pltpu.VMEM((micro * rows, LANES), F32),
-            pltpu.VMEM((micro * rows, LANES), F32),
-            pltpu.VMEM((keys, rows), F32),
-            pltpu.VMEM((KVH, 2, keys, LANES), BF),
-            pltpu.VMEM((KVH, 2, LANES, keys), BF),
-            pltpu.VMEM((rows, HQ * HD), BF),
-            pltpu.VMEM((micro, ctx, rows, 2 * LANES), BF),
-            pltpu.SemaphoreType.DMA((copies,)),
-            pltpu.SemaphoreType.DMA((copies,)),
-            pltpu.SemaphoreType.DMA((micro,)),
-        ],
+        out_specs=Forward.specs(),
+        scratch_shapes=Forward.scratch(micro, rows, ctx, width),
         compiler_params=pltpu.CompilerParams(
             collective_id=1, has_side_effects=True, vmem_limit_bytes=VMEM_LIMIT
         ),
@@ -366,11 +440,312 @@
     )(order, lens, x, wq, wo, bias_qkv, gain_attn, gain_mlp, freq)
 
 
+def front_kernel(
+    size, order, lens, x, wq, wo, sm, wgu_raw, wd, gy, freq,
+    h2, x2, qs, kv, lse, obt, wq_out, wo_out, gain_attn, gain_mlp, wgu_t, wd_t, gd_all,
+    wq_all, wo_all, sm_all, pieces, bias_qkv, zeros, wgu_in, wd_in, gy_in, staged_sems,
+    send, recv, ys, yr, zs, zr, here, *scratch
+):
+    n, micro, rows, ctx = size
+    replicas = n // TP
+    peers_n = replicas - 1
+    high = wgu_raw.shape[0]
+    staged = Staged([(wgu_raw, wgu_in), (wd, wd_in), (gy, gy_in)], staged_sems)
+    units, width = wd.shape
+    padded = wd_t.shape[1]
+    proj = wq.shape[1]
+    work = Forward((micro, rows, ctx), order, lens, x, freq, (h2, x2, qs, kv, lse, obt), scratch)
+    f, c = lax.axis_index("fsdp"), lax.axis_index("ctx")
+    t, r = f % TP, f // TP
+    even = c % 2 == 0
+    odd = c % 2 == 1
+    sib, par, cross = (flip1(f), c), (flip2(f), c), (flip2(flip1(f)), c)
+    t_sib, t_par, t_cross = flip1(t), flip2(t), flip2(flip1(t))
+    twin = (f, flip1(c))
+    peers = [((f + TP * j) % n, c) for j in range(1, replicas)]
+    back = [(f - TP * j + n) % n for j in range(1, replicas)]
+    rback = [(r - j + replicas) % replicas for j in range(1, replicas)]
+    enter([sib, par, cross] + peers + work.others)
+    links = Links(send, recv)
+    local = []
+
+    def keep(src, dst):
+        copy = pltpu.make_async_copy(src, dst, here.at[len(local)])
+        copy.start()
+        local.append(copy)
+        return copy
+
+    class Spread:
+        def __init__(self, own, every):
+            self.every = every
+            self.ys = [links.put(own, every.at[f], peer) for peer in peers]
+            self.mine = own
+            self.pending = [(links.put(own, every.at[f], sib), every.at[flip1(f)])]
+            self.own = keep(own, every.at[f])
+            self.later = []
+            self.slots = [
+                tuple(every.at[k] for k in (p, flip1(p), flip2(p), flip1(flip2(p)))) for p in back
+            ]
+            self.across = (every.at[flip2(f)], every.at[flip1(flip2(f))])
+
+        def start_x(self):
+            self.x = links.put(self.mine, self.every.at[f], par)
+
+        def on_y(self):
+            for at, (p, p_sib, p_par, p_cross) in zip(self.ys, self.slots):
+                links.arrive(at, p)
+                self.later.append((links.put(p, p, par), p_par, p_cross))
+                self.pending.append((links.put(p, p, sib), p_sib))
+
+        def on_x(self):
+            p, p_cross = self.across
+            links.arrive(self.x, p)
+            self.pending.append((links.put(p, p, sib), p_cross))
+
+        def on_late(self):
+            for at, p, p_cross in self.later:
+                links.arrive(at, p)
+                self.pending.append((links.put(p, p, sib), p_cross))
+
+        def done(self):
+            for at, p in self.pending:
+                links.arrive(at, p)
+            self.own.wait()
+
+    first = [Spread(wq, wq_all), Spread(sm, sm_all)]
+    for one in first:
+        one.start_x()
+    second = Spread(wo, wo_all)
+    pieces[...] = jnp.zeros_like(pieces)
+    zeros[...] = jnp.zeros_like(zeros)
+    staged.need(3)
+    for k in range(TP):
+        for q in range(2 * replicas):
+            at = (q * TP + k) * units
+            to = (q % replicas) * padded
+            pieces[k, q // replicas, :, to : to + units] = wgu_in[:, at : at + units]
+    gu_s = [links.put(pieces.at[t_sib, k], wgu_t.at[k, r, t], sib) for k in range(2)]
+    half = units // 2
+    last = wd_in.at[pl.ds(half, half)], wd_t.at[r, pl.ds(half, half)]
+    head = wd_in.at[pl.ds(0, half)], wd_t.at[r, pl.ds(0, half)]
+
+    def y_copy(at, j, src, dst):
+        at = at * peers_n + j
+        return pltpu.make_async_remote_copy(
+            src_ref=src, dst_ref=dst, send_sem=ys.at[at], recv_sem=yr.at[at],
+            device_id=peers[j], device_id_type=MESH,
+        )
+
+    def z_copy(at, j, src):
+        at = at * peers_n + j
+        return pltpu.make_async_remote_copy(
+            src_ref=src, dst_ref=src, send_sem=zs.at[at], recv_sem=zr.at[at],
+            device_id=twin, device_id_type=MESH,
+        )
+
+    def down_put(at, pair):
+        for j in range(peers_n):
+            y_copy(at, j, *pair).start()
+
+    kinds = ((t, t_sib), (t_par, t_cross))
+
+    def piece(parity, item, replica):
+        return wgu_t.at[item % 2, replica, kinds[parity][item // 2]]
+
+    def y_put(parity, item):
+        for j in range(peers_n):
+            mine = piece(parity, item, r)
+            src = pieces.at[t, item] if (parity, item // 2) == (0, 0) else mine
+            y_copy(item, j, src, mine).start()
+
+    def z_put(parity, item):
+        for j in range(peers_n):
+            got = piece(parity, item, rback[j])
+            y_copy(item, j, got, got).wait_recv()
+            z_copy(item, j, got).start()
+
+    @pl.when(even)
+    def _():
+        y_put(0, 0)
+        y_put(0, 1)
+
+    @pl.when(odd)
+    def _():
+        down_put(4, head)
+
+    for q in range(replicas):
+        keep(zeros, wd_t.at[q, pl.ds(units, padded - units)])
+    keep(wd_in, wd_t.at[r, pl.ds(0, units)])
+    for k in range(2):
+        keep(pieces.at[t, k], wgu_t.at[k, r, t])
+    keep(gy_in, gd_all.at[:, t])
+    gd_s = links.put(gy_in, gd_all.at[:, t], sib)
+    for one in first:
+        one.on_y()
+    gu_x = [links.put(pieces.at[t_par, k], wgu_t.at[k, r, t], par) for k in range(2)]
+    gu_c = [links.put(pieces.at[t_cross, k], wgu_t.at[k, r, t], cross) for k in range(2)]
+    second.start_x()
+    work.tables()
+    for one in first:
+        one.on_x()
+    for k in range(2):
+        links.arrive(gu_s[k], wgu_t.at[k, r, t_sib])
+
+    @pl.when(even)
+    def _():
+        y_put(0, 2)
+        y_put(0, 3)
+        down_put(4, head)
+        down_put(5, last)
+
+    for one in first:
+        one.on_late()
+    for one in first:
+        one.done()
+    keep(wq_all, wq_out)
+    share = proj // n
+    for k in range(n):
+        small = sm_all[k].astype(F32)
+        bias_qkv[:, k * share : k * share + min(share, LANES)] = small[0:1, : min(share, LANES)]
+        if share > LANES:
+            bias_qkv[:, k * share + LANES : (k + 1) * share] = small[1:2, : share - LANES]
+        gain_attn[:, k * high : (k + 1) * high] = small[2:3, :high]
+        gain_mlp[:, k * high : (k + 1) * high] = small[3:4, :high]
+    work.norms(gain_attn[...])
+    for m in range(micro):
+        work.project(m, wq_all[...].reshape(width, proj), bias_qkv[...])
+    second.on_y()
+    gd_x = [links.put(gy_in.at[m], gd_all.at[m, t], par) for m in range(micro)]
+    gd_par = [gd_all.at[m, t_par] for m in range(micro)]
+    gd_c = []
+
+    def x_piece(k):
+        links.arrive(gu_x[k], wgu_t.at[k, r, t_par])
+        pl.when(odd)(lambda: y_put(1, k))
+
+    def c_piece(k):
+        links.arrive(gu_c[k], wgu_t.at[k, r, t_cross])
+
+        @pl.when(odd)
+        def _():
+            y_put(1, 2 + k)
+            if k == 1:
+                down_put(5, last)
+
+    def on_gd():
+        links.arrive(gd_x[0], gd_par[0])
+        gd_c.append(links.put(gd_par[0], gd_par[0], sib))
+
+    x_piece(0)
+    x_piece(1)
+    steps = {
+        (0, 0): [lambda: pl.when(even)(lambda: z_put(0, 0))],
+        (0, 1): [lambda: pl.when(even)(lambda: z_put(0, 1)), lambda: c_piece(0)],
+        (0, 2): [lambda: pl.when(even)(lambda: z_put(0, 2))],
+        (0, 3): [lambda: c_piece(1), lambda: pl.when(odd)(lambda: z_put(1, 0))],
+        (0, 4): [lambda: pl.when(even)(lambda: z_put(0, 3))],
+        (0, 6): [lambda: pl.when(odd)(lambda: z_put(1, 1))],
+        (1, 1): [lambda: pl.when(odd)(lambda: z_put(1, 2)), second.on_x],
+        (1, 3): [lambda: pl.when(odd)(lambda: z_put(1, 3)), second.on_late],
+        (1, 6): [on_gd],
+    }
+    for m in range(micro):
+
+        def tick(p, m=m):
+            for (at_m, at_p), todo in steps.items():
+                if at_m == m:
+
+                    @pl.when(p == at_p)
+                    def _(todo=todo):
+                        for one in todo:
+                            one()
+
+        work.attend(m, tick)
+    second.done()
+    keep(wo_all, wo_out)
+    for m in range(micro):
+        work.close(m, wo_all[...].reshape(width, width), gain_mlp[...])
+    for m in range(1, micro):
+        links.arrive(gd_x[m], gd_par[m])
+        gd_c.append(links.put(gd_par[m], gd_par[m], sib))
+    links.arrive(gd_s, gd_all.at[:, t_sib])
+    for m in range(micro):
+        links.arrive(gd_c[m], gd_all.at[m, t_cross])
+    for parity in range(2):
+
+        @pl.when(even if parity == 0 else odd)
+        def _(parity=parity):
+            for j in range(peers_n):
+                for item in range(4):
+                    z_copy(item, j, piece(1 - parity, item, rback[j])).wait_recv()
+                    mine = piece(parity, item, r)
+                    z_copy(item, j, mine).wait_send()
+                    y_copy(item, j, mine, mine).wait_send()
+
+    for j in range(peers_n):
+        for at, pair in ((4, head), (5, last)):
+            y_copy(at, j, *pair).wait_send()
+            first_row = 0 if at == 4 else half
+            y_copy(at, j, pair[0], wd_t.at[rback[j], pl.ds(first_row, half)]).wait_recv()
+    for copy in local:
+        if copy is not second.own and all(copy is not one.own for one in first):
+            copy.wait()
+    work.drain()
+    links.drain()
+
+
+def gather_and_attend(n, ctx, order, lens, x, wq, wo, sm, wgu, wd, gy, freq, padded):
+    micro, rows, width = x.shape
+    replicas = n // TP
+    peers = replicas - 1
+    high, proj = wq.shape
+    quarter = replicas * padded
+    vmem = pl.BlockSpec(memory_space=pltpu.VMEM)
+    smem = pl.BlockSpec(memory_space=pltpu.SMEM)
+    anywhere = pl.BlockSpec(memory_space=pl.ANY)
+    sems = pltpu.SemaphoreType.DMA
+    copies = 3 * (4 * peers + 3) + 6 + 1 + 2 * micro
+    gain = jax.ShapeDtypeStruct((1, width), F32)
+    return pl.pallas_call(
+        functools.partial(front_kernel, (n, micro, rows, ctx)),
+        out_shape=Forward.shapes(micro, rows, ctx, width) + (
+            jax.ShapeDtypeStruct((n, high, proj), BF),
+            jax.ShapeDtypeStruct((n, high, width), BF),
+            gain,
+            gain,
+            jax.ShapeDtypeStruct((2, replicas, TP, high, quarter), BF),
+            jax.ShapeDtypeStruct((replicas, padded, width), BF),
+            jax.ShapeDtypeStruct((micro, TP, rows, width), BF),
+        ),
+        in_specs=[smem, smem, vmem] + [anywhere] * 6 + [vmem],
+        out_specs=Forward.specs() + [anywhere, anywhere, vmem, vmem] + [anywhere] * 3,
+        scratch_shapes=[
+            pltpu.VMEM((n, high, proj), BF),
+            pltpu.VMEM((n, high, width), BF),
+            pltpu.VMEM((n,) + sm.shape, BF),
+            pltpu.VMEM((TP, 2, high, quarter), BF),
+            pltpu.VMEM((1, proj), F32),
+            pltpu.VMEM((padded - wd.shape[0], width), BF),
+            pltpu.VMEM(wgu.shape, BF),
+            pltpu.VMEM(wd.shape, BF),
+            pltpu.VMEM(gy.shape, BF),
+            sems((3,)),
+            sems((copies,)), sems((copies,)),
+            sems((6 * peers,)), sems((6 * peers,)), sems((4 * peers,)), sems((4 * peers,)),
+            sems((9 + replicas,)),
+        ] + Forward.scratch(micro, rows, ctx, width),
+        compiler_params=pltpu.CompilerParams(
+            collective_id=5, has_side_effects=True, vmem_limit_bytes=VMEM_LIMIT
+        ),
+        name="gather_and_attend",
+    )(order, lens, x, wq, wo, sm, wgu, wd, gy, freq)
+
+
 def mlp_kernel(
-    size, h2, gd, wgu, wd,
-    out, gh2, grads,
-    hbuf, turned_h, turned_g, acc_out, acc_gh, dgate, dup, ddown,
-    sib_out, sib_in, par_out, par_in, keep_sum, stage, send, recv, out_sem,
+    size, h2, gd_hbm, wgu_hbm, wd_hbm,
+    out, out_par, gh2, grads,
+    gd, wgu, wd, hbuf, turned_h, turned_g, acc_out, acc_gh, dgate, dup, ddown,
+    sib_out, sib_in, par_out, par_in, keep_sum, stage, send, recv, out_sem, staged_sems,
 ):
     micro, rows, width, replicas, padded = size
     quarter = replicas * padded
@@ -379,27 +754,35 @@
     t = f % TP
     core = t % 2
     mine, theirs = t - core, flip2(t) - core
+    t_sib, t_par, t_cross = flip1(t), flip2(t), flip2(flip1(t))
     sib, par = (flip1(f), c), (flip2(f), c)
+    staged = Staged(
+        [(h2.at[m], hbuf.at[m, t]) for m in range(micro)]
+        + [(gd_hbm.at[0], gd.at[0]), (wgu_hbm, wgu), (wd_hbm, wd)]
+        + [(gd_hbm.at[m], gd.at[m]) for m in range(1, micro)],
+        staged_sems,
+    )
     enter([sib, par])
     links = Links(send, recv)
-    from_sib, from_par = [], []
+    from_sib, from_par, from_cross = [], [], [None] * micro
     for m in range(micro):
-        hbuf[m, t] = h2[m]
-        from_sib.append(links.put(hbuf.at[m, t], hbuf.at[m, t], sib))
-        from_par.append(links.put(hbuf.at[m, t], hbuf.at[m, t], par))
-    from_cross = [None] * micro
+        from_par.append(links.put(h2.at[m], hbuf.at[m, t], par))
+        from_sib.append(links.put(h2.at[m], hbuf.at[m, t], sib))
+
+    def grad_of(m, side):
+        return gd[m, pl.ds(side, 2)].reshape(both, width)
 
     def forward_on(m):
-        links.arrive(from_par[m], hbuf.at[m, flip2(t)])
-        from_cross[m] = links.put(hbuf.at[m, flip2(t)], hbuf.at[m, flip2(t)], sib)
+        buf = hbuf.at[m, t_par]
+        links.arrive(from_par[m], buf)
+        from_cross[m] = links.put(buf, buf, sib)
 
     def chunk(m, side, first, j):
         at = pl.multiple_of(j * CHUNK, CHUNK)
-        up_at = pl.multiple_of(quarter + j * CHUNK, CHUNK)
         hidden_in = hbuf[m, pl.ds(side, 2)].reshape(both, width)
-        grad_in = gd[m, pl.ds(side, 2)].reshape(both, width)
-        w_gate = wgu[:, pl.ds(at, CHUNK)]
-        w_up = wgu[:, pl.ds(up_at, CHUNK)]
+        grad_in = grad_of(m, side)
+        w_gate = wgu[0, :, pl.ds(at, CHUNK)]
+        w_up = wgu[1, :, pl.ds(at, CHUNK)]
         w_down = wd[pl.ds(at, CHUNK), :]
         gate = dot(hidden_in, w_gate)
         up = dot(hidden_in, w_up)
@@ -420,9 +803,9 @@
             dup[:, pl.ds(at, CHUNK)] += dot(turned_h[...], gup)
             ddown[:, pl.ds(at, CHUNK)] += dot(turned_g[...], mb)
 
-    def compute(m, side, first, middle):
+    def compute(m, side, first, middle, late):
         turned_h[...] = hbuf[m, pl.ds(side, 2)].reshape(both, width).T
-        turned_g[...] = gd[m, pl.ds(side, 2)].reshape(both, width).T
+        turned_g[...] = grad_of(m, side).T
         acc_out[...] = jnp.zeros_like(acc_out)
         acc_gh[...] = jnp.zeros_like(acc_gh)
         chunks = quarter // CHUNK
@@ -431,9 +814,11 @@
             chunk(m, side, first, j)
             return carry
 
-        lax.fori_loop(0, 1, body, 0)
+        lax.fori_loop(0, 2, body, 0)
         middle()
-        lax.fori_loop(1, chunks, body, 0)
+        lax.fori_loop(2, chunks - 1, body, 0)
+        late()
+        lax.fori_loop(chunks - 1, chunks, body, 0)
 
     def share(step):
         here = pl.multiple_of(core * rows, rows)
@@ -446,22 +831,19 @@
         return ats
 
     def pass_on(step, m, ats):
-        got = []
-        for k, at in enumerate(ats):
+        for k, (at, ref) in enumerate(zip(ats, (par_out, out_par))):
             links.arrive(at, sib_in.at[step, k])
-            par_out[m, k] = (keep_sum[k] + sib_in[step, k].astype(F32)).astype(BF)
-            got.append(links.put(par_out.at[m, k], par_in.at[m, k], par))
-        return got
+            ref[m] = (keep_sum[k] + sib_in[step, k].astype(F32)).astype(BF)
+        return links.put(par_out.at[m], par_in.at[m], par)
 
     def stay(step, m, ats):
-        for k, at in enumerate(ats):
+        for k, (at, ref) in enumerate(zip(ats, (gh2, out))):
             links.arrive(at, sib_in.at[step, k])
-            (gh2, out)[k][m] = keep_sum[k] + sib_in[step, k].astype(F32)
-
-    def finish(m, ats):
-        for k, (at, ref) in enumerate(zip(ats, (gh2, out))):
-            links.arrive(at, par_in.at[m, k])
-            ref[m] = ref[m] + par_in[m, k].astype(F32)
+            ref[m] = keep_sum[k] + sib_in[step, k].astype(F32)
+
+    def finish(m, at):
+        links.arrive(at, par_in.at[m])
+        gh2[m] = gh2[m] + par_in[m].astype(F32)
 
     plan = [(0, True)] + [(m, False) for m in range(micro)] + [(m, True) for m in range(1, micro)]
     waiting = None
@@ -469,13 +851,16 @@
     ready_own = [False] * micro
     for step, (m, own) in enumerate(plan):
         if own:
-            links.arrive(from_sib[m], hbuf.at[m, flip1(t)])
+            links.arrive(from_sib[m], hbuf.at[m, t_sib])
         else:
-            links.arrive(from_cross[m], hbuf.at[m, flip2(flip1(t))])
-
-        def middle(step=step):
+            links.arrive(from_cross[m], hbuf.at[m, t_cross])
+        staged.need((micro + 3) if m == 0 else len(staged.copies))
+
+        def late(step=step):
             if step < micro:
                 forward_on(step)
+
+        def middle(step=step):
             if step > 0:
                 last_m, last_own = plan[step - 1]
                 if last_own:
@@ -483,21 +868,24 @@
                 else:
                     sums[last_m] = pass_on(step - 1, last_m, waiting)
 
-        compute(m, mine if own else theirs, step == 0, middle)
+        compute(m, mine if own else theirs, step == 0, middle, late)
         waiting = share(step)
     high = width // (replicas * TP)
     copies = []
     for replica in range(replicas):
         for k in range(PIECES):
-            slot = len(copies) % 2
-            if len(copies) >= 2:
-                copies[-2].wait()
-            if k < 2 * TP:
-                at = (replica * TP + k // 2) * high
-                stage[slot] = (dgate, dup)[k % 2][at : at + high, :].astype(BF)
+            slot = len(copies) % SLOTS
+            if len(copies) >= SLOTS:
+                copies[-SLOTS].wait()
+            if k < 4 * TP:
+                at = (replica * TP + k // 4) * high
+                lane = (k % 2) * (quarter // 2)
+                stage[slot] = (dgate, dup)[(k // 2) % 2][
+                    at : at + high, lane : lane + quarter // 2
+                ].astype(BF)
             else:
-                for q in range(replicas):
-                    at = (k - 2 * TP) * replicas + q
+                for q in range(replicas // 2):
+                    at = (k - 4 * TP) * (replicas // 2) + q
                     stage[slot, :, q * padded : (q + 1) * padded] = ddown[
                         at * high : (at + 1) * high, replica * padded : (replica + 1) * padded
                     ].astype(BF)
@@ -511,7 +899,7 @@
         sums[last_m] = pass_on(len(plan) - 1, last_m, waiting)
     for m in range(micro):
         finish(m, sums[m])
-    for copy in copies[-2:]:
+    for copy in copies[-SLOTS:]:
         copy.wait()
     links.drain()
 
@@ -523,17 +911,22 @@
     quarter = replicas * padded
     vmem = pl.BlockSpec(memory_space=pltpu.VMEM)
     steps = 2 * micro
-    copies = micro * 3 + steps * 2 + micro * 2
+    copies = micro * 3 + steps * 2 + micro
+    whole = jax.ShapeDtypeStruct((micro, rows, width), F32)
     return pl.pallas_call(
         functools.partial(mlp_kernel, (micro, rows, width, replicas, padded)),
         out_shape=(
-            jax.ShapeDtypeStruct((micro, rows, width), F32),
-            jax.ShapeDtypeStruct((micro, rows, width), F32),
-            jax.ShapeDtypeStruct((replicas, PIECES, width // n, quarter), BF),
+            whole,
+            jax.ShapeDtypeStruct((micro, rows, width), BF),
+            whole,
+            jax.ShapeDtypeStruct((replicas, PIECES, width // n, quarter // 2), BF),
         ),
-        in_specs=[vmem] * 4,
-        out_specs=[vmem, vmem, pl.BlockSpec(memory_space=pl.ANY)],
+        in_specs=[pl.BlockSpec(memory_space=pl.ANY)] * 4,
+        out_specs=[vmem, vmem, vmem, pl.BlockSpec(memory_space=pl.ANY)],
         scratch_shapes=[
+            pltpu.VMEM(gd.shape, BF),
+            pltpu.VMEM(wgu.shape, BF),
+            pltpu.VMEM(wd.shape, BF),
             pltpu.VMEM((micro, TP, rows, width), BF),
             pltpu.VMEM((width, 2 * rows), BF),
             pltpu.VMEM((width, 2 * rows), BF),
@@ -544,13 +937,14 @@
             pltpu.VMEM((width, quarter), F32),
             pltpu.VMEM((steps, 2, rows, width), BF),
             pltpu.VMEM((steps, 2, rows, width), BF),
-            pltpu.VMEM((micro, 2, rows, width), BF),
-            pltpu.VMEM((micro, 2, rows, width), BF),
+            pltpu.VMEM((micro, rows, width), BF),
+            pltpu.VMEM((micro, rows, width), BF),
             pltpu.VMEM((2, rows, width), F32),
-            pltpu.VMEM((2, width // n, quarter), BF),
+            pltpu.VMEM((SLOTS, width // n, quarter // 2), BF),
             pltpu.SemaphoreType.DMA((copies,)),
             pltpu.SemaphoreType.DMA((copies,)),
-            pltpu.SemaphoreType.DMA((2,)),
+            pltpu.SemaphoreType.DMA((SLOTS,)),
+            pltpu.SemaphoreType.DMA((2 * micro + 2,)),
         ],
         compiler_params=pltpu.CompilerParams(
             collective_id=2, has_side_effects=True, vmem_limit_bytes=VMEM_LIMIT
@@ -560,15 +954,7 @@
 
 
 def add_into(dst, a, b):
-    width = dst.shape[-1]
-    step = 256 if width % 256 == 0 else LANES
-
-    def body(k, carry):
-        at = pl.ds(pl.multiple_of(k * step, step), step)
-        dst[:, at] = (a[:, at].astype(F32) + b[:, at].astype(F32)).astype(BF)
-        return carry
-
-    lax.fori_loop(0, width // step, body, 0)
+    dst[...] = (a[...].astype(F32) + b[...].astype(F32)).astype(BF)
 
 
 class Sums:
@@ -602,7 +988,7 @@
             pltpu.VMEM((ALL_PIECES, high, wide), BF),
             pltpu.VMEM((ALL_PIECES, high, wide), BF),
             pltpu.VMEM((RING, high, wide), BF),
-            pltpu.VMEM((2 * TP, high, wide), BF),
+            pltpu.VMEM((4 * TP, high, wide), BF),
             pltpu.VMEM((replicas, 2, high, width), BF),
             pltpu.VMEM((replicas, high, width), BF),
             pltpu.VMEM((peers, high, width), BF),
@@ -613,7 +999,7 @@
             pltpu.VMEM((2 + peers, VEC, LANES), F32),
             sems((peers * PIECES,)), sems((peers * PIECES,)),
             sems((ALL_PIECES,)), sems((ALL_PIECES,)), sems((ALL_PIECES,)), sems((ALL_PIECES,)),
-            sems((2 * TP,)), sems((2 * TP,)),
+            sems((4 * TP,)), sems((4 * TP,)),
             sems((6 + 3 * peers,)), sems((6 + 3 * peers,)), sems((1,)), sems((ALL_PIECES,)),
         ]
 
@@ -636,12 +1022,15 @@
             self.grads.at[self.r], self.total.at[pl.ds(0, PIECES)], self.own_sem.at[0]
         )
 
-    def start(self, ahead):
+    def start(self):
         self.own_copy().start()
-        for k in range(ahead):
+
+        def body(k, carry):
             for j in range(self.replicas - 1):
                 self.peer_copy(j, k).start()
-        self.ahead = ahead
+            return carry
+
+        lax.fori_loop(0, PIECES, body, 0)
 
     def pre_copy(self, k, src):
         return pltpu.make_async_remote_copy(
@@ -655,23 +1044,15 @@
             recv_sem=self.sr.at[k], device_id=self.left, device_id_type=MESH,
         )
 
-    def fin_copy(self, k, slot):
-        return pltpu.make_async_remote_copy(
-            src_ref=self.suf.at[k], dst_ref=self.land.at[slot], send_sem=self.fs.at[k],
-            recv_sem=self.fr.at[slot], device_id=(self.f - self.t + k // 2, self.c),
-            device_id_type=MESH,
-        )
-
     def out_copy(self, k, src):
         return pltpu.make_async_copy(src.at[k], self.fin.at[k], self.out_sem.at[k])
 
+    def step(self, time, carry):
+        self.tick(time)
+        return carry
+
     def tick(self, time):
         c, ctx, total = self.c, self.ctx, self.total
-
-        @pl.when(time + self.ahead < PIECES)
-        def _():
-            for j in range(self.replicas - 1):
-                self.peer_copy(j, time + self.ahead).start()
 
         @pl.when(time < PIECES)
         def _():
@@ -679,7 +1060,7 @@
                 self.peer_copy(j, time).wait_recv()
                 add_into(total.at[time], total.at[time], self.peer_in.at[j, time])
 
-        k = time - c
+        k = time - HOP * c
 
         @pl.when((k >= 0) & (k < ALL_PIECES))
         def _():
@@ -696,7 +1077,7 @@
             def _():
                 self.pre_copy(k, total).start()
 
-        k2 = time - (ctx - 1 - c)
+        k2 = time - HOP * (ctx - 1 - c)
 
         @pl.when((k2 >= 0) & (k2 < ALL_PIECES))
         def _():
@@ -717,7 +1098,7 @@
             def _():
                 self.suf_copy(k2, total.at[k2]).start()
 
-        k3 = time - jnp.maximum(c, ctx - 1 - c)
+        k3 = time - HOP * jnp.maximum(c, ctx - 1 - c)
 
         @pl.when((k3 >= 0) & (k3 < ALL_PIECES))
         def _():
@@ -729,7 +1110,7 @@
             def _():
                 add_into(self.suf.at[k3], self.suf.at[k3], self.pre.at[k3])
 
-            @pl.when((k3 < 2 * TP) & (k3 // 2 != self.t))
+            @pl.when((k3 < 4 * TP) & (k3 // 4 != self.t))
             def _():
                 @pl.when(c == ctx - 1)
                 def _():
@@ -739,7 +1120,7 @@
                 def _():
                     self.fin_copy_from(k3, self.suf).start()
 
-            @pl.when((k3 >= 2 * TP) | (k3 // 2 == self.t))
+            @pl.when((k3 >= 4 * TP) | (k3 // 4 == self.t))
             def _():
                 @pl.when(c == ctx - 1)
                 def _():
@@ -751,24 +1132,24 @@
 
     def fin_copy_from(self, k, src):
         return pltpu.make_async_remote_copy(
-            src_ref=src.at[k], dst_ref=self.land.at[2 * self.t + k % 2], send_sem=self.fs.at[k],
-            recv_sem=self.fr.at[2 * self.t + k % 2],
-            device_id=(self.f - self.t + k // 2, self.c), device_id_type=MESH,
+            src_ref=src.at[k], dst_ref=self.land.at[4 * self.t + k % 4], send_sem=self.fs.at[k],
+            recv_sem=self.fr.at[4 * self.t + k % 4],
+            device_id=(self.f - self.t + k // 4, self.c), device_id_type=MESH,
         )
 
     @property
     def ticks(self):
-        return ALL_PIECES + self.ctx - 1
+        return ALL_PIECES + HOP * (self.ctx - 1)
 
     def close(self):
         c, ctx = self.c, self.ctx
 
         def arrive(k, carry):
-            @pl.when(k // 2 != self.t)
+            @pl.when(k // 4 != self.t)
             def _():
                 pltpu.make_async_remote_copy(
                     src_ref=self.land.at[k], dst_ref=self.land.at[k], send_sem=self.fs.at[k],
-                    recv_sem=self.fr.at[k], device_id=(self.f - self.t + k // 2, c),
+                    recv_sem=self.fr.at[k], device_id=(self.f - self.t + k // 4, c),
                     device_id_type=MESH,
                 ).wait_recv()
                 self.out_copy(k, self.land).start()
@@ -776,7 +1157,7 @@
 
             return carry
 
-        lax.fori_loop(0, 2 * TP, arrive, 0)
+        lax.fori_loop(0, 4 * TP, arrive, 0)
 
         def settle(k, carry):
             @pl.when(c < ctx - 1)
@@ -801,11 +1182,11 @@
         self.links.drain()
 
 
-    def fold(self, own, got_core, got_par, got_ring, place, extra=None):
+    def fold(self, own, got_core, got_par, got_ring, first, extra=False):
         replicas = self.replicas
         at = self.links.put(own.at[:, :, 1 - self.core], got_core, self.sib)
         at_vec = None
-        if extra is not None:
+        if extra:
             at_vec = self.links.put(self.vec.at[0], self.vec_in.at[0], self.sib)
         yield
         self.links.arrive(at, got_core)
@@ -816,7 +1197,7 @@
                     own.at[replica, s, self.core],
                 )
         at = self.links.put(got_core.at[:, 1 - self.side], got_par, self.par)
-        if extra is not None:
+        if extra:
             self.links.arrive(at_vec, self.vec_in.at[0])
             self.vec[1] = self.vec[0] + self.vec_in[0]
             at_vec = self.links.put(self.vec.at[1], self.vec_in.at[1], self.par)
@@ -825,41 +1206,49 @@
         for replica in range(replicas):
             add_into(got_par.at[replica], got_par.at[replica], got_core.at[replica, self.side])
         ats, vec_ats = [], []
-        if extra is not None:
+        if extra:
             self.links.arrive(at_vec, self.vec_in.at[1])
             self.vec[2] = self.vec[1] + self.vec_in[1]
         for j, peer in enumerate(self.peers):
             ats.append(
                 self.links.put(got_par.at[(self.r + j + 1) % replicas], got_ring.at[j], peer)
             )
-            if extra is not None:
+            if extra:
                 vec_ats.append(self.links.put(self.vec.at[2], self.vec_in.at[2 + j], peer))
         yield
-        width = got_ring.shape[-1]
+        width, wide = got_ring.shape[-1], self.total.shape[-1]
+        mine = got_par.at[self.r]
         for j, at in enumerate(ats):
             self.links.arrive(at, got_ring.at[j])
-            source = got_par.at[self.r] if j == 0 else place
-            add_into(place, source, got_ring.at[j])
-        if extra is not None:
+            add_into(mine, mine, got_ring.at[j])
+        self.total[first] = mine[:, :wide]
+        self.total[first + 1, :, : width - wide] = mine[:, wide:]
+        if extra:
             vec = self.vec[2]
             for j, at in enumerate(vec_ats):
                 self.links.arrive(at, self.vec_in.at[2 + j])
                 vec = vec + self.vec_in[2 + j]
-            extra[...] = vec.astype(BF)
+            self.total[first + 1, :VEC, width - wide : width - wide + LANES] = vec.astype(BF)
         yield
 
 
 def backward_kernel(
-    size, merged, order, lens, gh2, x2, gy, x, wq, wo, gain_attn, gain_mlp, freq, qs, kv, lse, obt,
-    grads, dx, *rest
+    size, merged, order, lens, gain_attn, gain_mlp, freq, *rest
 ):
     n, micro, rows, ctx = size
+    hbm, rest = rest[:11], rest[11:]
+    out_par, grads, dx, outputs = rest[:4]
+    rest = rest[4:]
     outs = 1 if merged else 3
     fin, rest = rest[:outs], rest[outs:]
     (
-        cos_ref, sin_ref, bias_ref, kvar, kvar_turned, vvar, go_ref, gp, h1t, gk, gv, part, land,
+        x2, gh2, gy, wo, obt, kv, qs, lse, x, wq, out, staged_sems,
+        out_in, out_send, out_recv, cos_ref, sin_ref, bias_ref, kvar, kvar_turned, vvar, go_ref, gp, h1t, gk, gv, part, land,
         att_o, att_q, vec_wide, send, recv,
-    ), rest = rest[:18], rest[18:]
+    ), rest = rest[:33], rest[33:]
+    staged = Staged(
+        list(zip(hbm, (x2, gh2, gy, wo, obt, kv, qs, lse, x, wq, out))), staged_sems
+    )
     group = HQ // KVH
     pairs = HQ // 2
     width = HQ * HD
@@ -873,13 +1262,22 @@
     if merged:
         sums = Sums(n, ctx, grads, fin[0], rest)
         enter(others + sums.around())
-        sums.start(2)
+        sums.start()
     else:
-        enter(others)
+        enter(others + [(flip2(f), c)])
+    out_links = Links(out_send, out_recv)
+    out_at = out_links.put(out_par, out_in, (flip2(f), c))
     links = Links(send, recv)
     arrivals = []
+    if merged:
+        for k in range(PIECES, ALL_PIECES):
+            sums.total[k] = jnp.zeros(sums.total.shape[1:], BF)
+        sums.own_copy().wait()
     for m in range(micro):
         fill_tables(m, rows, c, freq, order, lens, cos_ref, sin_ref)
+        if merged:
+            lax.fori_loop(EARLY * m // micro, EARLY * (m + 1) // micro, sums.step, 0)
+        staged.need(4)
         stream = x2[m]
         inverse = inverse_norm(stream)
         normed = stream * inverse
@@ -895,19 +1293,14 @@
         spread = dot_nt(grad.astype(BF), wo[...]).astype(BF)
         for p in range(pairs):
             go_ref[m, p] = spread[:, p * LANES : (p + 1) * LANES]
+    staged.need(len(staged.copies))
     for k in range(n):
         term = dot(obt[0, k * high : (k + 1) * high, :], dx[0].astype(BF))
         for m in range(1, micro):
             term = term + dot(obt[m, k * high : (k + 1) * high, :], dx[m].astype(BF))
         att_o[k // TP, (k // 2) % 2, k % 2] = term.astype(BF)
     if merged:
-        sums.total[PIECES] = jnp.zeros(sums.total.shape[1:], BF)
-        sums.total[PIECES + 1] = jnp.zeros(sums.total.shape[1:], BF)
-        sums.own_copy().wait()
-        fold_o = sums.fold(
-            att_o, sums.core_o, sums.par_o, sums.ring_o,
-            sums.total.at[PIECES, :, pl.ds(0, width)],
-        )
+        fold_o = sums.fold(att_o, sums.core_o, sums.par_o, sums.ring_o, PIECES)
         next(fold_o)
     for m in range(micro):
         if merged and m > 0:
@@ -943,10 +1336,9 @@
             gp[m * rows : (m + 1) * rows, pl.ds(at, LANES)] = turned.astype(BF)
             if merged:
                 step = m * pairs + p
-
-                @pl.when(step % 3 != 2)
-                def _():
-                    sums.tick(step - step // 3)
+                lax.fori_loop(
+                    EARLY + RATE * step // 2, EARLY + RATE * (step + 1) // 2, sums.step, 0
+                )
 
             return carry
 
@@ -996,45 +1388,38 @@
         dx[m] = dx[m] + inverse * (
             grad - normed * jnp.mean(grad * normed, axis=1, keepdims=True)
         )
+    out_links.arrive(out_at, out_in)
+    for m in range(micro):
+        outputs[m] = (x2[m] + out[m] + out_in[m].astype(F32)).astype(BF)
+    out_links.drain()
     vec = sums.vec.at[0] if merged else fin[2]
     vec[...] = jnp.zeros((VEC, LANES), F32)
     for k in range(vec_wide.shape[1] // LANES):
         vec[k : k + 1, :] = vec_wide[:, k * LANES : (k + 1) * LANES]
     if merged:
         next(fold_o)
-        done = micro * pairs - (micro * pairs) // 3
-        fold_sums(sums, att_q, done, width, proj)
+        fold_sums(sums, att_q, EARLY + RATE * micro * pairs // 2)
     else:
         fin[0][...] = att_o[...]
         fin[1][...] = att_q[...]
     links.drain()
 
 
-def fold_sums(sums, att_q, done, width, proj):
-    fold_q = sums.fold(
-        att_q, sums.core_q, sums.par_q, sums.ring_q,
-        sums.total.at[PIECES + 1, :, pl.ds(0, proj)],
-        sums.total.at[PIECES + 1, pl.ds(0, VEC), pl.ds(proj, LANES)],
-    )
-    between = max(0, min(2, PIECES - done))
-
-    def body(k, carry):
-        sums.tick(k)
-        return carry
-
+def fold_sums(sums, att_q, done):
+    fold_q = sums.fold(att_q, sums.core_q, sums.par_q, sums.ring_q, PIECES + 2, True)
+    ready = max(0, PIECES + 2 - done)
     next(fold_q)
-    for _ in range(between):
-        sums.tick(jnp.int32(done))
-        done += 1
+    for k in range(3):
+        upto = done + ready * (k + 1) // 3
+        lax.fori_loop(done + ready * k // 3, upto, sums.step, 0)
         next(fold_q)
-    for _ in range(3 - between):
-        next(fold_q)
-    lax.fori_loop(done, sums.ticks, body, 0)
+    lax.fori_loop(done + ready, sums.ticks, sums.step, 0)
     sums.close()
 
 
 def attention_backward(
-    n, ctx, order, lens, gh2, x2, gy, x, wq, wo, gain_attn, gain_mlp, freq, qs, kv, lse, obt, grads
+    n, ctx, order, lens, gh2, x2, gy, x, wq, wo, gain_attn, gain_mlp, freq, qs, kv, lse, obt,
+    out, out_par, grads,
 ):
     micro, rows, width = x.shape
     keys = rows * ctx
@@ -1046,7 +1431,10 @@
     smem = pl.BlockSpec(memory_space=pltpu.SMEM)
     anywhere = pl.BlockSpec(memory_space=pl.ANY)
     copies = micro * (ctx - 1)
-    out_shape = [jax.ShapeDtypeStruct((micro, rows, width), F32)]
+    out_shape = [
+        jax.ShapeDtypeStruct((micro, rows, width), F32),
+        jax.ShapeDtypeStruct((micro, rows, width), BF),
+    ]
     shape_o = (replicas, 2, 2, high, width)
     shape_q = (replicas, 2, 2, high, proj)
     if merged:
@@ -1057,12 +1445,18 @@
             jax.ShapeDtypeStruct(shape_q, BF),
             jax.ShapeDtypeStruct((VEC, LANES), F32),
         ]
+    operands = (x2, gh2, gy, wo, obt, kv, qs, lse, x, wq, out)
     result = pl.pallas_call(
         functools.partial(backward_kernel, (n, micro, rows, ctx), merged),
         out_shape=out_shape,
-        in_specs=[smem, smem] + [vmem] * 13 + [anywhere],
-        out_specs=[vmem] + ([anywhere] if merged else [vmem] * 3),
-        scratch_shapes=[
+        in_specs=[smem, smem] + [vmem] * 3 + [anywhere] * 13,
+        out_specs=[vmem] * 2 + ([anywhere] if merged else [vmem] * 3),
+        scratch_shapes=[pltpu.VMEM(one.shape, one.dtype) for one in operands]
+        + [
+            pltpu.SemaphoreType.DMA((len(operands),)),
+            pltpu.VMEM((micro, rows, width), BF),
+            pltpu.SemaphoreType.DMA((1,)),
+            pltpu.SemaphoreType.DMA((1,)),
             pltpu.VMEM((micro * rows, LANES), F32),
             pltpu.VMEM((micro * rows, LANES), F32),
             pltpu.VMEM((keys, rows), F32),
@@ -1087,27 +1481,24 @@
             collective_id=3, has_side_effects=True, vmem_limit_bytes=VMEM_LIMIT
         ),
         name="attention_backward",
-    )(order, lens, gh2, x2, gy, x, wq, wo, gain_attn, gain_mlp, freq, qs, kv, lse, obt, grads)
+    )(order, lens, gain_attn, gain_mlp, freq, *operands, out_par, grads)
     if merged:
         return result
-    dx, att_o, att_q, vec = result
-    return dx, reduce_grads(n, ctx, grads, att_o, att_q, vec)
+    dx, outputs, att_o, att_q, vec = result
+    return dx, outputs, reduce_grads(n, ctx, grads, att_o, att_q, vec)
 
 
 def reduce_kernel(n, ctx, grads, att_o, att_q, vec, fin, *scratch):
     sums = Sums(n, ctx, grads, fin, scratch)
-    width, proj = att_o.shape[-1], att_q.shape[-1]
     enter(sums.around())
-    sums.start(2)
+    sums.start()
     sums.vec[0] = vec[...]
-    sums.total[PIECES] = jnp.zeros(sums.total.shape[1:], BF)
-    sums.total[PIECES + 1] = jnp.zeros(sums.total.shape[1:], BF)
+    for k in range(PIECES, ALL_PIECES):
+        sums.total[k] = jnp.zeros(sums.total.shape[1:], BF)
     sums.own_copy().wait()
-    for _ in sums.fold(
-        att_o, sums.core_o, sums.par_o, sums.ring_o, sums.total.at[PIECES, :, pl.ds(0, width)]
-    ):
+    for _ in sums.fold(att_o, sums.core_o, sums.par_o, sums.ring_o, PIECES):
         pass
-    fold_sums(sums, att_q, 0, width, proj)
+    fold_sums(sums, att_q, 0)
 
 
 def reduce_grads(n, ctx, grads, att_o, att_q, vec):
@@ -1131,21 +1522,25 @@
     n, units, padded, proj, width = size
     replicas = n // TP
     high = width // n
+    wide = fin.shape[-1]
     for half in range(2):
         for k in range(TP):
-            whole = fin[2 * k + half].astype(F32)
+            whole = jnp.concatenate(
+                [fin[4 * k + 2 * half + q].astype(F32) for q in range(2)], axis=1
+            )
             for q in range(replicas):
                 at = ((half * replicas + q) * TP + k) * units
                 g_gu[:, at : at + units] = whole[:, q * padded : q * padded + units]
+    each = wide // padded
     for k in range(n):
-        at = (k % replicas) * padded
-        turn[k * high : (k + 1) * high, :] = fin[2 * TP + k // replicas, :, at : at + padded].astype(
-            F32
-        )
+        at = (k % each) * padded
+        turn[k * high : (k + 1) * high, :] = fin[4 * TP + k // each, :, at : at + padded].astype(F32)
     g_down[...] = turn[...].T[:units, :]
-    g_out[...] = fin[PIECES, :, :width].astype(F32)
-    g_qkv[...] = fin[PIECES + 1, :, :proj].astype(F32)
-    vec[...] = fin[PIECES + 1, :VEC, proj : proj + LANES].astype(F32)
+    g_out[:, :wide] = fin[PIECES].astype(F32)
+    g_out[:, wide:] = fin[PIECES + 1, :, : width - wide].astype(F32)
+    g_qkv[:, :wide] = fin[PIECES + 2].astype(F32)
+    g_qkv[:, wide:] = fin[PIECES + 3, :, : proj - wide].astype(F32)
+    vec[...] = fin[PIECES + 3, :VEC, proj - wide : proj - wide + LANES].astype(F32)
 
 
 def finish_grads(n, fin, units, padded, proj, width):
@@ -1190,9 +1585,6 @@
     qk = (HQ + KVH) * HD
     vw = KVH * HD
 
-    wgu = w_gate_up.reshape(high, 2, replicas, TP, units)
-    wgu = pad_to(wgu.transpose(3, 0, 1, 2, 4), 4, padded).reshape(TP, high, 2 * quarter)
-    wd = pad_to(w_down, 0, padded)
     small = jnp.concatenate(
         [
             pad_to(b_qkv, 0, 2 * LANES).reshape(2, LANES),
@@ -1201,29 +1593,39 @@
             jnp.zeros((12, LANES), BF),
         ]
     )
-    wq_all, wo_all, sm_all, wgu_t, wd_t, gd_all = gather_weights(
-        n, w_qkv, w_out, small, wgu, wd, gy
-    )
-    wq_all = wq_all.reshape(width, proj)
-    wo_all = wo_all.reshape(width, width)
-    bias = sm_all[:, :2].reshape(n, 2 * LANES)[:, : b_qkv.shape[0]].reshape(1, proj).astype(F32)
-    gain_attn = sm_all[:, 2, :high].reshape(1, width).astype(F32)
-    gain_mlp = sm_all[:, 3, :high].reshape(1, width).astype(F32)
-    wgu_t = wgu_t.reshape(width, 2 * quarter)
-    wd_t = wd_t.reshape(quarter, width)
-
     half = HD // 2
     freqs = np.power(np.float32(ROPE_BASE), -(np.arange(half, dtype=np.float32) * (2.0 / HD)))
     freq = jnp.asarray(np.tile(freqs.astype(np.float32), (8, LANES // half)))
-    h2, x2, qs, kv, lse, obt = attention_forward(
-        ctx, order[0], lengths[0], x, wq_all, wo_all, bias, gain_attn, gain_mlp, freq
-    )
-    gd_all = gd_all.transpose(1, 0, 2, 3)
-    out, gh2, grads = mlp(n, h2, gd_all, wgu_t, wd_t)
-    outputs = (x2 + out).astype(BF)
-    dx, fin = attention_backward(
+    if ctx <= 4 and high % 16 == 0 and units % 32 == 0:
+        (
+            h2, x2, qs, kv, lse, obt, wq_all, wo_all, gain_attn, gain_mlp, wgu_t, wd_t, gd_all,
+        ) = gather_and_attend(
+            n, ctx, order[0], lengths[0], x, w_qkv, w_out, small, w_gate_up, w_down, gy, freq,
+            padded,
+        )
+        wq_all = wq_all.reshape(width, proj)
+        wo_all = wo_all.reshape(width, width)
+    else:
+        wgu = w_gate_up.reshape(high, 2, replicas, TP, units)
+        wgu = pad_to(wgu.transpose(3, 1, 0, 2, 4), 4, padded).reshape(TP, 2, high, quarter)
+        wq_all, wo_all, sm_all, wgu_t, wd_t, gd_all = gather_weights(
+            n, w_qkv, w_out, small, wgu, pad_to(w_down, 0, padded), gy
+        )
+        wq_all = wq_all.reshape(width, proj)
+        wo_all = wo_all.reshape(width, width)
+        bias = sm_all[:, :2].reshape(n, 2 * LANES)[:, : b_qkv.shape[0]].reshape(1, proj)
+        gain_attn = sm_all[:, 2, :high].reshape(1, width).astype(F32)
+        gain_mlp = sm_all[:, 3, :high].reshape(1, width).astype(F32)
+        h2, x2, qs, kv, lse, obt = attention_forward(
+            ctx, order[0], lengths[0], x, wq_all, wo_all, bias.astype(F32), gain_attn, gain_mlp,
+            freq,
+        )
+    wgu_t = wgu_t.reshape(2, width, quarter)
+    wd_t = wd_t.reshape(quarter, width)
+    out, out_par, gh2, grads = mlp(n, h2, gd_all, wgu_t, wd_t)
+    dx, outputs, fin = attention_backward(
         n, ctx, order[0], lengths[0], gh2, x2, gy, x, wq_all, wo_all, gain_attn, gain_mlp, freq,
-        qs, kv, lse, obt, grads,
+        qs, kv, lse, obt, out, out_par, grads,
     )
     g_gu, g_down, g_qkv, g_out, vec = finish_grads(n, fin, units, padded, proj, width)
     vec = vec.reshape(VEC * LANES)

time: 449 us -> 325 us (0.72)
  Pallas kernels: 411 us -> 312 us
  local copies, waits for them, and re-layouts: 24.4 us -> 7.47 us
    pallas_call x2 -> x1, Pallas kernels: 144 us -> 80.5 us  [gather_and_attend(): pl.pallas_call(functools.partial(front_kernel, (n, micro, rows, ctx)), ou...]
    pallas_call x1, Pallas kernels: 90.4 us -> 67.6 us  [mlp(): pl.pallas_call(functools.partial(mlp_kernel, (micro, rows, width, replica...]
    pallas_call x1, Pallas kernels: 170 us -> 157 us  [attention_backward(): pl.pallas_call(functools.partial(backward_kernel, (n, micro, rows, ctx),...]
    reshape x3 -> x0, local copies, waits for them, and re-layouts: 9.97 us -> none  [the longest x2 7.24 us: local(): wgu = w_gate_up.reshape(high, 2, replicas, TP, units)]
where the time goes in v3:
time: 325 us; the launch traced here: 321 us
  Pallas kernels  312 us (96%)
  local copies, waits for them, and re-layouts  7.47 us (2%)
    pallas_call x1, Pallas kernels, attention_backward(): pl.pallas_call(functools.partial(backward_kernel, (n, micro, rows, ctx),...  157 us
    pallas_call x1, Pallas kernels, gather_and_attend(): pl.pallas_call(functools.partial(front_kernel, (n, micro, rows, ctx)), ou...  80.5 us
    pallas_call x1, Pallas kernels, mlp(): pl.pallas_call(functools.partial(mlp_kernel, (micro, rows, width, replica...  67.6 us

profile of v3, /device:TPU:0, one launch (start us, length us, event | category | flops | bytes accessed | tf_op | source)
XLA Modules:
  0.0 321.0 jit_solution(10178969779407194605)
XLA Ops:
  0.6 0.7 pad_bitcast_fusion
  1.3 0.1 pad.17.clone
  1.4 0.7 pad_bitcast_fusion.2
  2.1 0.7 maximum_maximum_fusion.sm
  2.7 80.5 %gather_and_attend.1 = (bf16[2,256,896]{2,1,0:T(8,128)(2,1)}, f32[2,256,896]{2,1,0:T(8,128)}, bf16[2,7,256,128]{3,2,1,0:T(8,128)(2,1)}, bf16[2,4,256,256]{3,2,1,...) custom-call(s32[2,8]{1,0:T(2,128)} %bitcast.27, ...), custom_call_target="tpu_custom_call" | custom-call | tf_op jit(solution)/shard_map/gather_and_attend/pallas_call | solution.py:709
  83.3 67.6 %mlp.1 = (f32[2,256,896]{2,1,0:T(8,128)}, bf16[2,256,896]{2,1,0:T(8,128)(2,1)}, f32[2,256,896]{2,1,0:T(8,128)}, bf16[2,24,112,640]{3,2,1,0:T(8,128)(2,1)}) custom-call(bf16[2,256,896]{2,1,0:T(8,128)(2,1)} %get-tuple-element.38.h2, bf16[2,4,256,896]{3,2,1,0:T(8,128)(2,1)} %get-tuple-element.39.gd_hbm, bf16[2,896,1280]{2,1,0:T(8,128)(2,1)} %bitcast.17, ...), custom_call_target="tpu_custom_call" | custom-call | tf_op jit(solution)/shard_map/mlp/pallas_call | solution.py:916
  150.9 157.3 %attention_backward.1 = (f32[2,256,896]{2,1,0:T(8,128)}, bf16[2,256,896]{2,1,0:T(8,128)(2,1)}, bf16[28,112,640]{2,1,0:T(8,128)(2,1)}) custom-call(s32[2,8]{1,0:T(2,128)} %bitcast.28, s32[2,4]{1,0:T(2,128)} %bitcast.30, f32[1,896]{1,0:T(1,128)} %get-tuple-element.35.gain_attn, f32[1,896]{1,0:T(1,128)} %get-tuple-element.36.gain_mlp, ...), custom_call_target="tpu_custom_call" | custom-call | tf_op jit(solution)/shard_map/attention_backward/pallas_call | solution.py:1449
  308.3 0.0 copy-start.1
  308.3 0.0 copy-start
  308.3 6.2 %finish_grads.1 = (f32[112,9728]{1,0:T(8,128)}, f32[608,896]{1,0:T(8,128)}, f32[112,1152]{1,0:T(8,128)}, f32[112,896]{1,0:T(8,128)}, f32[32,128]{1,0:T(8,128)}) custom-call(bf16[28,112,640]{2,1,0:T(8,128)(2,1)} %get-tuple-element.54.fin), custom_call_target="tpu_custom_call" | custom-call | tf_op jit(solution)/shard_map/finish_grads/pallas_call | solution.py:1549
  314.4 1.4 fusion
  315.8 1.3 dynamic_slice.13
  317.1 1.3 dynamic_slice.12
  318.3 0.0 copy-done.1
  318.3 0.9 copy.24
  319.3 0.0 copy-done
  319.3 1.2 copy.25
  (1 shorter events, 0.0 us)
Async XLA Ops:
  308.3 10.1 %copy-start.1 = (bf16[2,256,896]{2,1,0:T(8,128)(2,1)S(1)}, bf16[2,256,896]{2,1,0:T(8,128)(2,1)}, u32[]{:S(2)}) copy-start(bf16[2,256,896]{2,1,0:T(8,128)(2,1)} %get-tuple-element.52) | copy-start | bytes 2752516
  308.3 11.0 %copy-start = (f32[2,256,896]{2,1,0:T(8,128)S(1)}, f32[2,256,896]{2,1,0:T(8,128)}, u32[]{:S(2)}) copy-start(f32[2,256,896]{2,1,0:T(8,128)} %get-tuple-element.53) | copy-start | bytes 5505028

commit v4 on v3

--- a/solution.py
+++ b/solution.py
@@ -22,14 +22,15 @@
 ALL_PIECES = PIECES + 4
 RING = 6
 HOP = 2
-RATE = 3
+RATE = 2
 EARLY = 2
+AHEAD = 4
 SLOTS = 8
 VEC = 32
 BF = jnp.bfloat16
 F32 = jnp.float32
 MESH = pl.DeviceIdType.MESH
-VMEM_LIMIT = 60 * 1024 * 1024
+VMEM_LIMIT = 62 * 1024 * 1024
 
 
 def flip1(v):
@@ -962,11 +963,11 @@
         self.n, self.ctx, self.grads, self.fin = n, ctx, grads, fin
         (
             self.total, self.peer_in, self.pre, self.suf, self.suf_out, self.land,
-            self.core_o, self.par_o, self.ring_o, self.core_q, self.par_q, self.ring_q,
             self.vec, self.vec_in,
             self.ys, self.yr, self.ps, self.pr, self.ss, self.sr, self.fs, self.fr,
             self.asend, self.arecv, self.own_sem, self.out_sem,
-        ) = scratch
+        ) = scratch[:20]
+        self.fold_scratch = scratch[20:]
         self.replicas = n // TP
         self.f, self.c = lax.axis_index("fsdp"), lax.axis_index("ctx")
         f, c = self.f, self.c
@@ -978,7 +979,7 @@
         self.links = Links(self.asend, self.arecv)
 
     @staticmethod
-    def scratch(n, high, wide, width, proj):
+    def scratch(n, high, wide, columns):
         replicas = n // TP
         sems = pltpu.SemaphoreType.DMA
         peers = replicas - 1
@@ -989,18 +990,22 @@
             pltpu.VMEM((ALL_PIECES, high, wide), BF),
             pltpu.VMEM((RING, high, wide), BF),
             pltpu.VMEM((4 * TP, high, wide), BF),
-            pltpu.VMEM((replicas, 2, high, width), BF),
-            pltpu.VMEM((replicas, high, width), BF),
-            pltpu.VMEM((peers, high, width), BF),
-            pltpu.VMEM((replicas, 2, high, proj), BF),
-            pltpu.VMEM((replicas, high, proj), BF),
-            pltpu.VMEM((peers, high, proj), BF),
             pltpu.VMEM((3, VEC, LANES), F32),
             pltpu.VMEM((2 + peers, VEC, LANES), F32),
             sems((peers * PIECES,)), sems((peers * PIECES,)),
             sems((ALL_PIECES,)), sems((ALL_PIECES,)), sems((ALL_PIECES,)), sems((ALL_PIECES,)),
             sems((4 * TP,)), sems((4 * TP,)),
-            sems((6 + 3 * peers,)), sems((6 + 3 * peers,)), sems((1,)), sems((ALL_PIECES,)),
+            sems(((len(columns) + 1) * (2 + peers),)), sems(((len(columns) + 1) * (2 + peers),)),
+            sems((1,)), sems((ALL_PIECES,)),
+        ] + [
+            one
+            for wide_here in columns
+            for one in (
+                pltpu.VMEM((replicas, 2, 2, high, wide_here), BF),
+                pltpu.VMEM((replicas, 2, high, wide_here), BF),
+                pltpu.VMEM((replicas, high, wide_here), BF),
+                pltpu.VMEM((peers, high, wide_here), BF),
+            )
         ]
 
     def around(self):
@@ -1024,13 +1029,9 @@
 
     def start(self):
         self.own_copy().start()
-
-        def body(k, carry):
+        for k in range(AHEAD):
             for j in range(self.replicas - 1):
                 self.peer_copy(j, k).start()
-            return carry
-
-        lax.fori_loop(0, PIECES, body, 0)
 
     def pre_copy(self, k, src):
         return pltpu.make_async_remote_copy(
@@ -1053,6 +1054,11 @@
 
     def tick(self, time):
         c, ctx, total = self.c, self.ctx, self.total
+
+        @pl.when(time + AHEAD < PIECES)
+        def _():
+            for j in range(self.replicas - 1):
+                self.peer_copy(j, time + AHEAD).start()
 
         @pl.when(time < PIECES)
         def _():
@@ -1181,103 +1187,174 @@
         lax.fori_loop(0, PIECES, peers, 0)
         self.links.drain()
 
-
-    def fold(self, own, got_core, got_par, got_ring, first, extra=False):
-        replicas = self.replicas
-        at = self.links.put(own.at[:, :, 1 - self.core], got_core, self.sib)
-        at_vec = None
-        if extra:
-            at_vec = self.links.put(self.vec.at[0], self.vec_in.at[0], self.sib)
-        yield
-        self.links.arrive(at, got_core)
-        for replica in range(replicas):
-            for s in range(2):
-                add_into(
-                    got_core.at[replica, s], got_core.at[replica, s],
-                    own.at[replica, s, self.core],
-                )
-        at = self.links.put(got_core.at[:, 1 - self.side], got_par, self.par)
-        if extra:
-            self.links.arrive(at_vec, self.vec_in.at[0])
-            self.vec[1] = self.vec[0] + self.vec_in[0]
-            at_vec = self.links.put(self.vec.at[1], self.vec_in.at[1], self.par)
-        yield
-        self.links.arrive(at, got_par)
-        for replica in range(replicas):
-            add_into(got_par.at[replica], got_par.at[replica], got_core.at[replica, self.side])
-        ats, vec_ats = [], []
-        if extra:
-            self.links.arrive(at_vec, self.vec_in.at[1])
-            self.vec[2] = self.vec[1] + self.vec_in[1]
-        for j, peer in enumerate(self.peers):
-            ats.append(
-                self.links.put(got_par.at[(self.r + j + 1) % replicas], got_ring.at[j], peer)
-            )
-            if extra:
-                vec_ats.append(self.links.put(self.vec.at[2], self.vec_in.at[2 + j], peer))
-        yield
-        width, wide = got_ring.shape[-1], self.total.shape[-1]
-        mine = got_par.at[self.r]
-        for j, at in enumerate(ats):
-            self.links.arrive(at, got_ring.at[j])
-            add_into(mine, mine, got_ring.at[j])
-        self.total[first] = mine[:, :wide]
-        self.total[first + 1, :, : width - wide] = mine[:, wide:]
-        if extra:
-            vec = self.vec[2]
-            for j, at in enumerate(vec_ats):
-                self.links.arrive(at, self.vec_in.at[2 + j])
-                vec = vec + self.vec_in[2 + j]
-            self.total[first + 1, :VEC, width - wide : width - wide + LANES] = vec.astype(BF)
-        yield
-
-
-def backward_kernel(
-    size, merged, order, lens, gain_attn, gain_mlp, freq, *rest
-):
+    def place(self, column, value):
+        wide = self.total.shape[-1]
+        done = 0
+        while done < value.shape[1]:
+            piece, at = divmod(column + done, wide)
+            count = min(wide - at, value.shape[1] - done)
+            self.total[PIECES + piece, : value.shape[0], at : at + count] = value[
+                :, done : done + count
+            ]
+            done += count
+
+
+class Fold:
+    def __init__(self, sums, index, column):
+        self.sums, self.column = sums, column
+        self.own, self.got_core, self.got_par, self.got_ring = sums.fold_scratch[
+            4 * index : 4 * index + 4
+        ]
+        replicas, r = sums.replicas, sums.r
+        self.src_core = self.own.at[:, :, 1 - sums.core]
+        self.mine_core = [
+            [self.own.at[k, s, sums.core] for s in range(2)] for k in range(replicas)
+        ]
+        self.src_par = self.got_core.at[:, 1 - sums.side]
+        self.mine_par = [self.got_core.at[k, sums.side] for k in range(replicas)]
+        self.src_ring = [
+            self.got_par.at[(r + j + 1) % replicas] for j in range(replicas - 1)
+        ]
+        self.mine = self.got_par.at[r]
+
+    def set(self, k, value):
+        self.own[k // TP, (k // 2) % 2, k % 2] = value.astype(BF)
+
+    def over_core(self):
+        self.at = self.sums.links.put(self.src_core, self.got_core, self.sums.sib)
+
+    def over_x(self):
+        links = self.sums.links
+        links.arrive(self.at, self.got_core)
+        for k, pair in enumerate(self.mine_core):
+            for s, mine in enumerate(pair):
+                add_into(self.got_core.at[k, s], self.got_core.at[k, s], mine)
+        self.at = links.put(self.src_par, self.got_par, self.sums.par)
+
+    def over_y(self):
+        links = self.sums.links
+        links.arrive(self.at, self.got_par)
+        for k, mine in enumerate(self.mine_par):
+            add_into(self.got_par.at[k], self.got_par.at[k], mine)
+        self.ats = [
+            links.put(src, self.got_ring.at[j], peer)
+            for j, (src, peer) in enumerate(zip(self.src_ring, self.sums.peers))
+        ]
+
+    def finish(self):
+        for j, at in enumerate(self.ats):
+            self.sums.links.arrive(at, self.got_ring.at[j])
+            add_into(self.mine, self.mine, self.got_ring.at[j])
+        self.sums.place(self.column, self.mine[...])
+
+
+class FoldVectors:
+    def __init__(self, sums, column):
+        self.sums, self.column = sums, column
+
+    def over_core(self):
+        sums = self.sums
+        self.at = sums.links.put(sums.vec.at[0], sums.vec_in.at[0], sums.sib)
+
+    def over_x(self):
+        sums = self.sums
+        sums.links.arrive(self.at, sums.vec_in.at[0])
+        sums.vec[1] = sums.vec[0] + sums.vec_in[0]
+        self.at = sums.links.put(sums.vec.at[1], sums.vec_in.at[1], sums.par)
+
+    def over_y(self):
+        sums = self.sums
+        sums.links.arrive(self.at, sums.vec_in.at[1])
+        sums.vec[2] = sums.vec[1] + sums.vec_in[1]
+        self.ats = [
+            sums.links.put(sums.vec.at[2], sums.vec_in.at[2 + j], peer)
+            for j, peer in enumerate(sums.peers)
+        ]
+
+    def finish(self):
+        sums = self.sums
+        vec = sums.vec[2]
+        for j, at in enumerate(self.ats):
+            sums.links.arrive(at, sums.vec_in.at[2 + j])
+            vec = vec + sums.vec_in[2 + j]
+        sums.place(self.column, vec.astype(BF))
+
+
+def fold_columns(width, proj):
+    pairs = HQ // 2
+    early = (pairs // 2 + 1) * LANES
+    sizes = (width, early, HQ * HD - early, proj - HQ * HD)
+    return sizes, (0, width, width + early)
+
+
+class Plain:
+    def __init__(self, own):
+        self.own = own
+
+    def set(self, k, value):
+        self.own[k // TP, (k // 2) % 2, k % 2] = value.astype(BF)
+
+    def over_core(self):
+        pass
+
+    over_x = over_y = finish = over_core
+
+
+def backward_kernel(size, merged, order, lens, gain_attn, gain_mlp, freq, *rest):
     n, micro, rows, ctx = size
     hbm, rest = rest[:11], rest[11:]
     out_par, grads, dx, outputs = rest[:4]
     rest = rest[4:]
-    outs = 1 if merged else 3
+    outs = 1 if merged else 5
     fin, rest = rest[:outs], rest[outs:]
     (
-        x2, gh2, gy, wo, obt, kv, qs, lse, x, wq, out, staged_sems,
-        out_in, out_send, out_recv, cos_ref, sin_ref, bias_ref, kvar, kvar_turned, vvar, go_ref, gp, h1t, gk, gv, part, land,
-        att_o, att_q, vec_wide, send, recv,
-    ), rest = rest[:33], rest[33:]
+        x2, gh2, gy, wo, x, obt, kv, qs, lse, wq, out, staged_sems,
+        out_in, out_send, out_recv, cos_ref, sin_ref, bias_ref, kvar, kvar_turned, vvar,
+        go_ref, gp, h1t, gk, gv, part, land, vec_wide, send, recv,
+    ), rest = rest[:31], rest[31:]
     staged = Staged(
-        list(zip(hbm, (x2, gh2, gy, wo, obt, kv, qs, lse, x, wq, out))), staged_sems
+        list(zip(hbm, (x2, gh2, gy, wo, x, obt, kv, qs, lse, wq, out))), staged_sems
     )
     group = HQ // KVH
     pairs = HQ // 2
     width = HQ * HD
-    replicas = n // TP
     high = width // n
     proj = wq.shape[1]
     scale = 1.0 / math.sqrt(HD)
     f, c = lax.axis_index("fsdp"), lax.axis_index("ctx")
     others = [(f, (c + j) % ctx) for j in range(1, ctx)]
     back = [(c - j + ctx) % ctx for j in range(1, ctx)]
+    sizes, starts = fold_columns(width, proj)
     if merged:
         sums = Sums(n, ctx, grads, fin[0], rest)
         enter(others + sums.around())
         sums.start()
+        last = (ALL_PIECES - PIECES - 1) * sums.total.shape[-1]
+        folds = [Fold(sums, k, start) for k, start in enumerate(starts + (last,))]
+        fold_v = FoldVectors(sums, last + sizes[3])
     else:
         enter(others + [(flip2(f), c)])
+        folds = [Plain(own) for own in fin[:4]]
+        fold_v = Plain(None)
+    fold_o, fold_a, fold_b, fold_k = folds
     out_links = Links(out_send, out_recv)
     out_at = out_links.put(out_par, out_in, (flip2(f), c))
     links = Links(send, recv)
-    arrivals = []
+    ticks = [0]
+
+    def advance(upto):
+        if merged and upto > ticks[0]:
+            lax.fori_loop(ticks[0], upto, sums.step, 0)
+            ticks[0] = upto
+
     if merged:
         for k in range(PIECES, ALL_PIECES):
             sums.total[k] = jnp.zeros(sums.total.shape[1:], BF)
         sums.own_copy().wait()
     for m in range(micro):
         fill_tables(m, rows, c, freq, order, lens, cos_ref, sin_ref)
-        if merged:
-            lax.fori_loop(EARLY * m // micro, EARLY * (m + 1) // micro, sums.step, 0)
-        staged.need(4)
+        advance(EARLY * (m + 1) // micro)
+        staged.need(5)
         stream = x2[m]
         inverse = inverse_norm(stream)
         normed = stream * inverse
@@ -1293,18 +1370,40 @@
         spread = dot_nt(grad.astype(BF), wo[...]).astype(BF)
         for p in range(pairs):
             go_ref[m, p] = spread[:, p * LANES : (p + 1) * LANES]
+        stream = x[m].astype(F32)
+        h1t[:, m * rows : (m + 1) * rows] = (
+            (stream * inverse_norm(stream) * gain_attn[...]).T.astype(BF)
+        )
     staged.need(len(staged.copies))
     for k in range(n):
         term = dot(obt[0, k * high : (k + 1) * high, :], dx[0].astype(BF))
         for m in range(1, micro):
             term = term + dot(obt[m, k * high : (k + 1) * high, :], dx[m].astype(BF))
-        att_o[k // TP, (k // 2) % 2, k % 2] = term.astype(BF)
-    if merged:
-        fold_o = sums.fold(att_o, sums.core_o, sums.par_o, sums.ring_o, PIECES)
-        next(fold_o)
+        fold_o.set(k, term)
+    fold_o.over_core()
+
+    def columns(fold, lo, hi):
+        for k in range(n):
+            fold.set(k, dot(h1t[k * high : (k + 1) * high, :], gp[:, lo:hi]))
+
+    low = lax.broadcasted_iota(jnp.int32, (ctx * rows, LANES), 1) < HD
+    mid = pairs // 2
+    part_src = [
+        [[part.at[m, g, other[1]] for other in others] for g in range(KVH)] for m in range(micro)
+    ]
+    part_dst = [[land.at[m, g, c] for g in range(KVH)] for m in range(micro)]
+    arrivals = [[None] * KVH for _ in range(micro)]
+
+    def send_group(m, g):
+        keys = gk[g, 0] + pltpu.roll(gk[g, 1], HD, 1)
+        values = pltpu.roll(gv[g, 0], HD, 1) + gv[g, 1]
+        whole = jnp.where(low, keys, values).astype(BF)
+        part[m, g] = whole.reshape(ctx, rows, LANES)
+        arrivals[m][g] = [
+            links.put(src, part_dst[m][g], other) for src, other in zip(part_src[m][g], others)
+        ]
+
     for m in range(micro):
-        if merged and m > 0:
-            next(fold_o)
         fill_bias(m, rows, c, order, lens, bias_ref)
         both = kv[m].reshape(ctx * rows, 2 * LANES).astype(F32)
         fill_heads(both[:, :LANES], kvar)
@@ -1334,45 +1433,64 @@
             turned = turned * cosine - swap_halves(turned) * sine
             at = pl.multiple_of(p * LANES, LANES)
             gp[m * rows : (m + 1) * rows, pl.ds(at, LANES)] = turned.astype(BF)
+
+            if m == 0:
+                pl.when(p == 0)(fold_o.over_x)
+
+            @pl.when(p == mid)
+            def _():
+                send_group(m, 0)
+                if m == micro - 1:
+                    columns(fold_a, 0, sizes[1])
+                    fold_a.over_core()
+                elif m == 0:
+                    fold_o.over_y()
+
+            if m == micro - 1:
+                pl.when(p == mid + 1)(fold_a.over_x)
+
+            @pl.when(p == pairs - 1)
+            def _():
+                send_group(m, 1)
+                if m == micro - 1:
+                    fold_a.over_y()
+
             if merged:
                 step = m * pairs + p
                 lax.fori_loop(
                     EARLY + RATE * step // 2, EARLY + RATE * (step + 1) // 2, sums.step, 0
                 )
-
             return carry
 
         lax.fori_loop(0, pairs, pair, 0)
-        low = lax.broadcasted_iota(jnp.int32, (ctx * rows, LANES), 1) < HD
-        for k, acc in enumerate((gk, gv)):
-            first = acc[0, 0] + pltpu.roll(acc[0, 1], HD, 1)
-            second = pltpu.roll(acc[1, 0], HD, 1) + acc[1, 1]
-            whole = jnp.where(low, first, second).astype(BF)
-            part[m, :, :, k * LANES : (k + 1) * LANES] = whole.reshape(ctx, rows, LANES)
-        arrivals.append(
-            [links.put(part.at[m, other[1]], land.at[m, c], other) for other in others]
-        )
-    if merged:
-        next(fold_o)
+    ticks[0] = EARLY + RATE * micro * pairs // 2
+    spare = max(0, PIECES - ticks[0])
+    first = ticks[0]
+    columns(fold_b, sizes[1], width)
+    fold_b.over_core()
+    advance(first + spare * 2 // 8)
+    fold_b.over_x()
+    advance(first + spare * 4 // 8)
     for m in range(micro):
-        stream = x[m].astype(F32)
-        h1t[:, m * rows : (m + 1) * rows] = (
-            (stream * inverse_norm(stream) * gain_attn[...]).T.astype(BF)
-        )
-    for m in range(micro):
-        total = part[m, c].astype(F32)
-        for at, source in zip(arrivals[m], back):
-            links.arrive(at, land.at[m, source])
-            total = total + land[m, source].astype(F32)
+        totals = []
+        for g in range(KVH):
+            total = part[m, g, c].astype(F32)
+            for at, source in zip(arrivals[m][g], back):
+                links.arrive(at, land.at[m, g, source])
+                total = total + land[m, g, source].astype(F32)
+            totals.append(total)
+        lower = lax.broadcasted_iota(jnp.int32, (rows, LANES), 1) < HD
         cosine = cos_ref[m * rows : (m + 1) * rows, :]
         sine = sin_ref[m * rows : (m + 1) * rows, :]
-        grad_keys = total[:, :LANES]
+        grad_keys = jnp.where(lower, totals[0], pltpu.roll(totals[1], HD, 1))
         grad_keys = grad_keys * cosine - swap_halves(grad_keys) * sine
         gp[m * rows : (m + 1) * rows, width : width + LANES] = grad_keys.astype(BF)
-        gp[m * rows : (m + 1) * rows, width + LANES :] = total[:, LANES:].astype(BF)
-    for k in range(n):
-        term = dot(h1t[k * high : (k + 1) * high, :], gp[...])
-        att_q[k // TP, (k // 2) % 2, k % 2] = term.astype(BF)
+        grad_values = jnp.where(lower, pltpu.roll(totals[0], HD, 1), totals[1])
+        gp[m * rows : (m + 1) * rows, width + LANES :] = grad_values.astype(BF)
+    columns(fold_k, width, proj)
+    fold_k.over_core()
+    advance(first + spare * 5 // 8)
+    fold_b.over_y()
     for m in range(micro):
         grad_project = gp[m * rows : (m + 1) * rows, :]
         stream = x[m].astype(F32)
@@ -1388,33 +1506,32 @@
         dx[m] = dx[m] + inverse * (
             grad - normed * jnp.mean(grad * normed, axis=1, keepdims=True)
         )
+    vec = sums.vec.at[0] if merged else fin[4]
+    vec[...] = jnp.zeros((VEC, LANES), F32)
+    for k in range(vec_wide.shape[1] // LANES):
+        vec[k : k + 1, :] = vec_wide[:, k * LANES : (k + 1) * LANES]
+    fold_v.over_core()
+    fold_k.over_x()
+    advance(first + spare * 6 // 8)
+    fold_v.over_x()
+    fold_o.finish()
+    fold_a.finish()
+    advance(first + spare * 7 // 8)
+    fold_k.over_y()
+    fold_v.over_y()
+    advance(first + spare)
     out_links.arrive(out_at, out_in)
     for m in range(micro):
         outputs[m] = (x2[m] + out[m] + out_in[m].astype(F32)).astype(BF)
     out_links.drain()
-    vec = sums.vec.at[0] if merged else fin[2]
-    vec[...] = jnp.zeros((VEC, LANES), F32)
-    for k in range(vec_wide.shape[1] // LANES):
-        vec[k : k + 1, :] = vec_wide[:, k * LANES : (k + 1) * LANES]
+    fold_b.finish()
+    advance(ALL_PIECES - 1)
+    fold_k.finish()
+    fold_v.finish()
     if merged:
-        next(fold_o)
-        fold_sums(sums, att_q, EARLY + RATE * micro * pairs // 2)
-    else:
-        fin[0][...] = att_o[...]
-        fin[1][...] = att_q[...]
+        advance(sums.ticks)
+        sums.close()
     links.drain()
-
-
-def fold_sums(sums, att_q, done):
-    fold_q = sums.fold(att_q, sums.core_q, sums.par_q, sums.ring_q, PIECES + 2, True)
-    ready = max(0, PIECES + 2 - done)
-    next(fold_q)
-    for k in range(3):
-        upto = done + ready * (k + 1) // 3
-        lax.fori_loop(done + ready * k // 3, upto, sums.step, 0)
-        next(fold_q)
-    lax.fori_loop(done + ready, sums.ticks, sums.step, 0)
-    sums.close()
 
 
 def attention_backward(
@@ -1430,27 +1547,24 @@
     vmem = pl.BlockSpec(memory_space=pltpu.VMEM)
     smem = pl.BlockSpec(memory_space=pltpu.SMEM)
     anywhere = pl.BlockSpec(memory_space=pl.ANY)
-    copies = micro * (ctx - 1)
+    copies = micro * KVH * (ctx - 1)
+    sizes, _ = fold_columns(width, proj)
     out_shape = [
         jax.ShapeDtypeStruct((micro, rows, width), F32),
         jax.ShapeDtypeStruct((micro, rows, width), BF),
     ]
-    shape_o = (replicas, 2, 2, high, width)
-    shape_q = (replicas, 2, 2, high, proj)
     if merged:
         out_shape += [jax.ShapeDtypeStruct((ALL_PIECES, high, wide), BF)]
     else:
         out_shape += [
-            jax.ShapeDtypeStruct(shape_o, BF),
-            jax.ShapeDtypeStruct(shape_q, BF),
-            jax.ShapeDtypeStruct((VEC, LANES), F32),
-        ]
-    operands = (x2, gh2, gy, wo, obt, kv, qs, lse, x, wq, out)
+            jax.ShapeDtypeStruct((replicas, 2, 2, high, size), BF) for size in sizes
+        ] + [jax.ShapeDtypeStruct((VEC, LANES), F32)]
+    operands = (x2, gh2, gy, wo, x, obt, kv, qs, lse, wq, out)
     result = pl.pallas_call(
         functools.partial(backward_kernel, (n, micro, rows, ctx), merged),
         out_shape=out_shape,
         in_specs=[smem, smem] + [vmem] * 3 + [anywhere] * 13,
-        out_specs=[vmem] * 2 + ([anywhere] if merged else [vmem] * 3),
+        out_specs=[vmem] * 2 + ([anywhere] if merged else [vmem] * 5),
         scratch_shapes=[pltpu.VMEM(one.shape, one.dtype) for one in operands]
         + [
             pltpu.SemaphoreType.DMA((len(operands),)),
@@ -1468,15 +1582,13 @@
             pltpu.VMEM((width, micro * rows), BF),
             pltpu.VMEM((KVH, 2, keys, LANES), F32),
             pltpu.VMEM((KVH, 2, keys, LANES), F32),
-            pltpu.VMEM((micro, ctx, rows, 2 * LANES), BF),
-            pltpu.VMEM((micro, ctx, rows, 2 * LANES), BF),
-            pltpu.VMEM(shape_o, BF),
-            pltpu.VMEM(shape_q, BF),
+            pltpu.VMEM((micro, KVH, ctx, rows, LANES), BF),
+            pltpu.VMEM((micro, KVH, ctx, rows, LANES), BF),
             pltpu.VMEM((1, proj + 2 * width), F32),
             pltpu.SemaphoreType.DMA((copies,)),
             pltpu.SemaphoreType.DMA((copies,)),
         ]
-        + (Sums.scratch(n, high, wide, width, proj) if merged else []),
+        + (Sums.scratch(n, high, wide, sizes) if merged else []),
         compiler_params=pltpu.CompilerParams(
             collective_id=3, has_side_effects=True, vmem_limit_bytes=VMEM_LIMIT
         ),
@@ -1484,11 +1596,12 @@
     )(order, lens, gain_attn, gain_mlp, freq, *operands, out_par, grads)
     if merged:
         return result
-    dx, outputs, att_o, att_q, vec = result
-    return dx, outputs, reduce_grads(n, ctx, grads, att_o, att_q, vec)
-
-
-def reduce_kernel(n, ctx, grads, att_o, att_q, vec, fin, *scratch):
+    dx, outputs, *parts, vec = result
+    return dx, outputs, reduce_grads(n, ctx, grads, parts, vec)
+
+
+def reduce_kernel(n, ctx, grads, *rest):
+    parts, vec, fin, scratch = rest[:4], rest[4], rest[5], rest[6:]
     sums = Sums(n, ctx, grads, fin, scratch)
     enter(sums.around())
     sums.start()
@@ -1496,32 +1609,71 @@
     for k in range(PIECES, ALL_PIECES):
         sums.total[k] = jnp.zeros(sums.total.shape[1:], BF)
     sums.own_copy().wait()
-    for _ in sums.fold(att_o, sums.core_o, sums.par_o, sums.ring_o, PIECES):
-        pass
-    fold_sums(sums, att_q, 0)
-
-
-def reduce_grads(n, ctx, grads, att_o, att_q, vec):
+    sizes = [part.shape[-1] for part in parts]
+    last = (ALL_PIECES - PIECES - 1) * sums.total.shape[-1]
+    folds = [
+        Fold(sums, k, start)
+        for k, start in enumerate((0, sizes[0], sizes[0] + sizes[1], last))
+    ] + [FoldVectors(sums, last + sizes[3])]
+    for fold, part in zip(folds, parts):
+        fold.own[...] = part[...]
+    for stage in ("over_core", "over_x", "over_y", "finish"):
+        for fold in folds:
+            getattr(fold, stage)()
+    lax.fori_loop(0, sums.ticks, sums.step, 0)
+    sums.close()
+
+
+def reduce_grads(n, ctx, grads, parts, vec):
     high, wide = grads.shape[2:]
     vmem = pl.BlockSpec(memory_space=pltpu.VMEM)
     anywhere = pl.BlockSpec(memory_space=pl.ANY)
     return pl.pallas_call(
         functools.partial(reduce_kernel, n, ctx),
         out_shape=jax.ShapeDtypeStruct((ALL_PIECES, high, wide), BF),
-        in_specs=[anywhere, vmem, vmem, vmem],
+        in_specs=[anywhere] + [vmem] * 5,
         out_specs=anywhere,
-        scratch_shapes=Sums.scratch(n, high, wide, att_o.shape[-1], att_q.shape[-1]),
+        scratch_shapes=Sums.scratch(n, high, wide, [part.shape[-1] for part in parts]),
         compiler_params=pltpu.CompilerParams(
             collective_id=4, has_side_effects=True, vmem_limit_bytes=VMEM_LIMIT
         ),
         name="reduce_grads",
-    )(grads, att_o, att_q, vec)
-
-
-def finish_kernel(size, fin, g_gu, g_down, g_qkv, g_out, vec, turn):
+    )(grads, *parts, vec)
+
+
+def finish_kernel(
+    size, dx, outputs, fin, g_gu, g_down, g_qkv, g_out, g_qk, g_v, g_attn, g_mlp, dx_out, outputs_out,
+    turn, vecs, dx_in, outputs_in, sems,
+):
     n, units, padded, proj, width = size
     replicas = n // TP
     high = width // n
+    through = [(dx, dx_in, dx_out), (outputs, outputs_in, outputs_out)]
+    coming = [
+        pltpu.make_async_copy(src, buf, sems.at[k]) for k, (src, buf, _) in enumerate(through)
+    ]
+    going = [
+        pltpu.make_async_copy(buf, dst, sems.at[2 + k]) for k, (_, buf, dst) in enumerate(through)
+    ]
+    for copy in coming:
+        copy.start()
+    f = lax.axis_index("fsdp")
+    vec = fin.at[ALL_PIECES - 1]
+    lane = proj - width
+    rows = vec[0:VEC, lane : lane + LANES].astype(F32)
+    vecs[...] = rows
+    for first, ref in ((0, g_qk), (width + LANES, g_v), (proj, g_attn), (proj + width, g_mlp)):
+        count = ref.shape[-1]
+        at = first + f * count
+        row = at // LANES
+        pair = jnp.concatenate(
+            [vecs[pl.ds(row, 1), :], vecs[pl.ds(row + 1, 1), :]], axis=1
+        )
+        pair = jnp.broadcast_to(pair, (8, 2 * LANES))
+        ref[...] = pltpu.roll(pair, 2 * LANES - (at - row * LANES), 1)[0:1, :count]
+    for a, b in zip(coming, going):
+        a.wait()
+        b.start()
     wide = fin.shape[-1]
     for half in range(2):
         for k in range(TP):
@@ -1536,16 +1688,20 @@
         at = (k % each) * padded
         turn[k * high : (k + 1) * high, :] = fin[4 * TP + k // each, :, at : at + padded].astype(F32)
     g_down[...] = turn[...].T[:units, :]
-    g_out[:, :wide] = fin[PIECES].astype(F32)
-    g_out[:, wide:] = fin[PIECES + 1, :, : width - wide].astype(F32)
-    g_qkv[:, :wide] = fin[PIECES + 2].astype(F32)
-    g_qkv[:, wide:] = fin[PIECES + 3, :, : proj - wide].astype(F32)
-    vec[...] = fin[PIECES + 3, :VEC, proj - wide : proj - wide + LANES].astype(F32)
-
-
-def finish_grads(n, fin, units, padded, proj, width):
+    ahead = ALL_PIECES - PIECES - 1
+    whole = jnp.concatenate([fin[PIECES + k] for k in range(ahead)], axis=1)
+    g_out[...] = whole[:, :width].astype(F32)
+    g_qkv[:, :width] = whole[:, width : 2 * width].astype(F32)
+    g_qkv[:, width:] = fin[ALL_PIECES - 1, :, : proj - width].astype(F32)
+    for copy in going:
+        copy.wait()
+
+
+def finish_grads(n, dx, outputs, fin, units, padded, proj, width):
     high = width // n
     vmem = pl.BlockSpec(memory_space=pltpu.VMEM)
+    anywhere = pl.BlockSpec(memory_space=pl.ANY)
+    one = lambda count: jax.ShapeDtypeStruct((1, count), F32)
     return pl.pallas_call(
         functools.partial(finish_kernel, (n, units, padded, proj, width)),
         out_shape=(
@@ -1553,14 +1709,25 @@
             jax.ShapeDtypeStruct((units, width), F32),
             jax.ShapeDtypeStruct((high, proj), F32),
             jax.ShapeDtypeStruct((high, width), F32),
-            jax.ShapeDtypeStruct((VEC, LANES), F32),
+            one((width + LANES) // n),
+            one(LANES // n),
+            one(high),
+            one(high),
+            jax.ShapeDtypeStruct(dx.shape, dx.dtype),
+            jax.ShapeDtypeStruct(outputs.shape, outputs.dtype),
         ),
-        in_specs=[vmem],
-        out_specs=[vmem] * 5,
-        scratch_shapes=[pltpu.VMEM((width, padded), F32)],
+        in_specs=[anywhere, anywhere, vmem],
+        out_specs=[vmem] * 8 + [anywhere] * 2,
+        scratch_shapes=[
+            pltpu.VMEM((width, padded), F32),
+            pltpu.VMEM((VEC, LANES), F32),
+            pltpu.VMEM(dx.shape, dx.dtype),
+            pltpu.VMEM(outputs.shape, outputs.dtype),
+            pltpu.SemaphoreType.DMA((4,)),
+        ],
         compiler_params=pltpu.CompilerParams(vmem_limit_bytes=VMEM_LIMIT),
         name="finish_grads",
-    )(fin)
+    )(dx, outputs, fin)
 
 
 def pad_to(v, axis, size):
@@ -1582,8 +1749,6 @@
     padded = -(-units // LANES) * LANES
     quarter = replicas * padded
     proj = w_qkv.shape[1]
-    qk = (HQ + KVH) * HD
-    vw = KVH * HD
 
     small = jnp.concatenate(
         [
@@ -1627,22 +1792,18 @@
         n, ctx, order[0], lengths[0], gh2, x2, gy, x, wq_all, wo_all, gain_attn, gain_mlp, freq,
         qs, kv, lse, obt, out, out_par, grads,
     )
-    g_gu, g_down, g_qkv, g_out, vec = finish_grads(n, fin, units, padded, proj, width)
-    vec = vec.reshape(VEC * LANES)
-    f = lax.axis_index("fsdp")
-
-    def own(first, size):
-        return lax.dynamic_slice(vec, (first + f * size,), (size,))
-
+    g_gu, g_down, g_qkv, g_out, g_qk, g_v, g_attn, g_mlp, dx, outputs = finish_grads(
+        n, dx, outputs, fin, units, padded, proj, width
+    )
     return (
         outputs[None],
         dx[None],
         g_qkv,
-        own(0, qk // n),
-        own(qk, vw // n),
+        g_qk[0],
+        g_v[0],
         g_out,
-        own(proj, high),
-        own(proj + width, high),
+        g_attn[0],
+        g_mlp[0],
         g_gu,
         g_down,
     )

time: 325 us -> 302 us (0.929)
  Pallas kernels: 312 us -> 295 us
  local copies, waits for them, and re-layouts: 7.47 us -> 1.42 us
    pallas_call x1, Pallas kernels: 157 us -> 138 us  [attention_backward(): pl.pallas_call(functools.partial(backward_kernel, (n, micro, rows, ctx),...]
    dynamic_slice x3 -> x0, local copies, waits for them, and re-layouts: 3.9 us -> none  [own(): return lax.dynamic_slice(vec, (first + f * size,), (size,))]
where the time goes in v4:
time: 302 us; the launch traced here: 298 us
  Pallas kernels  295 us (98%)
    pallas_call x1, Pallas kernels, attention_backward(): pl.pallas_call(functools.partial(backward_kernel, (n, micro, rows, ctx),...  138 us
    pallas_call x1, Pallas kernels, gather_and_attend(): pl.pallas_call(functools.partial(front_kernel, (n, micro, rows, ctx)), ou...  80.5 us
    pallas_call x1, Pallas kernels, mlp(): pl.pallas_call(functools.partial(mlp_kernel, (micro, rows, width, replica...  67.8 us
    pallas_call x1, Pallas kernels, finish_grads(): pl.pallas_call(functools.partial(finish_kernel, (n, units, padded, proj,...  8.29 us

profile of v4, /device:TPU:0, one launch (start us, length us, event | category | flops | bytes accessed | tf_op | source)
XLA Modules:
  0.0 297.6 jit_solution(17106063823832008256)
XLA Ops:
  0.6 0.7 pad_bitcast_fusion.2
  1.3 0.1 pad.17.clone
  1.4 0.7 pad_bitcast_fusion
  2.1 0.7 maximum_maximum_fusion.sm
  2.7 80.5 %gather_and_attend.1 = (bf16[2,256,896]{2,1,0:T(8,128)(2,1)}, f32[2,256,896]{2,1,0:T(8,128)}, bf16[2,7,256,128]{3,2,1,0:T(8,128)(2,1)}, bf16[2,4,256,256]{3,2,1,...) custom-call(s32[2,8]{1,0:T(2,128)} %bitcast.28, ...), custom_call_target="tpu_custom_call" | custom-call | tf_op jit(solution)/shard_map/gather_and_attend/pallas_call | solution.py:710
  83.3 67.8 %mlp.1 = (f32[2,256,896]{2,1,0:T(8,128)}, bf16[2,256,896]{2,1,0:T(8,128)(2,1)}, f32[2,256,896]{2,1,0:T(8,128)}, bf16[2,24,112,640]{3,2,1,0:T(8,128)(2,1)}) custom-call(bf16[2,256,896]{2,1,0:T(8,128)(2,1)} %get-tuple-element.43.h2, bf16[2,4,256,896]{3,2,1,0:T(8,128)(2,1)} %get-tuple-element.44.gd_hbm, bf16[2,896,1280]{2,1,0:T(8,128)(2,1)} %bitcast.20, ...), custom_call_target="tpu_custom_call" | custom-call | tf_op jit(solution)/shard_map/mlp/pallas_call | solution.py:917
  151.1 138.0 %attention_backward.1 = (f32[2,256,896]{2,1,0:T(8,128)}, bf16[2,256,896]{2,1,0:T(8,128)(2,1)}, bf16[28,112,640]{2,1,0:T(8,128)(2,1)}) custom-call(s32[2,8]{1,0:T(2,128)} %bitcast.29, s32[2,4]{1,0:T(2,128)} %bitcast.31, f32[1,896]{1,0:T(1,128)} %get-tuple-element.40.gain_attn, f32[1,896]{1,0:T(1,128)} %get-tuple-element.41.gain_mlp, ...), custom_call_target="tpu_custom_call" | custom-call | tf_op jit(solution)/shard_map/attention_backward/pallas_call | solution.py:1563
  289.1 8.3 %finish_grads.1 = (f32[112,9728]{1,0:T(8,128)}, f32[608,896]{1,0:T(8,128)}, f32[112,1152]{1,0:T(8,128)}, f32[112,896]{1,0:T(8,128)}, f32[1,128]{1,0:T(1,128)}, /...) custom-call(f32[2,256,896]{2,1,0:T(8,128)} %get-tuple-element.57.dx,, ...), custom_call_target="tpu_custom_call" | custom-call | tf_op jit(solution)/shard_map/finish_grads/pallas_call | solution.py:1705
  (1 shorter events, 0.0 us)

commit v5 on v4

--- a/solution.py
+++ b/solution.py
@@ -17,13 +17,16 @@
 NEGATIVE = -1e30
 TP = 4
 LANES = 128
-CHUNK = 256
 PIECES = 6 * TP
-ALL_PIECES = PIECES + 4
+EXTRA = 6
+ALL_PIECES = PIECES + EXTRA
 RING = 6
-HOP = 2
-RATE = 2
-EARLY = 2
+HOP = 3
+RATE = 4
+FIRST = 2
+PACE = 4
+FIRST_PIECES = 3 * TP
+EARLY = 4
 AHEAD = 4
 SLOTS = 8
 VEC = 32
@@ -52,7 +55,7 @@
 class Links:
     def __init__(self, send_sems, recv_sems):
         self.send_sems, self.recv_sems = send_sems, recv_sems
-        self.started = []
+        self.started, self.gone = [], set()
 
     def put(self, src, dst, device):
         at = len(self.started)
@@ -78,16 +81,23 @@
             device_id_type=MESH,
         ).wait_recv()
 
+    def sent(self, at):
+        if at in self.gone:
+            return
+        self.gone.add(at)
+        src, device = self.started[at]
+        pltpu.make_async_remote_copy(
+            src_ref=src,
+            dst_ref=src,
+            send_sem=self.send_sems.at[at],
+            recv_sem=self.recv_sems.at[at],
+            device_id=device,
+            device_id_type=MESH,
+        ).wait_send()
+
     def drain(self):
-        for at, (src, device) in enumerate(self.started):
-            pltpu.make_async_remote_copy(
-                src_ref=src,
-                dst_ref=src,
-                send_sem=self.send_sems.at[at],
-                recv_sem=self.recv_sems.at[at],
-                device_id=device,
-                device_id_type=MESH,
-            ).wait_send()
+        for at in range(len(self.started)):
+            self.sent(at)
 
 
 class Staged:
@@ -743,13 +753,20 @@
 
 
 def mlp_kernel(
-    size, h2, gd_hbm, wgu_hbm, wd_hbm,
-    out, out_par, gh2, grads,
-    gd, wgu, wd, hbuf, turned_h, turned_g, acc_out, acc_gh, dgate, dup, ddown,
-    sib_out, sib_in, par_out, par_in, keep_sum, stage, send, recv, out_sem, staged_sems,
+    size, ctx, h2, gd_hbm, wgu_hbm, wd_hbm,
+    out, out_par, gh2, grads, *rest
 ):
     micro, rows, width, replicas, padded = size
-    quarter = replicas * padded
+    n = replicas * TP
+    columns = replicas * LANES
+    tiles = padded // LANES
+    split = ctx is not None
+    if split:
+        kept, fin_first, rest = rest[0], rest[1], rest[2:]
+    (
+        gd, wgu, wd, hbuf, turned_h, turned_g, acc_out, acc_gh, dgate, dup, ddown,
+        sib_out, sib_in, par_out, par_in, keep_sum, stage, send, recv, out_sem, staged_sems,
+    ), rest = rest[:21], rest[21:]
     both = 2 * rows
     f, c = lax.axis_index("fsdp"), lax.axis_index("ctx")
     t = f % TP
@@ -763,7 +780,12 @@
         + [(gd_hbm.at[m], gd.at[m]) for m in range(1, micro)],
         staged_sems,
     )
-    enter([sib, par])
+    if split:
+        acc_stage, grads_first, kept_sem = rest[:3]
+        first_sums = Sums(n, ctx, grads_first, fin_first, rest[3:], 2, 0, 2)
+        enter(first_sums.around())
+    else:
+        enter([sib, par])
     links = Links(send, recv)
     from_sib, from_par, from_cross = [], [], [None] * micro
     for m in range(micro):
@@ -778,13 +800,14 @@
         links.arrive(from_par[m], buf)
         from_cross[m] = links.put(buf, buf, sib)
 
-    def chunk(m, side, first, j):
-        at = pl.multiple_of(j * CHUNK, CHUNK)
+    def chunk(m, side, first, base, j):
+        at = [pl.multiple_of(q * padded + j * LANES, LANES) for q in range(replicas)]
+        to = pl.ds(pl.multiple_of((j - base) * columns, columns), columns)
         hidden_in = hbuf[m, pl.ds(side, 2)].reshape(both, width)
         grad_in = grad_of(m, side)
-        w_gate = wgu[0, :, pl.ds(at, CHUNK)]
-        w_up = wgu[1, :, pl.ds(at, CHUNK)]
-        w_down = wd[pl.ds(at, CHUNK), :]
+        w_gate = jnp.concatenate([wgu[0, :, pl.ds(k, LANES)] for k in at], axis=1)
+        w_up = jnp.concatenate([wgu[1, :, pl.ds(k, LANES)] for k in at], axis=1)
+        w_down = jnp.concatenate([wd[pl.ds(k, LANES), :] for k in at], axis=0)
         gate = dot(hidden_in, w_gate)
         up = dot(hidden_in, w_up)
         gm = dot_nt(grad_in, w_down)
@@ -796,134 +819,195 @@
         acc_out[...] += dot(mb, w_down)
         acc_gh[...] += dot_nt(ggate, w_gate) + dot_nt(gup, w_up)
         if first:
-            dgate[:, pl.ds(at, CHUNK)] = dot(turned_h[...], ggate)
-            dup[:, pl.ds(at, CHUNK)] = dot(turned_h[...], gup)
-            ddown[:, pl.ds(at, CHUNK)] = dot(turned_g[...], mb)
+            dgate[:, to] = dot(turned_h[...], ggate)
+            dup[:, to] = dot(turned_h[...], gup)
+            ddown[:, to] = dot(turned_g[...], mb)
         else:
-            dgate[:, pl.ds(at, CHUNK)] += dot(turned_h[...], ggate)
-            dup[:, pl.ds(at, CHUNK)] += dot(turned_h[...], gup)
-            ddown[:, pl.ds(at, CHUNK)] += dot(turned_g[...], mb)
-
-    def compute(m, side, first, middle, late):
-        turned_h[...] = hbuf[m, pl.ds(side, 2)].reshape(both, width).T
-        turned_g[...] = grad_of(m, side).T
-        acc_out[...] = jnp.zeros_like(acc_out)
-        acc_gh[...] = jnp.zeros_like(acc_gh)
-        chunks = quarter // CHUNK
-
-        def body(j, carry):
-            chunk(m, side, first, j)
-            return carry
-
-        lax.fori_loop(0, 2, body, 0)
-        middle()
-        lax.fori_loop(2, chunks - 1, body, 0)
-        late()
-        lax.fori_loop(chunks - 1, chunks, body, 0)
+            dgate[:, to] += dot(turned_h[...], ggate)
+            dup[:, to] += dot(turned_h[...], gup)
+            ddown[:, to] += dot(turned_g[...], mb)
 
     def share(step):
         here = pl.multiple_of(core * rows, rows)
         there = pl.multiple_of(rows - core * rows, rows)
         ats = []
         for k, acc in enumerate((acc_gh, acc_out)):
-            sib_out[step, k] = acc[pl.ds(there, rows), :].astype(BF)
-            ats.append(links.put(sib_out.at[step, k], sib_in.at[step, k], sib))
+            if step >= 2:
+                links.sent(shared[step - 2][k])
+            sib_out[step % 2, k] = acc[pl.ds(there, rows), :].astype(BF)
+            ats.append(links.put(sib_out.at[step % 2, k], sib_in.at[step, k], sib))
             keep_sum[k] = acc[pl.ds(here, rows), :]
-        return ats
-
-    def pass_on(step, m, ats):
-        for k, (at, ref) in enumerate(zip(ats, (par_out, out_par))):
+        shared.append(ats)
+
+    shared = []
+    passed = [None] * micro
+
+    def settle(step, m, own):
+        for k, at in enumerate(shared[step]):
             links.arrive(at, sib_in.at[step, k])
-            ref[m] = (keep_sum[k] + sib_in[step, k].astype(F32)).astype(BF)
-        return links.put(par_out.at[m], par_in.at[m], par)
-
-    def stay(step, m, ats):
-        for k, (at, ref) in enumerate(zip(ats, (gh2, out))):
-            links.arrive(at, sib_in.at[step, k])
-            ref[m] = keep_sum[k] + sib_in[step, k].astype(F32)
-
-    def finish(m, at):
-        links.arrive(at, par_in.at[m])
-        gh2[m] = gh2[m] + par_in[m].astype(F32)
-
-    plan = [(0, True)] + [(m, False) for m in range(micro)] + [(m, True) for m in range(1, micro)]
-    waiting = None
-    sums = [None] * micro
-    ready_own = [False] * micro
-    for step, (m, own) in enumerate(plan):
-        if own:
-            links.arrive(from_sib[m], hbuf.at[m, t_sib])
-        else:
-            links.arrive(from_cross[m], hbuf.at[m, t_cross])
-        staged.need((micro + 3) if m == 0 else len(staged.copies))
-
-        def late(step=step):
-            if step < micro:
-                forward_on(step)
-
-        def middle(step=step):
-            if step > 0:
-                last_m, last_own = plan[step - 1]
-                if last_own:
-                    stay(step - 1, last_m, waiting)
+            whole = keep_sum[k] + sib_in[step, k].astype(F32)
+            if own:
+                (gh2, out)[k][m] = whole
+            else:
+                (par_out, out_par)[k][m] = whole.astype(BF)
+        if not own:
+            passed[m] = links.put(par_out.at[m], par_in.at[m], par)
+
+    def piece_of(per, base, count, replica, k):
+        high = width // n
+        wide = columns * count * 2 // per
+        if k < per * TP:
+            at = (replica * TP + k // per) * high
+            half, lane = divmod(k % per, per // 2)
+            return (dgate, dup)[half][at : at + high, lane * wide : (lane + 1) * wide].astype(BF)
+        blocks = 2 * replicas // per
+        parts = []
+        for q in range(blocks):
+            at = ((k - per * TP) * blocks + q) * high
+            for j in range(count):
+                lane = (j * replicas + replica) * LANES
+                parts.append(ddown[at : at + high, lane : lane + LANES])
+        return jnp.concatenate(parts, axis=1).astype(BF)
+
+    own_steps = [(m, True) for m in range(micro)]
+    other_steps = [(m, False) for m in range(micro)]
+    if split:
+        passes = [(0, FIRST, own_steps + other_steps), (FIRST, tiles, other_steps + own_steps)]
+    else:
+        passes = [(0, tiles, own_steps[:1] + other_steps + own_steps[1:])]
+    seen = set()
+    writing = None
+    ticks = 0
+    for number, (base, end, plan) in enumerate(passes):
+        final = number == len(passes) - 1
+        second = split and final
+        for step, (m, own) in enumerate(plan):
+            if (m, own) not in seen:
+                seen.add((m, own))
+                if own:
+                    links.arrive(from_sib[m], hbuf.at[m, t_sib])
                 else:
-                    sums[last_m] = pass_on(step - 1, last_m, waiting)
-
-        compute(m, mine if own else theirs, step == 0, middle, late)
-        waiting = share(step)
-    high = width // (replicas * TP)
+                    if from_cross[m] is None:
+                        forward_on(m)
+                    links.arrive(from_cross[m], hbuf.at[m, t_cross])
+            staged.need((micro + 3) if m == 0 else len(staged.copies))
+            side = mine if own else theirs
+            turned_h[...] = hbuf[m, pl.ds(side, 2)].reshape(both, width).T
+            turned_g[...] = grad_of(m, side).T
+            if second:
+                index = passes[0][2].index((m, own))
+                pltpu.make_async_copy(kept.at[index], acc_stage, kept_sem.at[1]).wait()
+                acc_gh[...] = acc_stage[0].astype(F32)
+                acc_out[...] = acc_stage[1].astype(F32)
+                if step + 1 < len(plan):
+                    index = passes[0][2].index(plan[step + 1])
+                    pltpu.make_async_copy(kept.at[index], acc_stage, kept_sem.at[1]).start()
+            else:
+                acc_out[...] = jnp.zeros_like(acc_out)
+                acc_gh[...] = jnp.zeros_like(acc_gh)
+
+            def body(j, carry, m=m, side=side, step=step, second=second):
+                chunk(m, side, step == 0, base, j)
+                if second:
+                    i = step * (end - base) + j - base
+                    lax.fori_loop(
+                        jnp.minimum(PACE * i // 4, first_sums.ticks),
+                        jnp.minimum(PACE * (i + 1) // 4, first_sums.ticks),
+                        first_sums.step, 0,
+                    )
+                return carry
+
+            lax.fori_loop(base, end - 1, body, 0)
+            if final and step > 0:
+                settle(step - 1, *plan[step - 1])
+            upcoming = plan[step + 1 : step + 2]
+            if upcoming and not upcoming[0][1] and from_cross[upcoming[0][0]] is None:
+                forward_on(upcoming[0][0])
+            lax.fori_loop(end - 1, end, body, 0)
+            if final:
+                share(step)
+            else:
+                if writing is not None:
+                    writing.wait()
+                acc_stage[0] = acc_gh[...].astype(BF)
+                acc_stage[1] = acc_out[...].astype(BF)
+                writing = pltpu.make_async_copy(acc_stage, kept.at[step], kept_sem.at[0])
+                writing.start()
+        if not final:
+            for k in range(FIRST_PIECES):
+                for replica in range(replicas):
+                    grads_first[replica, k] = piece_of(2, base, end - base, replica, k)
+            first_sums.start()
+            writing.wait()
+            index = plan.index(passes[1][2][0])
+            pltpu.make_async_copy(kept.at[index], acc_stage, kept_sem.at[1]).start()
+            first_sums.own_copy().wait()
+    ticks = min(PACE * len(plan) * (end - base) // 4, first_sums.ticks) if split else 0
     copies = []
-    for replica in range(replicas):
-        for k in range(PIECES):
+    for k in range(PIECES):
+        if split and k % 4 == 0 and ticks < first_sums.ticks:
+            first_sums.tick(jnp.int32(ticks))
+            ticks += 1
+        for replica in range(replicas):
             slot = len(copies) % SLOTS
             if len(copies) >= SLOTS:
                 copies[-SLOTS].wait()
-            if k < 4 * TP:
-                at = (replica * TP + k // 4) * high
-                lane = (k % 2) * (quarter // 2)
-                stage[slot] = (dgate, dup)[(k // 2) % 2][
-                    at : at + high, lane : lane + quarter // 2
-                ].astype(BF)
-            else:
-                for q in range(replicas // 2):
-                    at = (k - 4 * TP) * (replicas // 2) + q
-                    stage[slot, :, q * padded : (q + 1) * padded] = ddown[
-                        at * high : (at + 1) * high, replica * padded : (replica + 1) * padded
-                    ].astype(BF)
+            stage[slot] = piece_of(4, base, end - base, replica, k)
             copy = pltpu.make_async_copy(stage.at[slot], grads.at[replica, k], out_sem.at[slot])
             copy.start()
             copies.append(copy)
-    last_m, last_own = plan[-1]
-    if last_own:
-        stay(len(plan) - 1, last_m, waiting)
-    else:
-        sums[last_m] = pass_on(len(plan) - 1, last_m, waiting)
+    settle(len(plan) - 1, *plan[-1])
     for m in range(micro):
-        finish(m, sums[m])
+        links.arrive(passed[m], par_in.at[m])
+        gh2[m] = gh2[m] + par_in[m].astype(F32)
+    if split:
+        lax.fori_loop(ticks, max(ticks, first_sums.ticks), first_sums.step, 0)
+        first_sums.close()
     for copy in copies[-SLOTS:]:
         copy.wait()
     links.drain()
 
 
-def mlp(n, h2, gd, wgu, wd):
+def mlp(n, ctx, h2, gd, wgu, wd):
     micro, rows, width = h2.shape
     replicas = n // TP
     padded = wd.shape[0] // replicas
-    quarter = replicas * padded
+    high = width // n
+    columns = replicas * LANES
+    tiles = padded // LANES
+    split = ctx <= 4 and tiles > FIRST
+    count = tiles - FIRST if split else tiles
     vmem = pl.BlockSpec(memory_space=pltpu.VMEM)
+    anywhere = pl.BlockSpec(memory_space=pl.ANY)
+    sems = pltpu.SemaphoreType.DMA
     steps = 2 * micro
     copies = micro * 3 + steps * 2 + micro
     whole = jax.ShapeDtypeStruct((micro, rows, width), F32)
-    return pl.pallas_call(
-        functools.partial(mlp_kernel, (micro, rows, width, replicas, padded)),
-        out_shape=(
-            whole,
-            jax.ShapeDtypeStruct((micro, rows, width), BF),
-            whole,
-            jax.ShapeDtypeStruct((replicas, PIECES, width // n, quarter // 2), BF),
+    most = columns * max(FIRST, count)
+    out_shape = [
+        whole,
+        jax.ShapeDtypeStruct((micro, rows, width), BF),
+        whole,
+        jax.ShapeDtypeStruct((replicas, PIECES, high, columns * count // 2), BF),
+    ]
+    extra = []
+    if split:
+        out_shape += [
+            jax.ShapeDtypeStruct((steps, 2, 2 * rows, width), BF),
+            jax.ShapeDtypeStruct((FIRST_PIECES, high, columns * FIRST), BF),
+        ]
+        extra = [
+            pltpu.VMEM((2, 2 * rows, width), BF),
+            pltpu.VMEM((replicas, FIRST_PIECES, high, columns * FIRST), BF),
+            sems((2,)),
+        ] + Sums.scratch(n, high, columns * FIRST, (), 2, 0)
+    result = pl.pallas_call(
+        functools.partial(
+            mlp_kernel, (micro, rows, width, replicas, padded), ctx if split else None
         ),
-        in_specs=[pl.BlockSpec(memory_space=pl.ANY)] * 4,
-        out_specs=[vmem, vmem, vmem, pl.BlockSpec(memory_space=pl.ANY)],
+        out_shape=out_shape,
+        in_specs=[anywhere] * 4,
+        out_specs=[vmem, vmem, vmem] + [anywhere] * (len(out_shape) - 3),
         scratch_shapes=[
             pltpu.VMEM(gd.shape, BF),
             pltpu.VMEM(wgu.shape, BF),
@@ -933,25 +1017,28 @@
             pltpu.VMEM((width, 2 * rows), BF),
             pltpu.VMEM((2 * rows, width), F32),
             pltpu.VMEM((2 * rows, width), F32),
-            pltpu.VMEM((width, quarter), F32),
-            pltpu.VMEM((width, quarter), F32),
-            pltpu.VMEM((width, quarter), F32),
-            pltpu.VMEM((steps, 2, rows, width), BF),
+            pltpu.VMEM((width, most), F32),
+            pltpu.VMEM((width, most), F32),
+            pltpu.VMEM((width, most), F32),
+            pltpu.VMEM((2, 2, rows, width), BF),
             pltpu.VMEM((steps, 2, rows, width), BF),
             pltpu.VMEM((micro, rows, width), BF),
             pltpu.VMEM((micro, rows, width), BF),
             pltpu.VMEM((2, rows, width), F32),
-            pltpu.VMEM((SLOTS, width // n, quarter // 2), BF),
-            pltpu.SemaphoreType.DMA((copies,)),
-            pltpu.SemaphoreType.DMA((copies,)),
-            pltpu.SemaphoreType.DMA((SLOTS,)),
-            pltpu.SemaphoreType.DMA((2 * micro + 2,)),
-        ],
+            pltpu.VMEM((SLOTS, high, columns * count // 2), BF),
+            sems((copies,)),
+            sems((copies,)),
+            sems((SLOTS,)),
+            sems((2 * micro + 2,)),
+        ] + extra,
         compiler_params=pltpu.CompilerParams(
             collective_id=2, has_side_effects=True, vmem_limit_bytes=VMEM_LIMIT
         ),
         name="mlp",
     )(h2, gd, wgu, wd)
+    out, out_par, gh2, grads = result[:4]
+    fins = [(result[5], 2, FIRST)] if split else []
+    return out, out_par, gh2, grads, fins, count
 
 
 def add_into(dst, a, b):
@@ -959,8 +1046,11 @@
 
 
 class Sums:
-    def __init__(self, n, ctx, grads, fin, scratch):
+    def __init__(self, n, ctx, grads, fin, scratch, per=4, extra=EXTRA, hop=HOP):
         self.n, self.ctx, self.grads, self.fin = n, ctx, grads, fin
+        self.per, self.hop = per, hop
+        self.lots, self.pieces = per * TP, per * (TP + 2)
+        self.all = self.pieces + extra
         (
             self.total, self.peer_in, self.pre, self.suf, self.suf_out, self.land,
             self.vec, self.vec_in,
@@ -979,24 +1069,26 @@
         self.links = Links(self.asend, self.arecv)
 
     @staticmethod
-    def scratch(n, high, wide, columns):
+    def scratch(n, high, wide, columns, per=4, extra=EXTRA):
         replicas = n // TP
+        lots, pieces = per * TP, per * (TP + 2)
+        every = pieces + extra
         sems = pltpu.SemaphoreType.DMA
         peers = replicas - 1
         return [
-            pltpu.VMEM((ALL_PIECES, high, wide), BF),
-            pltpu.VMEM((peers, PIECES, high, wide), BF),
-            pltpu.VMEM((ALL_PIECES, high, wide), BF),
-            pltpu.VMEM((ALL_PIECES, high, wide), BF),
+            pltpu.VMEM((every, high, wide), BF),
+            pltpu.VMEM((peers, pieces, high, wide), BF),
+            pltpu.VMEM((every, high, wide), BF),
+            pltpu.VMEM((every, high, wide), BF),
             pltpu.VMEM((RING, high, wide), BF),
-            pltpu.VMEM((4 * TP, high, wide), BF),
+            pltpu.VMEM((lots, high, wide), BF),
             pltpu.VMEM((3, VEC, LANES), F32),
             pltpu.VMEM((2 + peers, VEC, LANES), F32),
-            sems((peers * PIECES,)), sems((peers * PIECES,)),
-            sems((ALL_PIECES,)), sems((ALL_PIECES,)), sems((ALL_PIECES,)), sems((ALL_PIECES,)),
-            sems((4 * TP,)), sems((4 * TP,)),
+            sems((peers * pieces,)), sems((peers * pieces,)),
+            sems((every,)), sems((every,)), sems((every,)), sems((every,)),
+            sems((lots,)), sems((lots,)),
             sems(((len(columns) + 1) * (2 + peers),)), sems(((len(columns) + 1) * (2 + peers),)),
-            sems((1,)), sems((ALL_PIECES,)),
+            sems((1,)), sems((every,)),
         ] + [
             one
             for wide_here in columns
@@ -1012,7 +1104,7 @@
         return [self.sib, self.par, self.cross] + self.peers + [self.left, self.right]
 
     def peer_copy(self, j, k):
-        at = j * PIECES + k
+        at = j * self.pieces + k
         return pltpu.make_async_remote_copy(
             src_ref=self.grads.at[(self.r + j + 1) % self.replicas, k],
             dst_ref=self.peer_in.at[j, k],
@@ -1024,7 +1116,7 @@
 
     def own_copy(self):
         return pltpu.make_async_copy(
-            self.grads.at[self.r], self.total.at[pl.ds(0, PIECES)], self.own_sem.at[0]
+            self.grads.at[self.r], self.total.at[pl.ds(0, self.pieces)], self.own_sem.at[0]
         )
 
     def start(self):
@@ -1055,20 +1147,20 @@
     def tick(self, time):
         c, ctx, total = self.c, self.ctx, self.total
 
-        @pl.when(time + AHEAD < PIECES)
+        @pl.when(time + AHEAD < self.pieces)
         def _():
             for j in range(self.replicas - 1):
                 self.peer_copy(j, time + AHEAD).start()
 
-        @pl.when(time < PIECES)
+        @pl.when(time < self.pieces)
         def _():
             for j in range(self.replicas - 1):
                 self.peer_copy(j, time).wait_recv()
                 add_into(total.at[time], total.at[time], self.peer_in.at[j, time])
 
-        k = time - HOP * c
-
-        @pl.when((k >= 0) & (k < ALL_PIECES))
+        k = time - self.hop * c
+
+        @pl.when((k >= 0) & (k < self.all))
         def _():
             @pl.when(c > 0)
             def _():
@@ -1083,9 +1175,9 @@
             def _():
                 self.pre_copy(k, total).start()
 
-        k2 = time - HOP * (ctx - 1 - c)
-
-        @pl.when((k2 >= 0) & (k2 < ALL_PIECES))
+        k2 = time - self.hop * (ctx - 1 - c)
+
+        @pl.when((k2 >= 0) & (k2 < self.all))
         def _():
             @pl.when(c < ctx - 1)
             def _():
@@ -1104,9 +1196,9 @@
             def _():
                 self.suf_copy(k2, total.at[k2]).start()
 
-        k3 = time - HOP * jnp.maximum(c, ctx - 1 - c)
-
-        @pl.when((k3 >= 0) & (k3 < ALL_PIECES))
+        k3 = time - self.hop * jnp.maximum(c, ctx - 1 - c)
+
+        @pl.when((k3 >= 0) & (k3 < self.all))
         def _():
             @pl.when(c == 0)
             def _():
@@ -1116,7 +1208,7 @@
             def _():
                 add_into(self.suf.at[k3], self.suf.at[k3], self.pre.at[k3])
 
-            @pl.when((k3 < 4 * TP) & (k3 // 4 != self.t))
+            @pl.when((k3 < self.lots) & (k3 // self.per != self.t))
             def _():
                 @pl.when(c == ctx - 1)
                 def _():
@@ -1126,7 +1218,7 @@
                 def _():
                     self.fin_copy_from(k3, self.suf).start()
 
-            @pl.when((k3 >= 4 * TP) | (k3 // 4 == self.t))
+            @pl.when((k3 >= self.lots) | (k3 // self.per == self.t))
             def _():
                 @pl.when(c == ctx - 1)
                 def _():
@@ -1138,24 +1230,24 @@
 
     def fin_copy_from(self, k, src):
         return pltpu.make_async_remote_copy(
-            src_ref=src.at[k], dst_ref=self.land.at[4 * self.t + k % 4], send_sem=self.fs.at[k],
-            recv_sem=self.fr.at[4 * self.t + k % 4],
-            device_id=(self.f - self.t + k // 4, self.c), device_id_type=MESH,
+            src_ref=src.at[k], dst_ref=self.land.at[self.per * self.t + k % self.per], send_sem=self.fs.at[k],
+            recv_sem=self.fr.at[self.per * self.t + k % self.per],
+            device_id=(self.f - self.t + k // self.per, self.c), device_id_type=MESH,
         )
 
     @property
     def ticks(self):
-        return ALL_PIECES + HOP * (self.ctx - 1)
+        return self.all + self.hop * (self.ctx - 1)
 
     def close(self):
         c, ctx = self.c, self.ctx
 
         def arrive(k, carry):
-            @pl.when(k // 4 != self.t)
+            @pl.when(k // self.per != self.t)
             def _():
                 pltpu.make_async_remote_copy(
                     src_ref=self.land.at[k], dst_ref=self.land.at[k], send_sem=self.fs.at[k],
-                    recv_sem=self.fr.at[k], device_id=(self.f - self.t + k // 4, c),
+                    recv_sem=self.fr.at[k], device_id=(self.f - self.t + k // self.per, c),
                     device_id_type=MESH,
                 ).wait_recv()
                 self.out_copy(k, self.land).start()
@@ -1163,28 +1255,28 @@
 
             return carry
 
-        lax.fori_loop(0, 4 * TP, arrive, 0)
+        lax.fori_loop(0, self.lots, arrive, 0)
 
         def settle(k, carry):
             @pl.when(c < ctx - 1)
             def _():
                 self.pre_copy(k, self.total).wait_send()
 
-            @pl.when((c == ctx - 1) | ((c > 0) & (k >= ALL_PIECES - RING)))
+            @pl.when((c == ctx - 1) | ((c > 0) & (k >= self.all - RING)))
             def _():
                 self.suf_copy(k, self.total.at[k]).wait_send()
 
             self.out_copy(k, self.suf).wait()
             return carry
 
-        lax.fori_loop(0, ALL_PIECES, settle, 0)
+        lax.fori_loop(0, self.all, settle, 0)
 
         def peers(k, carry):
             for j in range(self.replicas - 1):
                 self.peer_copy(j, k).wait_send()
             return carry
 
-        lax.fori_loop(0, PIECES, peers, 0)
+        lax.fori_loop(0, self.pieces, peers, 0)
         self.links.drain()
 
     def place(self, column, value):
@@ -1193,7 +1285,7 @@
         while done < value.shape[1]:
             piece, at = divmod(column + done, wide)
             count = min(wide - at, value.shape[1] - done)
-            self.total[PIECES + piece, : value.shape[0], at : at + count] = value[
+            self.total[self.pieces + piece, : value.shape[0], at : at + count] = value[
                 :, done : done + count
             ]
             done += count
@@ -1458,12 +1550,12 @@
             if merged:
                 step = m * pairs + p
                 lax.fori_loop(
-                    EARLY + RATE * step // 2, EARLY + RATE * (step + 1) // 2, sums.step, 0
+                    EARLY + RATE * step // 4, EARLY + RATE * (step + 1) // 4, sums.step, 0
                 )
             return carry
 
         lax.fori_loop(0, pairs, pair, 0)
-    ticks[0] = EARLY + RATE * micro * pairs // 2
+    ticks[0] = EARLY + RATE * micro * pairs // 4
     spare = max(0, PIECES - ticks[0])
     first = ticks[0]
     columns(fold_b, sizes[1], width)
@@ -1642,10 +1734,15 @@
 
 
 def finish_kernel(
-    size, dx, outputs, fin, g_gu, g_down, g_qkv, g_out, g_qk, g_v, g_attn, g_mlp, dx_out, outputs_out,
-    turn, vecs, dx_in, outputs_in, sems,
+    size, sets, dx, outputs, *rest
 ):
     n, units, padded, proj, width = size
+    fins, rest = rest[: len(sets)], rest[len(sets) :]
+    (
+        g_gu, g_down, g_qkv, g_out, g_qk, g_v, g_attn, g_mlp, dx_out, outputs_out,
+        turn, vecs, dx_in, outputs_in, sems,
+    ) = rest
+    fin = fins[-1]
     replicas = n // TP
     high = width // n
     through = [(dx, dx_in, dx_out), (outputs, outputs_in, outputs_out)]
@@ -1674,19 +1771,30 @@
     for a, b in zip(coming, going):
         a.wait()
         b.start()
-    wide = fin.shape[-1]
     for half in range(2):
         for k in range(TP):
-            whole = jnp.concatenate(
-                [fin[4 * k + 2 * half + q].astype(F32) for q in range(2)], axis=1
-            )
+            wholes = []
+            for ref, (per, count) in zip(fins, sets):
+                first = per * k + half * (per // 2)
+                whole = [ref[first + q].astype(F32) for q in range(per // 2)]
+                wholes.append(whole[0] if len(whole) == 1 else jnp.concatenate(whole, axis=1))
             for q in range(replicas):
+                tiles = []
+                for whole, (per, count) in zip(wholes, sets):
+                    for j in range(count):
+                        lane = (j * replicas + q) * LANES
+                        tiles.append(whole[:, lane : lane + LANES])
                 at = ((half * replicas + q) * TP + k) * units
-                g_gu[:, at : at + units] = whole[:, q * padded : q * padded + units]
-    each = wide // padded
-    for k in range(n):
-        at = (k % each) * padded
-        turn[k * high : (k + 1) * high, :] = fin[4 * TP + k // each, :, at : at + padded].astype(F32)
+                g_gu[:, at : at + units] = jnp.concatenate(tiles, axis=1)[:, :units]
+    done = 0
+    for ref, (per, count) in zip(fins, sets):
+        blocks = 2 * replicas // per
+        for k in range(n):
+            lane = (k % blocks) * count * LANES
+            turn[k * high : (k + 1) * high, done : done + count * LANES] = ref[
+                per * TP + k // blocks, :, lane : lane + count * LANES
+            ].astype(F32)
+        done += count * LANES
     g_down[...] = turn[...].T[:units, :]
     ahead = ALL_PIECES - PIECES - 1
     whole = jnp.concatenate([fin[PIECES + k] for k in range(ahead)], axis=1)
@@ -1697,13 +1805,15 @@
         copy.wait()
 
 
-def finish_grads(n, dx, outputs, fin, units, padded, proj, width):
+def finish_grads(n, dx, outputs, fins, units, padded, proj, width):
     high = width // n
     vmem = pl.BlockSpec(memory_space=pltpu.VMEM)
     anywhere = pl.BlockSpec(memory_space=pl.ANY)
     one = lambda count: jax.ShapeDtypeStruct((1, count), F32)
     return pl.pallas_call(
-        functools.partial(finish_kernel, (n, units, padded, proj, width)),
+        functools.partial(
+            finish_kernel, (n, units, padded, proj, width), [one[1:] for one in fins]
+        ),
         out_shape=(
             jax.ShapeDtypeStruct((high, 2 * n * units), F32),
             jax.ShapeDtypeStruct((units, width), F32),
@@ -1716,7 +1826,7 @@
             jax.ShapeDtypeStruct(dx.shape, dx.dtype),
             jax.ShapeDtypeStruct(outputs.shape, outputs.dtype),
         ),
-        in_specs=[anywhere, anywhere, vmem],
+        in_specs=[anywhere, anywhere] + [vmem] * len(fins),
         out_specs=[vmem] * 8 + [anywhere] * 2,
         scratch_shapes=[
             pltpu.VMEM((width, padded), F32),
@@ -1727,7 +1837,7 @@
         ],
         compiler_params=pltpu.CompilerParams(vmem_limit_bytes=VMEM_LIMIT),
         name="finish_grads",
-    )(dx, outputs, fin)
+    )(dx, outputs, *[one[0] for one in fins])
 
 
 def pad_to(v, axis, size):
@@ -1787,13 +1897,13 @@
         )
     wgu_t = wgu_t.reshape(2, width, quarter)
     wd_t = wd_t.reshape(quarter, width)
-    out, out_par, gh2, grads = mlp(n, h2, gd_all, wgu_t, wd_t)
+    out, out_par, gh2, grads, fins, count = mlp(n, ctx, h2, gd_all, wgu_t, wd_t)
     dx, outputs, fin = attention_backward(
         n, ctx, order[0], lengths[0], gh2, x2, gy, x, wq_all, wo_all, gain_attn, gain_mlp, freq,
         qs, kv, lse, obt, out, out_par, grads,
     )
     g_gu, g_down, g_qkv, g_out, g_qk, g_v, g_attn, g_mlp, dx, outputs = finish_grads(
-        n, dx, outputs, fin, units, padded, proj, width
+        n, dx, outputs, fins + [(fin, 4, count)], units, padded, proj, width
     )
     return (
         outputs[None],

time: 302 us -> 299 us (0.990)
  the two profiles are of different devices: /device:TPU:0 before, /device:TPU:6 now
where the time goes in v5:
time: 299 us; the launch traced here: 293 us
  Pallas kernels  289 us (97%)
    pallas_call x1, Pallas kernels, attention_backward(): pl.pallas_call(functools.partial(backward_kernel, (n, micro, rows, ctx),...  114 us
    pallas_call x1, Pallas kernels, mlp(): pl.pallas_call(functools.partial(mlp_kernel, (micro, rows, width, replica...  91.1 us
    pallas_call x1, Pallas kernels, gather_and_attend(): pl.pallas_call(functools.partial(front_kernel, (n, micro, rows, ctx)), ou...  76.2 us
    pallas_call x1, Pallas kernels, finish_grads(): pl.pallas_call(functools.partial(finish_kernel, (n, units, padded, proj,...  8.31 us

profile of v5, /device:TPU:6, one launch (start us, length us, event | category | flops | bytes accessed | tf_op | source)
XLA Modules:
  0.0 292.7 jit_solution(13055089667214075864)
XLA Ops:
  0.6 0.7 pad_bitcast_fusion.2
  1.3 0.1 pad.17.clone
  1.4 0.7 pad_bitcast_fusion
  2.1 0.7 maximum_maximum_fusion.sm
  2.7 76.2 %gather_and_attend.1 = (bf16[2,256,896]{2,1,0:T(8,128)(2,1)}, f32[2,256,896]{2,1,0:T(8,128)}, bf16[2,7,256,128]{3,2,1,0:T(8,128)(2,1)}, bf16[2,4,256,256]{3,2,1,...) custom-call(s32[2,8]{1,0:T(2,128)} %bitcast.28, ...), custom_call_target="tpu_custom_call" | custom-call | tf_op jit(solution)/shard_map/gather_and_attend/pallas_call | solution.py:720
  78.9 91.1 %mlp.1 = (f32[2,256,896]{2,1,0:T(8,128)}, bf16[2,256,896]{2,1,0:T(8,128)(2,1)}, f32[2,256,896]{2,1,0:T(8,128)}, bf16[2,24,112,384]{3,2,1,0:T(8,128)(2,1)}, bf16[...) custom-call(bf16[2,256,896]{2,1,0:T(8,128)(2,1)} %get-tuple-element.44.h2, ...), custom_call_target="tpu_custom_call" | custom-call | tf_op jit(solution)/shard_map/mlp/pallas_call | solution.py:1004
  170.1 113.8 %attention_backward.1 = (f32[2,256,896]{2,1,0:T(8,128)}, bf16[2,256,896]{2,1,0:T(8,128)(2,1)}, bf16[30,112,384]{2,1,0:T(8,128)(2,1)}) custom-call(s32[2,8]{1,0:T(2,128)} %bitcast.29, s32[2,4]{1,0:T(2,128)} %bitcast.31, f32[1,896]{1,0:T(1,128)} %get-tuple-element.41.gain_attn, f32[1,896]{1,0:T(1,128)} %get-tuple-element.42.gain_mlp, ...), custom_call_target="tpu_custom_call" | custom-call | tf_op jit(solution)/shard_map/attention_backward/pallas_call | solution.py:1655
  283.9 8.3 %finish_grads.1 = (f32[112,9728]{1,0:T(8,128)}, f32[608,896]{1,0:T(8,128)}, f32[112,1152]{1,0:T(8,128)}, f32[112,896]{1,0:T(8,128)}, f32[1,128]{1,0:T(1,128)}, /...) custom-call(f32[2,256,896]{2,1,0:T(8,128)} %get-tuple-element.58.dx,, ...), custom_call_target="tpu_custom_call" | custom-call | tf_op jit(solution)/shard_map/finish_grads/pallas_call | solution.py:1813
  (1 shorter events, 0.0 us)
